TPU v7x, 32 devices: a whole 2x2x4 slice. The times are simulated.
32 devices in a mesh: batch: 8 (over z, y), seq: 2 (over x), tensor: 2 (over core).
Axes of the slice: x: 2, y: 2, z: 4, core: 2. Of those that a mesh axis runs over, the one named last changes fastest.
Arguments:
- hidden_in: bfloat16 [8, 2, 128, 2048], P('batch', None, 'seq', 'tensor'), may hold values from -6 to 6
- summary_counts: int32 [8], P('batch'), may hold values from 20 to 50, as said below
- summary_embed: bfloat16 [50, 2048], P(None, 'tensor'), may hold values from -6 to 6
- ln1_gain: bfloat16 [2048], P('tensor'), may hold values from 0.5 to 1.5
- ln1_bias: bfloat16 [2048], P('tensor'), may hold values from -1.75 to 1.75
- w_query: bfloat16 [2048, 2048], P(None, 'tensor'), may hold values from -0.125 to 0.125
- b_query: bfloat16 [2048], P('tensor'), may hold values from -3 to 3
- w_key: bfloat16 [2048, 2048], P(None, 'tensor'), may hold values from -0.125 to 0.125
- w_value: bfloat16 [2048, 2048], P(None, 'tensor'), may hold values from -0.125 to 0.125
- b_value: bfloat16 [2048], P('tensor'), may hold values from -3 to 3
- w_out: bfloat16 [2048, 2048], P('tensor'), may hold values from -1 to 1
- b_out: bfloat16 [2048], P('tensor'), may hold values from -1.75 to 1.75
- ln2_gain: bfloat16 [2048], P('tensor'), may hold values from 0.5 to 1.5
- ln2_bias: bfloat16 [2048], P('tensor'), may hold values from -1.75 to 1.75
- w_up: bfloat16 [2048, 8192], P(None, 'tensor'), may hold values from -0.125 to 0.125
- b_up: bfloat16 [8192], P('tensor'), may hold values from -3 to 3
- w_down: bfloat16 [8192, 2048], P('tensor'), may hold values from -0.0625 to 0.0625
- b_down: bfloat16 [2048], P('tensor'), may hold values from -1.75 to 1.75
- d_hidden: bfloat16 [8, 2, 128, 2048], P('batch', None, 'seq', 'tensor'), may hold values from -6 to 6
- d_summary: bfloat16 [8, 2, 50, 2048], P('batch', None, None, 'tensor'), may hold values from -6 to 6
Outputs:
- hidden_out: bfloat16 [8, 2, 128, 2048], P('batch', None, 'seq', 'tensor')
- summary_out: bfloat16 [8, 2, 50, 2048], P('batch', None, None, 'tensor')
- grad_input: float32 [8, 2, 128, 2048], P('batch', None, 'seq', 'tensor')
- grad_embed: float32 [50, 2048], P(None, 'tensor')
- grad_ln1_gain: float32 [2048], P('tensor')
- grad_ln1_bias: float32 [2048], P('tensor')
- grad_query: float32 [2048, 2048], P(('batch', 'seq'), 'tensor')
- grad_query_bias: float32 [2048], P('tensor')
- grad_key: float32 [2048, 2048], P(('batch', 'seq'), 'tensor')
- grad_value: float32 [2048, 2048], P(('batch', 'seq'), 'tensor')
- grad_value_bias: float32 [2048], P('tensor')
- grad_out: float32 [2048, 2048], P('tensor', ('batch', 'seq'))
- grad_out_bias: float32 [2048], P('tensor')
- grad_ln2_gain: float32 [2048], P('tensor')
- grad_ln2_bias: float32 [2048], P('tensor')
- grad_up: float32 [2048, 8192], P(('batch', 'seq'), 'tensor')
- grad_up_bias: float32 [8192], P('tensor')
- grad_down: float32 [8192, 2048], P('tensor', ('batch', 'seq'))
- grad_down_bias: float32 [2048], P('tensor')
Inputs may be any that keep to these rules, and one draw needn't show every extreme that they name: Each item uses its first summary_counts[b] of the 50 slots; some item uses all 50 and some item uses 2 * 10.
All inputs are finite; a program needn't handle non-finite values.
Results may differ from a plain program's by a relative error of at most 0.015.
Values may be sent and summed in bfloat16 or wider, within the bound.
A program may use at most 320 MiB of HBM per device.

v0:
```python
import jax
import jax.numpy as jnp
from jax import lax
from jax.sharding import PartitionSpec as P

HD = 64


EPSILON = 1e-05
NEGATIVE = -1e30


def dot_nt(first, second):
    return lax.dot_general(
        first, second, (((1,), (1,)), ((), ())), preferred_element_type=jnp.float32
    )


def dot_tn(first, second):
    return lax.dot_general(
        first, second, (((0,), (0,)), ((), ())), preferred_element_type=jnp.float32
    )


def spread(block):
    return lax.all_gather(block, "tensor", axis=1, tiled=True)


def collect(partial_sum):
    return lax.psum_scatter(
        partial_sum.astype(jnp.bfloat16), "tensor", scatter_dimension=1, tiled=True
    ).astype(jnp.float32)


def row_totals(first, second):
    return lax.psum((first, second), "tensor")


def reduce_weights(grads):
    return (
        lax.psum_scatter(grads[0], ("batch", "seq"), scatter_dimension=0, tiled=True),
        lax.psum_scatter(grads[1], ("batch", "seq"), scatter_dimension=0, tiled=True),
        lax.psum_scatter(grads[2], ("batch", "seq"), scatter_dimension=0, tiled=True),
        lax.psum_scatter(grads[3], ("batch", "seq"), scatter_dimension=1, tiled=True),
        lax.psum_scatter(grads[4], ("batch", "seq"), scatter_dimension=0, tiled=True),
        lax.psum_scatter(grads[5], ("batch", "seq"), scatter_dimension=1, tiled=True),
    )


def norm_forward(resid):
    full_width = resid.shape[1] * lax.axis_size("tensor")
    totals, squares = row_totals(jnp.sum(resid, axis=1), jnp.sum(resid * resid, axis=1))
    row_mean = totals / full_width
    row_scale = lax.rsqrt(squares / full_width - row_mean * row_mean + EPSILON)
    return ((resid - row_mean[:, None]) * row_scale[:, None], row_scale)


def norm_backward(grad_act, normed, row_scale, gain_vec):
    full_width = grad_act.shape[1] * lax.axis_size("tensor")
    scaled = grad_act * gain_vec
    first, second = row_totals(jnp.sum(scaled, axis=1), jnp.sum(scaled * normed, axis=1))
    return row_scale[:, None] * (
        scaled - first[:, None] / full_width - normed * second[:, None] / full_width
    )


def split_heads(block):
    return block.reshape(block.shape[0], -1, HD).transpose(1, 0, 2)


def join_heads(block):
    return block.transpose(1, 0, 2).reshape(block.shape[1], -1)


def attend(queries, key_block, value_block, allowed, score_scale):

    def one_head(pieces):
        query_head, key_head, value_head = pieces
        scores = (
            jnp.einsum("qd,kd->qk", query_head, key_head, preferred_element_type=jnp.float32)
            * score_scale
        )
        scores = jnp.where(allowed, scores, NEGATIVE)
        row_max = jnp.max(scores, axis=1, keepdims=True)
        exponent = jnp.exp(scores - row_max)
        row_total = jnp.sum(exponent, axis=1, keepdims=True)
        weights = (exponent / row_total).astype(jnp.bfloat16)
        mixture = jnp.einsum("qk,kd->qd", weights, value_head, preferred_element_type=jnp.float32)
        return (mixture.astype(jnp.bfloat16), (row_max + jnp.log(row_total))[:, 0])

    mixture, logsum = lax.map(
        one_head, (split_heads(queries), split_heads(key_block), split_heads(value_block))
    )
    return (join_heads(mixture), logsum)


def attend_back(queries, key_block, value_block, grad_mixture, logsum, allowed, score_scale):

    def one_head(pieces):
        query_head, key_head, value_head, grad_head, logsum_head = pieces
        scores = (
            jnp.einsum("qd,kd->qk", query_head, key_head, preferred_element_type=jnp.float32)
            * score_scale
        )
        scores = jnp.where(allowed, scores, NEGATIVE)
        weights = jnp.exp(scores - logsum_head[:, None])
        grad_weights = jnp.einsum(
            "qd,kd->qk", grad_head, value_head, preferred_element_type=jnp.float32
        )
        value_grad = jnp.einsum(
            "qk,qd->kd", weights.astype(jnp.bfloat16), grad_head, preferred_element_type=jnp.float32
        )
        grad_scores = (
            weights * (grad_weights - jnp.sum(weights * grad_weights, axis=1, keepdims=True))
        ).astype(jnp.bfloat16)
        query_grad = (
            jnp.einsum("qk,kd->qd", grad_scores, key_head, preferred_element_type=jnp.float32)
            * score_scale
        )
        key_grad = (
            jnp.einsum("qk,qd->kd", grad_scores, query_head, preferred_element_type=jnp.float32)
            * score_scale
        )
        return (query_grad, key_grad, value_grad)

    query_grad, key_grad, value_grad = lax.map(
        one_head,
        (
            split_heads(queries),
            split_heads(key_block),
            split_heads(value_block),
            split_heads(grad_mixture),
            logsum,
        ),
    )
    return (join_heads(query_grad), join_heads(key_grad), join_heads(value_grad))


def column_sum(block):
    return jnp.sum(block.astype(jnp.float32), axis=0)


def local(
    hidden_in,
    summary_counts,
    summary_embed,
    ln1_gain,
    ln1_bias,
    w_query,
    b_query,
    w_key,
    w_value,
    b_value,
    w_out,
    b_out,
    ln2_gain,
    ln2_bias,
    w_up,
    b_up,
    w_down,
    b_down,
    d_hidden,
    d_summary,
):
    seq_count = lax.axis_size("seq")
    seq_rank = lax.axis_index("seq")
    owner_flag = (seq_rank == seq_count - 1).astype(jnp.float32)
    seg_count = hidden_in.shape[1]
    seg_rows = hidden_in.shape[2]
    slot_count = summary_embed.shape[0]
    own_rows = seg_rows + slot_count
    near_rows = seq_count * own_rows
    counted = summary_counts[0]
    slot_ids = jnp.arange(slot_count)
    live_slots = slot_ids < counted
    live = live_slots.astype(jnp.float32)
    score_scale = HD ** (-0.5)
    local_ids = jnp.arange(own_rows)
    query_pos = jnp.where(
        local_ids < seg_rows,
        seq_rank * seg_rows + local_ids,
        seq_count * seg_rows + local_ids - seg_rows,
    )
    whole_ids = jnp.arange(near_rows)
    source = whole_ids // own_rows
    within = whole_ids % own_rows
    key_pos = jnp.where(
        within < seg_rows, source * seg_rows + within, seq_count * seg_rows + within - seg_rows
    )
    key_live = (within < seg_rows) | (source == seq_count - 1) & (within - seg_rows < counted)
    seen = (key_pos[None, :] <= query_pos[:, None]) & key_live[None, :]
    seen_prefix = jnp.concatenate(
        [seen, jnp.broadcast_to(live_slots[None, :], (own_rows, slot_count))], 1
    )
    embedding = summary_embed.astype(jnp.float32)
    first_gain = ln1_gain.astype(jnp.float32)
    first_shift = ln1_bias.astype(jnp.float32)
    second_gain = ln2_gain.astype(jnp.float32)
    second_shift = ln2_bias.astype(jnp.float32)
    kept = []
    outputs = []
    summaries = []
    prefix = None
    for segment in range(seg_count):
        resid = jnp.concatenate([hidden_in[0, segment].astype(jnp.float32), embedding], 0)
        stacked = (
            resid if prefix is None else jnp.concatenate([resid, prefix.astype(jnp.float32)], 0)
        )
        normed1, scale1 = norm_forward(stacked)
        act1 = spread((normed1 * first_gain + first_shift).astype(jnp.bfloat16))
        queries = (
            jnp.dot(act1[:own_rows], w_query, preferred_element_type=jnp.float32)
            + b_query.astype(jnp.float32)
        ).astype(jnp.bfloat16)
        key_rows = jnp.dot(act1, w_key, preferred_element_type=jnp.float32).astype(jnp.bfloat16)
        value_rows = (
            jnp.dot(act1, w_value, preferred_element_type=jnp.float32) + b_value.astype(jnp.float32)
        ).astype(jnp.bfloat16)
        key_block, value_block = (
            lax.all_gather(key_rows[:own_rows], "seq", axis=0, tiled=True),
            lax.all_gather(value_rows[:own_rows], "seq", axis=0, tiled=True),
        )
        allowed = seen
        if prefix is not None:
            key_block = jnp.concatenate([key_block, key_rows[own_rows:]], 0)
            value_block = jnp.concatenate([value_block, value_rows[own_rows:]], 0)
            allowed = seen_prefix
        mixture, logsum = attend(queries, key_block, value_block, allowed, score_scale)
        middle = resid + (
            collect(jnp.dot(mixture, w_out, preferred_element_type=jnp.float32))
            + b_out.astype(jnp.float32)
        )
        normed2, scale2 = norm_forward(middle)
        act2 = spread((normed2 * second_gain + second_shift).astype(jnp.bfloat16))
        before = jnp.dot(act2, w_up, preferred_element_type=jnp.float32) + b_up.astype(jnp.float32)
        activated = jax.nn.gelu(before, approximate=True).astype(jnp.bfloat16)
        output_rows = middle + (
            collect(jnp.dot(activated, w_down, preferred_element_type=jnp.float32))
            + b_down.astype(jnp.float32)
        )
        outputs.append(output_rows[:seg_rows].astype(jnp.bfloat16))
        summary = (output_rows[seg_rows:] * live[:, None]).astype(jnp.bfloat16)
        prefix = summary
        summaries.append(summary)
        kept.append(
            (
                normed1,
                scale1,
                act1,
                queries,
                key_block,
                value_block,
                allowed,
                mixture,
                logsum,
                normed2,
                scale2,
                act2,
                before,
                activated,
            )
        )
    carried = jnp.zeros((slot_count, hidden_in.shape[3]), jnp.float32)
    input_grads = [None] * seg_count
    weight_totals = None
    small_parts = []
    for segment in reversed(range(seg_count)):
        (
            normed1,
            scale1,
            act1,
            queries,
            key_block,
            value_block,
            allowed,
            mixture,
            logsum,
            normed2,
            scale2,
            act2,
            before,
            activated,
        ) = kept[segment]
        out_grad = jnp.concatenate(
            [
                d_hidden[0, segment].astype(jnp.float32),
                (d_summary[0, segment].astype(jnp.float32) + carried)
                * (live * owner_flag)[:, None],
            ],
            0,
        )
        out_low = out_grad.astype(jnp.bfloat16)
        grad_down_shift = column_sum(out_low)
        out_full = spread(out_low)
        grad_down_weight = dot_tn(activated, out_full)
        _, gelu_pull = jax.vjp(lambda inner: jax.nn.gelu(inner, approximate=True), before)
        grad_before = gelu_pull(dot_nt(out_full, w_down))[0].astype(jnp.bfloat16)
        grad_up_shift = column_sum(grad_before)
        grad_up_weight = dot_tn(act2, grad_before)
        grad_act2 = collect(dot_nt(grad_before, w_up))
        grad_second_gain = jnp.sum(grad_act2 * normed2, axis=0)
        grad_second_shift = jnp.sum(grad_act2, axis=0)
        grad_middle = out_grad + norm_backward(grad_act2, normed2, scale2, second_gain)
        middle_low = grad_middle.astype(jnp.bfloat16)
        grad_out_shift = column_sum(middle_low)
        middle_full = spread(middle_low)
        grad_out_weight = dot_tn(mixture, middle_full)
        grad_mixture = dot_nt(middle_full, w_out).astype(jnp.bfloat16)
        query_grad, key_grad, value_grad = attend_back(
            queries, key_block, value_block, grad_mixture, logsum, allowed, score_scale
        )
        own_keys, own_values = (
            lax.psum_scatter(
                key_grad[:near_rows].astype(jnp.bfloat16), "seq", scatter_dimension=0, tiled=True
            ).astype(jnp.float32),
            lax.psum_scatter(
                value_grad[:near_rows].astype(jnp.bfloat16), "seq", scatter_dimension=0, tiled=True
            ).astype(jnp.float32),
        )
        query_low = query_grad.astype(jnp.bfloat16)
        keys_low = own_keys.astype(jnp.bfloat16)
        values_low = own_values.astype(jnp.bfloat16)
        own_act = act1[:own_rows]
        grad_query_weight = dot_tn(own_act, query_low)
        grad_query_shift = column_sum(query_low)
        grad_key_weight = dot_tn(own_act, keys_low)
        grad_value_weight = dot_tn(own_act, values_low)
        grad_value_shift = column_sum(values_low)
        grad_act1 = (
            dot_nt(query_low, w_query) + dot_nt(keys_low, w_key) + dot_nt(values_low, w_value)
        )
        row_weight = jnp.ones((own_rows,), jnp.float32)
        if segment > 0:
            prefix_keys, prefix_values = (
                lax.psum(key_grad[near_rows:].astype(jnp.bfloat16), "seq").astype(jnp.float32),
                lax.psum(value_grad[near_rows:].astype(jnp.bfloat16), "seq").astype(jnp.float32),
            )
            prefix_keys = prefix_keys.astype(jnp.bfloat16)
            prefix_values = prefix_values.astype(jnp.bfloat16)
            prefix_act = act1[own_rows:]
            grad_key_weight = grad_key_weight + owner_flag * dot_tn(prefix_act, prefix_keys)
            grad_value_weight = grad_value_weight + owner_flag * dot_tn(prefix_act, prefix_values)
            grad_value_shift = grad_value_shift + owner_flag * column_sum(prefix_values)
            grad_act1 = jnp.concatenate(
                [grad_act1, dot_nt(prefix_keys, w_key) + dot_nt(prefix_values, w_value)], 0
            )
            row_weight = jnp.concatenate(
                [row_weight, owner_flag * jnp.ones((slot_count,), jnp.float32)], 0
            )
        grad_act1 = collect(grad_act1)
        grad_first_gain = jnp.sum(grad_act1 * normed1 * row_weight[:, None], axis=0)
        grad_first_shift = jnp.sum(grad_act1 * row_weight[:, None], axis=0)
        grad_stacked = norm_backward(grad_act1, normed1, scale1, first_gain)
        grad_rows = grad_middle + grad_stacked[:own_rows]
        input_grads[segment] = grad_rows[:seg_rows]
        if segment > 0:
            carried = grad_stacked[own_rows:]
        small_parts.append(
            (
                grad_rows[seg_rows:],
                grad_first_gain,
                grad_first_shift,
                grad_query_shift,
                grad_value_shift,
                grad_out_shift,
                grad_second_gain,
                grad_second_shift,
                grad_up_shift,
                grad_down_shift,
            )
        )
        segment_weights = (
            grad_query_weight,
            grad_key_weight,
            grad_value_weight,
            grad_out_weight,
            grad_up_weight,
            grad_down_weight,
        )
        weight_totals = (
            segment_weights
            if weight_totals is None
            else jax.tree.map(lambda first, second: first + second, weight_totals, segment_weights)
        )
    weight_totals = reduce_weights(weight_totals)
    small_local = small_parts[0]
    for extra in small_parts[1:]:
        small_local = jax.tree.map(lambda first, second: first + second, small_local, extra)
    small_totals = lax.psum(small_local, ("batch", "seq"))
    hidden_out = jnp.stack(outputs)[None]
    summary_out = jnp.stack(summaries)[None]
    grad_input = jnp.stack(input_grads)[None]
    return (
        hidden_out,
        summary_out,
        grad_input,
        small_totals[0],
        small_totals[1],
        small_totals[2],
        weight_totals[0],
        small_totals[3],
        weight_totals[1],
        weight_totals[2],
        small_totals[4],
        weight_totals[3],
        small_totals[5],
        small_totals[6],
        small_totals[7],
        weight_totals[4],
        small_totals[8],
        weight_totals[5],
        small_totals[9],
    )


def solution(mesh):
    return jax.shard_map(
        local,
        mesh=mesh,
        in_specs=(
            P("batch", None, "seq", "tensor"),
            P("batch"),
            P(None, "tensor"),
            P("tensor"),
            P("tensor"),
            P(None, "tensor"),
            P("tensor"),
            P(None, "tensor"),
            P(None, "tensor"),
            P("tensor"),
            P("tensor", None),
            P("tensor"),
            P("tensor"),
            P("tensor"),
            P(None, "tensor"),
            P("tensor"),
            P("tensor", None),
            P("tensor"),
            P("batch", None, "seq", "tensor"),
            P("batch", None, None, "tensor"),
        ),
        out_specs=(
            P("batch", None, "seq", "tensor"),
            P("batch", None, None, "tensor"),
            P("batch", None, "seq", "tensor"),
            P(None, "tensor"),
            P("tensor"),
            P("tensor"),
            P(("batch", "seq"), "tensor"),
            P("tensor"),
            P(("batch", "seq"), "tensor"),
            P(("batch", "seq"), "tensor"),
            P("tensor"),
            P("tensor", ("batch", "seq")),
            P("tensor"),
            P("tensor"),
            P("tensor"),
            P(("batch", "seq"), "tensor"),
            P("tensor"),
            P("tensor", ("batch", "seq")),
            P("tensor"),
        ),
        check_vma=False,
    )
```

profile of v0, /device:TPU:0, one launch (start us, length us, event | category | flops | bytes accessed | tf_op | source)
XLA Modules:
  0.0 3030.3 jit_solution(7802005661660301164)
XLA Ops:
  48.9 34.2 %while.56 = (s32[]{:T(128)}, bf16[16,114,64]{1,2,0:T(8,128)(2,1)S(1)}, f32[16,114]{1,0:T(8,128)S(1)}, bf16[16,114,64]{2,1,0:T(8,128)(2,1)}, bf16[16,228,64]{2,1,...) while((s32[]{:T(128)}, ...), condition=%wide.region_7.8_spmd.clone, body=%wide.region_4.7_spmd.clone.sunk | while | flops 6921056 | bytes 501497 | solution.py:91
  151.4 12.0 all-gather.3
  191.4 91.1 %while.54 = (s32[]{:T(128)}, bf16[16,114,64]{1,2,0:T(8,128)(2,1)}, f32[16,114]{1,0:T(8,128)}, bf16[16,114,64]{2,1,0:T(8,128)(2,1)}, bf16[16,278,64]{2,1,0:T(8,12...) while((s32[]{:T(128)}, bf16[16,114,64]{1,2,0:T(8,128)(2,1)}, ...), condition=%wide.region_21.22_spmd, body=%wide.region_18.21_spmd.sunk | while | flops 8373872 | bytes 612989 | solution.py:91
  286.4 12.6 fusion.204
  305.1 12.6 convert_reduce_fusion.1
  317.7 12.5 convolution_convert_fusion.3
  330.3 9.9 convolution_convert_fusion.4
  363.8 123.4 %while.55 = (s32[]{:T(128)}, bf16[16,114,64]{1,2,0:T(8,128)(2,1)}, bf16[16,278,64]{1,2,0:T(8,128)(2,1)}, bf16[16,278,64]{1,2,0:T(8,128)(2,1)}, bf16[16,114,64]{2...) while((s32[]{:T(128)}, bf16[16,114,64]{1,2,0:T(8,128)(2,1)}, ...), condition=%wide.region_35.36_spmd, body=%wide.region_33.35_spmd.sunk | while | flops 20593084 | bytes 1528597 | solution.py:126
  499.8 47.4 %all-reduce.24.cloned.1.call-done = (bf16[50,1024]{0,1:T(8,128)(2,1)}, bf16[50,1024]{0,1:T(8,128)(2,1)}, bf16[228,1024]{0,1:T(8,128)(2,1)}, bf16[228,1024]{0,1:T(8,128)(2,1)}) async-done(((bf16[50,1024]{0,1:T(8,128)(2,1)}, bf16[50,1024]{0,1:T(8,128)(2,1)}, bf16[228,1024]{0,1:T(8,128)(2,1)}, bf16[228,1024]{0,1:T(8,128)(2,1)}), (bf16[50,1024]{0,1:T(8,128)(2,1)}, bf16[50,1024]{0,1:T(8,128)(2,1)}, ...) | async-done | bytes 1138704 | tf_op jit(solution)/shard_map/psum | solution.py:335
  577.3 14.2 convert_reduce_fusion
  591.6 12.5 convolution_convert_fusion.2
  626.8 110.8 %while.57 = (s32[]{:T(128)}, bf16[16,114,64]{1,2,0:T(8,128)(2,1)S(1)}, bf16[16,228,64]{1,2,0:T(8,128)(2,1)}, bf16[16,228,64]{1,2,0:T(8,128)(2,1)}, bf16[16,114,6...) while((s32[]{:T(128)}, ...), condition=%wide.region_52.53_spmd.clone, body=%wide.region_50.52_spmd.clone.sunk | while | flops 16942568 | bytes 1232525 | solution.py:126
  742.5 36.6 %all-reduce.22.cloned.1.call-done = (bf16[228,1024]{0,1:T(8,128)(2,1)}, bf16[228,1024]{0,1:T(8,128)(2,1)}) async-done(((bf16[228,1024]{0,1:T(8,128)(2,1)}, bf16[228,1024]{0,1:T(8,128)(2,1)}), (bf16[228,1024]{0,1:T(8,128)(2,1)}, bf16[228,1024]{0,1:T(8,128)(2,1)})) %all-reduce.22.cloned.1.call-update) | async-done | bytes 933904
  833.6 14.9 fusion.191
  848.5 24.8 convolution_add_fusion
  874.5 14.2 fusion.209
  888.7 24.8 convolution_add_fusion.1
  918.1 78.6 %all-reduce.5 = (f32[1024]{0:T(1024)}, f32[1024]{0:T(1024)}, f32[1024]{0:T(1024)}, f32[1024]{0:T(1024)}, f32[1024]{0:T(1024)}, /*index=5*/f32[1024]{0:T(1024)}, f32[1024]{0:T(1024)}, f32[4096]{0:T(1024)}, f32[1024]{0:T(1024)}) all-reduce(f32[1024]{0:T(1024)S(1)} %add.491, ...), channel_id=1, replica_groups=mesh['batch'=8,'seq'=2,'tensor'=2] {'batch','seq'}, use_global_device_ids=true, to_apply=%region_63.64 | all-reduce | flops 12288 | bytes 98304 | tf_op jit(solution)/shard_map/psum | solution.py:389
  997.5 94.0 %reduce-scatter.41.cloned.1.call-done = f32[1024,128]{1,0:T(8,128)} async-done(((f32[1024,2048]{1,0:T(8,128)}), f32[1024,128]{1,0:T(8,128)}) %reduce-scatter.41.cloned.1.call-update) | async-done | bytes 524304 | tf_op jit(solution)/shard_map/reduce_scatter | solution.py:44
  1091.5 183.2 %reduce-scatter.35.cloned.1.call-done = f32[128,1024]{1,0:T(8,128)} async-done(((f32[2048,1024]{1,0:T(8,128)}), f32[128,1024]{1,0:T(8,128)}) %reduce-scatter.35.cloned.1.call-update) | async-done | bytes 524304 | tf_op jit(solution)/shard_map/reduce_scatter | solution.py:41
  1274.7 183.1 %reduce-scatter.39.cloned.1.call-done = f32[128,1024]{1,0:T(8,128)} async-done(((f32[2048,1024]{1,0:T(8,128)}), f32[128,1024]{1,0:T(8,128)}) %reduce-scatter.39.cloned.1.call-update) | async-done | bytes 524304 | tf_op jit(solution)/shard_map/reduce_scatter | solution.py:43
  1457.8 183.1 %reduce-scatter.37.cloned.1.call-done = f32[128,1024]{1,0:T(8,128)} async-done(((f32[2048,1024]{1,0:T(8,128)}), f32[128,1024]{1,0:T(8,128)}) %reduce-scatter.37.cloned.1.call-update) | async-done | bytes 524304 | tf_op jit(solution)/shard_map/reduce_scatter | solution.py:42
  1640.9 688.8 %reduce-scatter.45.cloned.1.call-done = f32[4096,128]{1,0:T(8,128)} async-done(((f32[4096,2048]{1,0:T(8,128)}), f32[4096,128]{1,0:T(8,128)}) %reduce-scatter.45.cloned.1.call-update) | async-done | bytes 2097168 | tf_op jit(solution)/shard_map/reduce_scatter | solution.py:46
  2329.7 692.0 %reduce-scatter.43.cloned.1.call-done = f32[128,4096]{1,0:T(8,128)} async-done(((f32[2048,4096]{1,0:T(8,128)}), f32[128,4096]{1,0:T(8,128)}) %reduce-scatter.43.cloned.1.call-update) | async-done | bytes 2097168 | tf_op jit(solution)/shard_map/reduce_scatter | solution.py:45
  (871 shorter events, 660.2 us)
Async XLA Ops:
  7.2 89.5 %reduce-scatter.19.cloned.1.call-start = ((), (), s32[]{:S(2)}) async-start(), calls=%async_computation.14 | async-start | bytes 737280 | tf_op jit(solution)/shard_map/reduce_scatter | solution.py:30
  8.6 128.1 %copy-start.48 = (f32[1024]{0:T(1024)}, f32[1024]{0:T(1024)S(1)}, u32[]{:S(2)}) copy-start(f32[1024]{0:T(1024)S(1)} %convert_element_type.330) | copy-start | bytes 12292
  83.1 43.3 %copy-start.100 = (s32[228]{0:T(256)}, s32[228]{0:T(256)S(1)}, u32[]{:S(2)}) copy-start(s32[228]{0:T(256)S(1)} %get-tuple-element.1059) | copy-start | bytes 2740
  83.1 43.3 %copy-start.102 = (s32[114]{0:T(128)}, s32[114]{0:T(128)S(1)}, u32[]{:S(2)}) copy-start(s32[114]{0:T(128)S(1)} %get-tuple-element.1060) | copy-start | bytes 1372
  83.2 43.3 %copy-start.104 = (pred[228]{0:T(512)(128)(4,1)}, pred[228]{0:T(512)(128)(4,1)S(1)}, u32[]{:S(2)}) copy-start(pred[228]{0:T(512)(128)(4,1)S(1)} %get-tuple-element.1061) | copy-start | bytes 688
  87.4 44.1 %reduce-scatter.21.cloned.1.call-start = ((), (), s32[]{:S(2)}) async-start(), calls=%async_computation.15 | async-start | bytes 737280 | tf_op jit(solution)/shard_map/reduce_scatter | solution.py:30
  87.6 44.9 %copy-start.98 = (f32[50]{0:T(128)}, f32[50]{0:T(128)S(1)}, u32[]{:S(2)}) copy-start(f32[50]{0:T(128)S(1)} %fusion.186) | copy-start | bytes 604
  122.3 176.7 %reduce-scatter.23.cloned.1.call-start = ((), (), s32[]{:S(2)}) async-start(), calls=%async_computation.16 | async-start | bytes 737280 | tf_op jit(solution)/shard_map/reduce_scatter | solution.py:30
  126.5 159.9 %copy-start.9 = (bf16[114,2048]{1,0:T(8,128)(2,1)}, bf16[114,2048]{1,0:T(8,128)(2,1)S(1)}, u32[]{:S(2)}) copy-start(bf16[114,2048]{1,0:T(8,128)(2,1)S(1)} %all_gather.44) | copy-start | bytes 1400836
  286.3 53.9 %reduce-scatter.27.cloned.1.call-start = ((), (), s32[]{:S(2)}) async-start(), calls=%async_computation.18 | async-start | bytes 737280 | tf_op jit(solution)/shard_map/reduce_scatter | solution.py:30
  330.2 21.3 reduce-scatter.25.cloned.1.call-start
  340.2 207.0 %all-reduce.24.cloned.1.call-start = ((), (), s32[]{:S(2)}) async-start(), calls=%async_computation.30 | async-start | bytes 3145728 | tf_op jit(solution)/shard_map/psum | solution.py:335
  493.8 72.5 %reduce-scatter.29.cloned.1.call-start = ((), (), s32[]{:S(2)}) async-start(), calls=%async_computation.19 | async-start | bytes 1032192 | tf_op jit(solution)/shard_map/reduce_scatter | solution.py:30
  558.0 55.2 %reduce-scatter.31.cloned.1.call-start = ((), (), s32[]{:S(2)}) async-start(), calls=%async_computation.20 | async-start | bytes 737280 | tf_op jit(solution)/shard_map/reduce_scatter | solution.py:30
  604.0 175.1 %all-reduce.22.cloned.1.call-start = ((), (), s32[]{:S(2)}) async-start(), calls=%async_computation.29 | async-start | bytes 2097152
  737.6 56.6 %reduce-scatter.33.cloned.1.call-start = ((), (), s32[]{:S(2)}) async-start(), calls=%async_computation.21 | async-start | bytes 737280 | tf_op jit(solution)/shard_map/reduce_scatter | solution.py:30
  786.2 211.3 %all-reduce.20.cloned.1.call-start = ((), (), s32[]{:S(2)}) async-start(), calls=%async_computation.22 | async-start | bytes 458752 | tf_op jit(solution)/shard_map/psum | solution.py:389
  800.9 290.5 %reduce-scatter.41.cloned.1.call-start = ((), (), s32[]{:S(2)}) async-start(), calls=%async_computation.26 | async-start | bytes 8912896 | tf_op jit(solution)/shard_map/reduce_scatter | solution.py:44
  809.0 465.7 %reduce-scatter.35.cloned.1.call-start = ((), (), s32[]{:S(2)}) async-start(), calls=%async_computation.23 | async-start | bytes 8912896 | tf_op jit(solution)/shard_map/reduce_scatter | solution.py:41
  815.7 642.1 %reduce-scatter.39.cloned.1.call-start = ((), (), s32[]{:S(2)}) async-start(), calls=%async_computation.25 | async-start | bytes 8912896 | tf_op jit(solution)/shard_map/reduce_scatter | solution.py:43
  824.2 816.7 %reduce-scatter.37.cloned.1.call-start = ((), (), s32[]{:S(2)}) async-start(), calls=%async_computation.24 | async-start | bytes 8912896 | tf_op jit(solution)/shard_map/reduce_scatter | solution.py:42
  832.6 1497.1 %reduce-scatter.45.cloned.1.call-start = ((), (), s32[]{:S(2)}) async-start(), calls=%async_computation.28 | async-start | bytes 35651584 | tf_op jit(solution)/shard_map/reduce_scatter | solution.py:46
  873.4 2148.3 %reduce-scatter.43.cloned.1.call-start = ((), (), s32[]{:S(2)}) async-start(), calls=%async_computation.27 | async-start | bytes 35651584 | tf_op jit(solution)/shard_map/reduce_scatter | solution.py:45
  915.0 81.7 %copy-start.30 = (f32[114,1024]{1,0:T(8,128)S(1)}, f32[114,1024]{1,0:T(8,128)}, u32[]{:S(2)}) copy-start(f32[114,1024]{1,0:T(8,128)} %copy-done.29) | copy-start | bytes 1400836
  (130 other events, 678.8 us)
Sparse Core Ops, SparseCore 0:
  87.5 9.0 reduce-scatter.18
  122.4 9.0 reduce-scatter.20
  286.4 9.3 reduce-scatter.22
  330.3 9.3 reduce-scatter.26
  342.4 9.0 reduce-scatter.24
  493.9 53.1 all-reduce.23
  558.1 8.1 reduce-scatter.28
  604.2 9.0 reduce-scatter.30
  737.8 41.3 all-reduce.21
  786.3 7.9 reduce-scatter.32
  801.0 107.3 all-reduce.19
  911.3 180.1 reduce-scatter.40
  1094.4 180.1 reduce-scatter.34
  1277.5 180.2 reduce-scatter.38
  1460.6 180.2 reduce-scatter.36
  1643.8 685.8 reduce-scatter.44
  2332.6 689.0 reduce-scatter.42
where the time goes:
time: 3060 us; the launch traced here: 3030 us
  waiting for transfers between devices  2150 us (70%)
  matrix products  549 us (18%)
  blocking collectives  156 us (5%)
  local copies, waits for them, and re-layouts  108 us (4%)
  other arithmetic  47.7 us (2%)
    reduce_scatter x1, waiting for transfers between devices, reduce_weights(): lax.psum_scatter(grads[4], ('batch', 'seq'), scatter_dimension=0, tiled=T...  692 us
    reduce_scatter x1, waiting for transfers between devices, reduce_weights(): lax.psum_scatter(grads[5], ('batch', 'seq'), scatter_dimension=1, tiled=T...  689 us
    reduce_scatter x1, waiting for transfers between devices, reduce_weights(): lax.psum_scatter(grads[0], ('batch', 'seq'), scatter_dimension=0, tiled=T...  183 us
    reduce_scatter x1, waiting for transfers between devices, reduce_weights(): lax.psum_scatter(grads[2], ('batch', 'seq'), scatter_dimension=0, tiled=T...  183 us
    reduce_scatter x1, waiting for transfers between devices, reduce_weights(): lax.psum_scatter(grads[1], ('batch', 'seq'), scatter_dimension=0, tiled=T...  183 us
    dot_general x14, matrix products, dot_tn(): lax.dot_general(first, second, (((0,), (0,)), ((), ())), preferred_elemen...  112 us
    reduce_scatter x1, waiting for transfers between devices, reduce_weights(): lax.psum_scatter(grads[3], ('batch', 'seq'), scatter_dimension=1, tiled=T...  94 us
    dot_general x14, matrix products, dot_nt(): lax.dot_general(first, second, (((1,), (1,)), ((), ())), preferred_elemen...  85.9 us
  transfers between devices with their start and end apart: 17, of which 14 were waited for; matrix products, arithmetic and copies ran while one was open for 5% of the time, Pallas kernels for 0%

commit v1 on v0

v1 whole, which is shorter than its diff:
```python
import functools

import jax
import jax.numpy as jnp
from jax import lax
from jax.experimental import pallas as pl
from jax.experimental.pallas import tpu as pltpu
from jax.sharding import PartitionSpec as P

HD = 64
EPSILON = 1e-05
NEGATIVE = -1e30
MESH = pl.DeviceIdType.MESH
BF = jnp.bfloat16
F32 = jnp.float32
PAIR_BIT = 1


def flip(index, bit):
    weight = 1 << bit
    return index + weight - 2 * weight * lax.rem(index // weight, 2)


def bit_of(index, bit):
    return lax.rem(index // (1 << bit), 2)


def grads_kernel(
    bits,
    tiles,
    lhs_ref,
    rhs_ref,
    small_ref,
    out_ref,
    small_out_ref,
    send0,
    recv0,
    keep0,
    sends,
    recvs,
    keeps,
    send_p,
    recv_p,
    keep_p,
    send_x,
    recv_x,
    small_cur,
    small_recv,
    sem0,
    sems,
    sem_p,
    sem_x,
    sem_s,
):
    b, s, t = lax.axis_index("batch"), lax.axis_index("seq"), lax.axis_index("tensor")
    halving = list(range(bits - 1, PAIR_BIT, -1))
    at_y = (flip(b, 0), s, t)
    at_p = (flip(b, PAIR_BIT), s, t)
    at_x = (b, 1 - s, t)
    at_h = [(flip(b, bit), s, t) for bit in halving]
    partners = [at_y, at_p, at_x] + at_h
    barrier = pltpu.get_barrier_semaphore()
    for partner in partners:
        pl.semaphore_signal(barrier, inc=1, device_id=partner, device_id_type=MESH)
    pl.semaphore_wait(barrier, len(partners))

    features = lhs_ref.shape[1]
    chunk = features // (1 << bits)
    half_count = 1 << (bits - 1)
    mine = bit_of(b, 0)

    def operand(i):
        return i // 4 + ((i + 1) // 4 + 2) // 3

    def remote(src, dst, sem, partner):
        return pltpu.make_async_remote_copy(
            src_ref=src,
            dst_ref=dst,
            send_sem=sem.at[0],
            recv_sem=sem.at[1],
            device_id=partner,
            device_id_type=MESH,
        )

    def copy_y(i):
        return remote(send0.at[i], recv0.at[i], sem0.at[i], at_y)

    def copy_h(k, i):
        return remote(sends[k].at[i], recvs[k].at[i], sems[k].at[i], at_h[k])

    def copy_p(i):
        return remote(send_p.at[i], recv_p.at[i], sem_p.at[i], at_p)

    def copy_x(i):
        return remote(send_x.at[i], recv_x.at[i], sem_x.at[i], at_x)

    def product(i, j, side):
        start = pl.multiple_of((2 * j + side) * chunk, chunk)
        return jnp.dot(
            lhs_ref[operand(i), pl.ds(start, chunk), :],
            rhs_ref[i],
            preferred_element_type=F32,
        )

    small_cur[...] = small_ref[...]
    small_partners = [at_y] + at_h + [at_p]
    for k, partner in enumerate(small_partners):
        copy = remote(small_cur, small_recv.at[k], sem_s.at[k], partner)
        copy.start()

        if k == 0:

            @pl.loop(0, tiles)
            def _(i):
                @pl.loop(0, half_count)
                def _(j):
                    at = pl.ds(pl.multiple_of(j * chunk, chunk), chunk)
                    send0[i, at, :] = product(i, j, 1 - mine).astype(BF)

                copy_y(i).start()

        copy.wait()
        small_cur[...] = small_cur[...] + small_recv[k]
    last = len(small_partners)
    copy = remote(small_cur, small_recv.at[last], sem_s.at[last], at_x)
    copy.start()
    copy.wait()
    small_out_ref[s] = small_cur[...]
    small_out_ref[1 - s] = small_recv[last]

    stages = len(halving)

    def split(i, k, total, rows):
        bit = bit_of(b, halving[k])
        half = rows // 2
        keeps[k][i] = total(pl.multiple_of(bit * half, half), half)
        sends[k][i] = total(pl.multiple_of((1 - bit) * half, half), half).astype(BF)
        copy_h(k, i).start()

    def stage_first(i):
        copy_y(i).wait()

        @pl.loop(0, half_count)
        def _(j):
            at = pl.ds(pl.multiple_of(j * chunk, chunk), chunk)
            keep0[at, :] = product(i, j, mine) + recv0[i, at, :].astype(F32)

        split(i, 0, lambda at, n: keep0[pl.ds(at, n), :], half_count * chunk)

    def stage_next(k, i):
        copy_h(k, i).wait()

        def total(at, n):
            return keeps[k][i, pl.ds(at, n), :] + recvs[k][i, pl.ds(at, n), :].astype(F32)

        rows = (half_count * chunk) >> (k + 1)
        if k + 1 < stages:
            split(i, k + 1, total, rows)
        else:
            bit = bit_of(b, PAIR_BIT)
            keep_p[i] = total(pl.multiple_of(bit * chunk, chunk), chunk)
            send_p[i] = total(pl.multiple_of((1 - bit) * chunk, chunk), chunk).astype(BF)
            copy_p(i).start()

    def stage_pair(i):
        copy_p(i).wait()
        bit = bit_of(b, PAIR_BIT)
        half = chunk // 2
        mine_at = pl.multiple_of(s * half, half)
        other_at = pl.multiple_of((1 - s) * half, half)
        out_ref[i, s, bit] = keep_p[i, pl.ds(mine_at, half), :]
        out_ref[i, s, 1 - bit] = recv_p[i, pl.ds(mine_at, half), :].astype(F32)
        send_x[i, bit] = keep_p[i, pl.ds(other_at, half), :].astype(BF)
        send_x[i, 1 - bit] = recv_p[i, pl.ds(other_at, half), :]
        copy_x(i).start()

    def stage_last(i):
        copy_x(i).wait()
        out_ref[i, 1 - s] = recv_x[i].astype(F32)

    @pl.loop(0, tiles + stages + 2)
    def _(i):
        @pl.when(i < tiles)
        def _():
            stage_first(i)

        for k in range(stages):

            @pl.when((i >= k + 1) & (i < tiles + k + 1))
            def _():
                stage_next(k, i - (k + 1))

        @pl.when((i >= stages + 1) & (i < tiles + stages + 1))
        def _():
            stage_pair(i - (stages + 1))

        @pl.when(i >= stages + 2)
        def _():
            stage_last(i - (stages + 2))


def reduce_grads(lhs, rhs, small):
    count = lax.axis_size("batch")
    bits = count.bit_length() - 1
    tiles, _, width = rhs.shape
    features = lhs.shape[1]
    chunk = features // count
    rows = features // 2
    halving = bits - 1 - PAIR_BIT
    dma = pltpu.SemaphoreType.DMA
    pieces = [rows >> (k + 1) for k in range(halving)]
    scratch = [
        pltpu.VMEM((tiles, rows, width), BF),
        pltpu.VMEM((tiles, rows, width), BF),
        pltpu.VMEM((rows, width), F32),
        [pltpu.VMEM((tiles, n, width), BF) for n in pieces],
        [pltpu.VMEM((tiles, n, width), BF) for n in pieces],
        [pltpu.VMEM((tiles, n, width), F32) for n in pieces],
        pltpu.VMEM((tiles, chunk, width), BF),
        pltpu.VMEM((tiles, chunk, width), BF),
        pltpu.VMEM((tiles, chunk, width), F32),
        pltpu.VMEM((tiles, 2, chunk // 2, width), BF),
        pltpu.VMEM((tiles, 2, chunk // 2, width), BF),
        pltpu.VMEM(small.shape, F32),
        pltpu.VMEM((bits + 1,) + small.shape, F32),
        dma((tiles, 2)),
        [dma((tiles, 2)) for _ in pieces],
        dma((tiles, 2)),
        dma((tiles, 2)),
        dma((bits + 1, 2)),
    ]
    vmem = pl.BlockSpec(memory_space=pltpu.VMEM)
    return pl.pallas_call(
        functools.partial(grads_kernel, bits, tiles),
        name="weight_grads",
        out_shape=(
            jax.ShapeDtypeStruct((tiles, 2, 2, chunk // 2, width), F32),
            jax.ShapeDtypeStruct((2,) + small.shape, F32),
        ),
        in_specs=[vmem] * 3,
        out_specs=(vmem, vmem),
        scratch_shapes=scratch,
        compiler_params=pltpu.CompilerParams(
            collective_id=1, has_side_effects=True, vmem_limit_bytes=62 * 2**20
        ),
    )(lhs, rhs, small)


def dot_nn(a, b):
    return jnp.dot(a, b, preferred_element_type=F32)


def dot_nt(a, b):
    return lax.dot_general(a, b, (((1,), (1,)), ((), ())), preferred_element_type=F32)


def dot_tn(a, b):
    return lax.dot_general(a, b, (((0,), (0,)), ((), ())), preferred_element_type=F32)


def total4(x):
    return lax.psum(x, ("seq", "tensor"))


def stats(x):
    m = jnp.mean(x, axis=1, keepdims=True)
    e = jnp.mean(x * x, axis=1, keepdims=True)
    return m, lax.rsqrt(e - m * m + EPSILON)


def norm_back(d, xhat, r, g):
    q = d * g
    return r * (
        q - jnp.mean(q, axis=1, keepdims=True) - xhat * jnp.mean(q * xhat, axis=1, keepdims=True)
    )


def heads(x):
    return x.reshape(x.shape[0], -1, HD).transpose(1, 0, 2)


def unheads(x):
    return x.transpose(1, 0, 2).reshape(x.shape[1], -1)


def gelu_parts(v):
    c = 0.7978845608028654
    th = jnp.tanh(c * (v + 0.044715 * v * v * v))
    act = 0.5 * v * (1.0 + th)
    slope = 0.5 * (1.0 + th) + 0.5 * v * (1.0 - th * th) * c * (1.0 + 3 * 0.044715 * v * v)
    return act, slope


def local(
    hidden_in, summary_counts, summary_embed, ln1_gain, ln1_bias, w_query, b_query, w_key, w_value,
    b_value, w_out, b_out, ln2_gain, ln2_bias, w_up, b_up, w_down, b_down, d_hidden, d_summary,
):
    b, s, t = lax.axis_index("batch"), lax.axis_index("seq"), lax.axis_index("tensor")
    slots = summary_embed.shape[0]
    pad = 64
    seg_count = hidden_in.shape[1]
    toks = hidden_in.shape[2] * 2
    counted = summary_counts[0]
    full = lambda x: lax.all_gather(x, "tensor", axis=x.ndim - 1, tiled=True)
    tokens = lambda x: full(lax.all_gather(x[0], "seq", axis=1, tiled=True))
    padded = lambda x: jnp.pad(x, ((0, pad - x.shape[0]), (0, 0)))
    hid = tokens(hidden_in).astype(F32)
    dhid = tokens(d_hidden).astype(F32)
    dsum = full(d_summary[0]).astype(F32)
    emb = padded(full(summary_embed).astype(F32))
    g1, c1, g2, c2, bo, bd = (full(v).astype(F32)[None] for v in (ln1_gain, ln1_bias, ln2_gain, ln2_bias, b_out, b_down))
    nq = w_query.shape[1] // 2
    nu = w_up.shape[1] // 2
    cut = lambda x, n, axis: lax.dynamic_slice_in_dim(x, s * n, n, axis)
    wq, wk, wv = (cut(w, nq, 1) for w in (w_query, w_key, w_value))
    bq, bv = (cut(v, nq, 0).astype(F32)[None] for v in (b_query, b_value))
    wo = cut(w_out, nq, 0)
    wu, bu, wd = cut(w_up, nu, 1), cut(b_up, nu, 0).astype(F32)[None], cut(w_down, nu, 0)
    live = (jnp.arange(pad) < counted)
    livef = live.astype(F32)[:, None]
    n_own = toks + pad
    pos = jnp.arange(n_own)
    own_live = jnp.concatenate([jnp.ones(toks, bool), live])
    seen = (pos[None, :] <= pos[:, None]) & own_live[None, :]
    seen_p = jnp.concatenate([seen, jnp.broadcast_to(live[None], (n_own, pad))], 1)
    low = lambda x: x.astype(BF)
    kept, outs, sums = [], [], []
    prefix = None
    for seg in range(seg_count):
        rows = jnp.concatenate([hid[seg], emb], 0)
        stacked = rows if prefix is None else jnp.concatenate([rows, prefix.astype(F32)], 0)
        m1, r1 = stats(stacked)
        xh1 = (stacked - m1) * r1
        act1 = low(xh1 * g1 + c1)
        q = low(dot_nn(act1[:n_own], wq) + bq)
        k = low(dot_nn(act1, wk))
        v = low(dot_nn(act1, wv) + bv)
        sc = jnp.einsum("hqd,hkd->hqk", heads(q), heads(k), preferred_element_type=F32) * HD**-0.5
        sc = jnp.where((seen if prefix is None else seen_p)[None], sc, NEGATIVE)
        p = jax.nn.softmax(sc, axis=-1)
        mix = low(unheads(jnp.einsum("hqk,hkd->hqd", low(p), heads(v), preferred_element_type=F32)))
        mid = rows + total4(low(dot_nn(mix, wo))).astype(F32) + bo
        m2, r2 = stats(mid)
        xh2 = (mid - m2) * r2
        act2 = low(xh2 * g2 + c2)
        activated, slope = gelu_parts(dot_nn(act2, wu) + bu)
        activated = low(activated)
        out = mid + total4(low(dot_nn(activated, wd))).astype(F32) + bd
        outs.append(low(out[:toks]))
        prefix = low(out[toks:] * livef)
        sums.append(prefix[:slots])
        kept.append((xh1, r1, act1, q, k, v, p, mix, xh2, r2, act2, slope, activated))
    carried = jnp.zeros((pad, hid.shape[2]), F32)
    gin = [None] * seg_count
    got = [None] * seg_count
    small = 0.0
    f = hid.shape[2]
    quarter = f // 4
    fcut = lambda x: lax.dynamic_slice_in_dim(x, t * (f // 2) + s * quarter, quarter, 1)
    csum = lambda x: jnp.sum(x.astype(F32), axis=0, keepdims=True)
    for seg in reversed(range(seg_count)):
        xh1, r1, act1, q, k, v, p, mix, xh2, r2, act2, slope, activated = kept[seg]
        dout = jnp.concatenate([dhid[seg], (padded(dsum[seg]) + carried) * livef], 0)
        gd = low(dout)
        db = low(slope * dot_nt(gd, wd))
        da2 = total4(low(dot_nt(db, wu))).astype(F32)
        dmid = dout + norm_back(da2, xh2, r2, g2)
        gm = low(dmid)
        dmix = low(dot_nt(gm, wo))
        hq, hk, hv, hg = heads(q), heads(k), heads(v), heads(dmix)
        dp = jnp.einsum("hqd,hkd->hqk", hg, hv, preferred_element_type=F32)
        ds = low(p * (dp - jnp.sum(p * dp, axis=-1, keepdims=True)))
        ein = functools.partial(jnp.einsum, preferred_element_type=F32)
        dq = low(unheads(ein("hqk,hkd->hqd", ds, hk)) * HD**-0.5)
        dk = low(unheads(ein("hqk,hqd->hkd", ds, hq)) * HD**-0.5)
        dv = low(unheads(ein("hqk,hqd->hkd", low(p), hg)))
        da1 = dot_nt(dk, wk) + dot_nt(dv, wv)
        da1 = da1.at[:n_own].add(dot_nt(dq, wq))
        da1 = total4(low(da1)).astype(F32)
        dst = norm_back(da1, xh1, r1, g1)
        drows = dmid + dst[:n_own]
        gin[seg] = drows[:toks]
        if seg > 0:
            carried = dst[n_own:]
        fs = [drows[toks : toks + slots]] + [
            jnp.sum(a, axis=0, keepdims=True)
            for a in (da1 * xh1, da1, gm.astype(F32), da2 * xh2, da2, gd.astype(F32))
        ]
        fs = fcut(jnp.concatenate(fs, 0))
        us = [csum(dq), csum(dv), csum(db).reshape(4, -1)]
        rest = -(fs.shape[0] + 6) % 8
        small = small + jnp.concatenate([fs] + us + [jnp.zeros((rest, quarter), F32)], 0)
        got[seg] = (act1, gm, act2, gd, dq, dk, dv, mix, db, activated)

    def stack(n, prefix_rows):
        first, second = got[0][n], got[1][n]
        if prefix_rows:
            body = [first, second] if second.shape[0] > n_own else [first, second, jnp.zeros((pad, second.shape[1]), BF)]
        else:
            body = [first, second, jnp.zeros((pad, first.shape[1]), BF)]
        return jnp.concatenate(body, 0)

    lhs = jnp.stack([stack(0, True)] + [stack(n, False) for n in (1, 2, 3)])
    right = [stack(4, True), stack(5, True), stack(6, True), stack(7, False), stack(8, False), stack(9, False)]
    count = lax.axis_size("batch")
    pair = [(i, i ^ (1 << PAIR_BIT)) for i in range(count)]
    zl = bit_of(b, PAIR_BIT)
    half = lambda x, side: lax.dynamic_slice_in_dim(x, side * (x.shape[1] // 2), x.shape[1] // 2, 1)
    width = nq // 2
    tile = lambda x: x.reshape(x.shape[0], -1, width).transpose(1, 0, 2)
    keep = jnp.concatenate([tile(half(x, zl)) for x in right], 0)
    give = jnp.concatenate([tile(half(x, 1 - zl)) for x in right], 0)
    take = lax.ppermute(give, "batch", pair)
    lhs_take = lax.ppermute(lhs, "batch", pair)
    rhs = jnp.concatenate([keep, take], 1)
    lhs = jnp.concatenate([lhs, lhs_take], 1).transpose(0, 2, 1)
    w, sm = reduce_grads(lhs, rhs, small)
    def place(lo, hi):
        x = w[lo:hi]
        return x.transpose(3, 1, 2, 0, 4).reshape(x.shape[3], -1)
    per = nu // 2 // width
    gq, gk, gv, go = (place(i, i + 1) for i in range(4))
    gu, gdn = place(4, 4 + per), place(4 + per, 4 + 2 * per)
    sm = sm.transpose(1, 0, 2)
    fl = lambda r: sm[r].reshape(-1)
    n = slots
    bup = sm[n + 8 : n + 12].transpose(1, 0, 2).reshape(-1)
    cutf = lambda x: lax.dynamic_slice_in_dim(x, t * (f // 2), f // 2, x.ndim - 1)
    own = lambda x: lax.dynamic_slice_in_dim(cutf(x), s * (toks // 2), toks // 2, 1)
    return (
        own(jnp.stack(outs))[None], cutf(jnp.stack(sums))[None], own(jnp.stack(gin))[None],
        sm[:n].reshape(n, -1), fl(n), fl(n + 1), gq, fl(n + 6), gk, gv, fl(n + 7), go.T, fl(n + 2),
        fl(n + 3), fl(n + 4), gu, bup, gdn.T, fl(n + 5),
    )


def solution(mesh):
    return jax.shard_map(
        local,
        mesh=mesh,
        in_specs=(
            P("batch", None, "seq", "tensor"),
            P("batch"),
            P(None, "tensor"),
            P("tensor"),
            P("tensor"),
            P(None, "tensor"),
            P("tensor"),
            P(None, "tensor"),
            P(None, "tensor"),
            P("tensor"),
            P("tensor", None),
            P("tensor"),
            P("tensor"),
            P("tensor"),
            P(None, "tensor"),
            P("tensor"),
            P("tensor", None),
            P("tensor"),
            P("batch", None, "seq", "tensor"),
            P("batch", None, None, "tensor"),
        ),
        out_specs=(
            P("batch", None, "seq", "tensor"),
            P("batch", None, None, "tensor"),
            P("batch", None, "seq", "tensor"),
            P(None, "tensor"),
            P("tensor"),
            P("tensor"),
            P(("batch", "seq"), "tensor"),
            P("tensor"),
            P(("batch", "seq"), "tensor"),
            P(("batch", "seq"), "tensor"),
            P("tensor"),
            P("tensor", ("batch", "seq")),
            P("tensor"),
            P("tensor"),
            P("tensor"),
            P(("batch", "seq"), "tensor"),
            P("tensor"),
            P("tensor", ("batch", "seq")),
            P("tensor"),
        ),
        check_vma=False,
    )
```

time: 3060 us -> 898 us (0.29)
  waiting for transfers between devices: 2150 us -> 352 us
  matrix products: 549 us -> 100 us
  Pallas kernels: 0 us -> 187 us
  blocking collectives: 156 us -> 35.3 us
    reduce_scatter x14 -> x0, waiting for transfers between devices: 2060 us -> none  [the longest x1 692 us: reduce_weights(): lax.psum_scatter(grads[4], ('batch', 'seq'), scatter_dimension=0, tiled=T...]
    dot_general x264 -> x34, matrix products: 549 us -> 95.1 us  [the longest x12 39.6 us: dot_nn(): return jnp.dot(a, b, preferred_element_type=F32)]
    pallas_call x0 -> x1, Pallas kernels: none -> 187 us  [reduce_grads(): pl.pallas_call(functools.partial(grads_kernel, bits, tiles), name='weight...]
    psum x2 -> x7, waiting for transfers between devices: 47.4 us -> 205 us  [total4(): return lax.psum(x, ('seq', 'tensor'))]
    ppermute x0 -> x2, waiting for transfers between devices: none -> 147 us  [the longest x1 147 us: local(): take = lax.ppermute(give, 'batch', pair)]
    psum x9 -> x0, blocking collectives: 98.4 us -> none  [the longest x1 78.6 us: local(): small_totals = lax.psum(small_local, ('batch', 'seq'))]
    unnamed x18 -> x9, waiting for transfers between devices: 36.9 us -> 0.15 us
    transpose x0 -> x9, local copies, waits for them, and re-layouts: none -> 34.6 us  [the longest x1 20.8 us: local(): lhs = jnp.concatenate([lhs, lhs_take], 1).transpose(0, 2, 1)]
  transfers between devices with their start and end apart: 17 -> 11, of which waited for: 14 -> 8; matrix products, arithmetic and copies ran while one was open for 5% -> 11% of each run, Pallas kernels for 0% -> 0%
where the time goes in v1:
time: 898 us; the launch traced here: 889 us
  waiting for transfers between devices  352 us (39%)
  Pallas kernels  187 us (21%)
  local copies, waits for them, and re-layouts  118 us (13%)
  matrix products  100 us (11%)
  other arithmetic  76.2 us (8%)
  blocking collectives  35.3 us (4%)
  between operations  16.4 us (2%)
    psum x7, waiting for transfers between devices, total4(): return lax.psum(x, ('seq', 'tensor'))  205 us
    pallas_call x1, Pallas kernels, reduce_grads(): pl.pallas_call(functools.partial(grads_kernel, bits, tiles), name='weight...  187 us
    ppermute x1, waiting for transfers between devices, local(): take = lax.ppermute(give, 'batch', pair)  147 us
    dot_general x12, matrix products, dot_nn(): return jnp.dot(a, b, preferred_element_type=F32)  39.6 us
    unnamed x291, local copies, waits for them, and re-layouts  38 us
    dot_general x12, matrix products, dot_nt(): lax.dot_general(a, b, (((1,), (1,)), ((), ())), preferred_element_type=F32)  36.4 us
    transpose x1, local copies, waits for them, and re-layouts, local(): lhs = jnp.concatenate([lhs, lhs_take], 1).transpose(0, 2, 1)  20.8 us
    all_gather x2, blocking collectives, local(): tokens = lambda x: full(lax.all_gather(x[0], 'seq', axis=1, tiled=True))  20.5 us
  transfers between devices with their start and end apart: 11, of which 8 were waited for; matrix products, arithmetic and copies ran while one was open for 11% of the time, Pallas kernels for 0%

profile of v1, /device:TPU:0, one launch (start us, length us, event | category | flops | bytes accessed | tf_op | source)
XLA Modules:
  0.0 888.5 jit_solution(8206552376046064013)
XLA Ops:
  7.3 12.0 %all-gather = bf16[1,2,128,1024]{3,2,1,0:T(8,128)(2,1)} all-gather(bf16[1,2,64,1024]{3,2,1,0:T(8,128)(2,1)} %param.26), channel_id=2, replica_groups=mesh['batch'=8,'seq'=2,'tensor'=2] {'seq'}, dimensions={2}, use_global_device_ids=true | all-gather | bytes 786432 | tf_op jit(solution)/shard_map/all_gather | solution.py:305
  19.4 8.5 all-gather.2
  74.6 31.8 %all-reduce.13.cloned.1.call-done = bf16[192,2048]{1,0:T(8,128)(2,1)} async-done(((bf16[192,2048]{1,0:T(8,128)(2,1)}), bf16[192,2048]{1,0:T(8,128)(2,1)}) %all-reduce.13.cloned.1.call-update) | async-done | bytes 786448 | tf_op jit(solution)/shard_map/psum | solution.py:262
  108.7 7.0 multiply_convert_fusion.3
  116.7 6.1 fusion.40
  126.3 31.3 %all-reduce.15.cloned.1.call-done = bf16[192,2048]{1,0:T(8,128)(2,1)} async-done(((bf16[192,2048]{1,0:T(8,128)(2,1)}), bf16[192,2048]{1,0:T(8,128)(2,1)}) %all-reduce.15.cloned.1.call-update) | async-done | bytes 786448 | tf_op jit(solution)/shard_map/psum | solution.py:262
  179.9 31.4 %all-reduce.17.cloned.1.call-done = bf16[192,2048]{1,0:T(8,128)(2,1)} async-done(((bf16[192,2048]{1,0:T(8,128)(2,1)}), bf16[192,2048]{1,0:T(8,128)(2,1)}) %all-reduce.17.cloned.1.call-update) | async-done | bytes 786448 | tf_op jit(solution)/shard_map/psum | solution.py:262
  213.6 6.8 multiply_convert_fusion.2
  220.5 7.1 convert_reduce_fusion.7
  234.4 32.7 %all-reduce.19.cloned.1.call-done = bf16[192,2048]{1,0:T(8,128)(2,1)} async-done(((bf16[192,2048]{1,0:T(8,128)(2,1)}), bf16[192,2048]{1,0:T(8,128)(2,1)}) %all-reduce.19.cloned.1.call-update) | async-done | bytes 786448 | tf_op jit(solution)/shard_map/psum | solution.py:262
  275.3 4.7 convert_reduce_fusion.12
  296.4 6.4 fusion.43
  307.4 20.4 %all-reduce.21.cloned.1.call-done = bf16[256,2048]{1,0:T(8,128)(2,1)} async-done(((bf16[256,2048]{1,0:T(8,128)(2,1)}), bf16[256,2048]{1,0:T(8,128)(2,1)}) %all-reduce.21.cloned.1.call-update) | async-done | bytes 1048592 | tf_op jit(solution)/shard_map/psum | solution.py:262
  335.1 7.8 convert_reduce_fusion.4
  343.5 7.5 fusion.37
  359.1 27.1 %all-reduce.23.cloned.1.call-done = bf16[192,2048]{1,0:T(8,128)(2,1)} async-done(((bf16[192,2048]{1,0:T(8,128)(2,1)}), bf16[192,2048]{1,0:T(8,128)(2,1)}) %all-reduce.23.cloned.1.call-update) | async-done | bytes 786448 | tf_op jit(solution)/shard_map/psum | solution.py:262
  401.6 7.1 maximum_maximum_fusion.1
  442.5 30.4 %all-reduce.25.cloned.1.call-done = (bf16[192,2048]{1,0:T(8,128)(2,1)}, bf16[192,2048]{1,0:T(8,128)(2,1)}) async-done(((bf16[192,2048]{1,0:T(8,128)(2,1)}, bf16[192,2048]{1,0:T(8,128)(2,1)}), (bf16[192,2048]{1,0:T(8,128)(2,1)}, bf16[192,2048]{1,0:T(8,128)(2,1)})) %all-reduce.25.cloned.1.call-update) | async-done | bytes 1572880 | tf_op jit(solution)/shard_map/psum | solution.py:262
  484.6 146.6 %collective-permute-done.1 = bf16[12,448,256]{2,1,0:T(8,128)(2,1)} collective-permute-done((bf16[12,448,256]{2,1,0:T(8,128)(2,1)}, bf16[12,448,256]{2,1,0:T(8,128)(2,1)}, u32[]{:S(2)}, u32[]{:S(2)}) %collective-permute-start.1) | collective-permute-done | bytes 2752544 | tf_op jit(solution)/shard_map/ppermute | solution.py:413
  631.1 5.3 pad_maximum_fusion.1.rhs_ref
  636.5 12.9 %maximum_bitcast_fusion = bf16[4,2048,896]{1,2,0:T(8,128)(2,1)} fusion(bf16[4,448,2048]{2,1,0:T(8,128)(2,1)} %collective-permute-done, bf16[1,448,2048]{2,1,0:T(8,128)(2,1)S(1)} %copy-done.10, bf16[1,448,2048]{2,1,0:T(8,128)(2,1)S(1)} %copy-done.8, bf16[1,448,2048]{2,1,0:T(8,128)(2,1)S(1)} %copy-done.12, bf16[1,448,2048]{2,1,0:T(8,128)(2,1)S(1)} %copy-done.14), kind=kLoop, calls=%fused_computation.2 | loop fusion | flops 73400320 | bytes 29360128 | tf_op jit(solution)/shard_map/transpose | solution.py:416
  649.4 20.8 %copy.128.lhs_ref = bf16[4,2048,896]{2,1,0:T(8,128)(2,1)} copy(bf16[4,2048,896]{1,2,0:T(8,128)(2,1)} %maximum_bitcast_fusion) | data formatting | bytes 29360128 | tf_op jit(solution)/shard_map/transpose | solution.py:416
  670.2 186.7 %weight_grads.1 = (f32[12,2,2,128,256]{4,3,2,1,0:T(8,128)}, f32[2,64,512]{2,1,0:T(8,128)}) custom-call(bf16[4,2048,896]{2,1,0:T(8,128)(2,1)} %copy.128.lhs_ref, bf16[12,896,256]{2,1,0:T(8,128)(2,1)} %pad_maximum_fusion.1.rhs_ref, f32[64,512]{1,0:T(8,128)} %add.353.small_ref), custom_call_target="tpu_custom_call" | custom-call | tf_op jit(solution)/shard_map/weight_grads/pallas_call | solution.py:233
  862.1 4.7 slice_bitcast_fusion
  (476 shorter events, 209.1 us)
Async XLA Ops:
  7.3 35.5 %copy-start.97 = (bf16[50,1024]{1,0:T(8,128)(2,1)S(1)}, bf16[50,1024]{1,0:T(8,128)(2,1)}, u32[]{:S(2)}) copy-start(bf16[50,1024]{1,0:T(8,128)(2,1)} %param.28) | copy-start | bytes 307204
  7.3 37.5 %copy-start.95 = (bf16[1,2,50,1024]{3,1,2,0:T(2,128)(2,1)S(1)}, bf16[1,2,50,1024]{3,1,2,0:T(2,128)(2,1)}, u32[]{:S(2)}) copy-start(bf16[1,2,50,1024]{3,1,2,0:T(2,128)(2,1)} %param.45) | copy-start | bytes 614404
  7.3 41.6 %all-gather.8.cloned.1.call-start = ((), (), s32[]{:S(2)}) async-start(), calls=%async_computation.6 | async-start | bytes 1572864 | tf_op jit(solution)/shard_map/all_gather | solution.py:304
  19.4 52.5 %all-gather.10.cloned.1.call-start = ((), (), s32[]{:S(2)}) async-start(), calls=%async_computation.7 | async-start | bytes 1572864 | tf_op jit(solution)/shard_map/all_gather | solution.py:304
  27.9 78.5 %all-reduce.13.cloned.1.call-start = ((), (), s32[]{:S(2)}) async-start(), calls=%async_computation | async-start | bytes 1572864 | tf_op jit(solution)/shard_map/psum | solution.py:262
  70.0 87.6 %all-reduce.15.cloned.1.call-start = ((), (), s32[]{:S(2)}) async-start(), calls=%async_computation.1 | async-start | bytes 1572864 | tf_op jit(solution)/shard_map/psum | solution.py:262
  71.8 34.6 %copy-start.101 = (f32[2048]{0:T(1024)S(1)}, f32[2048]{0:T(1024)}, u32[]{:S(2)}) copy-start(f32[2048]{0:T(1024)} %convert_element_type.314) | copy-start | bytes 24580
  74.6 33.4 %copy-start.100 = (f32[2048]{0:T(1024)S(1)}, f32[2048]{0:T(1024)}, u32[]{:S(2)}) copy-start(f32[2048]{0:T(1024)} %convert_element_type.316) | copy-start | bytes 24580
  108.0 49.6 %copy-start = (f32[192,2048]{1,0:T(8,128)}, f32[192,2048]{1,0:T(8,128)S(1)}, u32[]{:S(2)}) copy-start(f32[192,2048]{1,0:T(8,128)S(1)} %get-tuple-element.132) | copy-start | bytes 4718596
  122.8 34.8 %copy-start.98 = (f32[2048]{0:T(1024)S(1)}, f32[2048]{0:T(1024)}, u32[]{:S(2)}) copy-start(f32[2048]{0:T(1024)} %convert_element_type.322) | copy-start | bytes 24580
  122.8 88.6 %all-reduce.17.cloned.1.call-start = ((), (), s32[]{:S(2)}) async-start(), calls=%async_computation.2 | async-start | bytes 1572864 | tf_op jit(solution)/shard_map/psum | solution.py:262
  126.3 33.9 %copy-start.120 = (f32[64]{0:T(128)S(1)}, f32[64]{0:T(128)}, u32[]{:S(2)}) copy-start(f32[64]{0:T(128)} %fusion.228) | copy-start | bytes 772
  167.5 107.8 %copy-start.69 = (bf16[192,512]{0,1:T(8,128)(2,1)}, bf16[192,512]{0,1:T(8,128)(2,1)S(1)}, u32[]{:S(2)}) copy-start(bf16[192,512]{0,1:T(8,128)(2,1)S(1)} %copy.106) | copy-start | bytes 589828
  176.5 90.5 %all-reduce.19.cloned.1.call-start = ((), (), s32[]{:S(2)}) async-start(), calls=%async_computation.3 | async-start | bytes 1572864 | tf_op jit(solution)/shard_map/psum | solution.py:262
  232.3 95.5 %all-reduce.21.cloned.1.call-start = ((), (), s32[]{:S(2)}) async-start(), calls=%async_computation.4 | async-start | bytes 2097152 | tf_op jit(solution)/shard_map/psum | solution.py:262
  291.4 94.7 %all-reduce.23.cloned.1.call-start = ((), (), s32[]{:S(2)}) async-start(), calls=%async_computation.5 | async-start | bytes 1572864 | tf_op jit(solution)/shard_map/psum | solution.py:262
  351.0 121.8 %all-reduce.25.cloned.1.call-start = ((), (), s32[]{:S(2)}) async-start(), calls=%async_computation.8 | async-start | bytes 3145728 | tf_op jit(solution)/shard_map/psum | solution.py:262
  355.5 33.8 %copy-start.105 = (f32[2,512]{1,0:T(2,128)}, f32[2,512]{1,0:T(2,128)S(1)}, u32[]{:S(2)}) copy-start(f32[2,512]{1,0:T(2,128)S(1)} %broadcast.280) | copy-start | bytes 12292
  413.2 223.2 %collective-permute-start = (bf16[4,448,2048]{2,1,0:T(8,128)(2,1)}, bf16[4,448,2048]{2,1,0:T(8,128)(2,1)}, u32[]{:S(2)}, u32[]{:S(2)}) collective-permute-start(bf16[4,448,2048]{2,1,0:T(8,128)(2,1)} %pad_maximum_fusion), channel_id=1, source_target_pairs={{0,8},{4,12},{8,0},{12,4},{16,24},{20,28},{24,16},{28,20},{1,9},{5... | collective-permute-start | bytes 22020104 | tf_op jit(solution)/shard_map/ppermute | solution.py:414
  439.9 191.2 %collective-permute-start.1 = (bf16[12,448,256]{2,1,0:T(8,128)(2,1)}, bf16[12,448,256]{2,1,0:T(8,128)(2,1)}, u32[]{:S(2)}, u32[]{:S(2)}) collective-permute-start(bf16[12,448,256]{2,1,0:T(8,128)(2,1)} %fusion.165), channel_id=1, source_target_pairs={{0,8},{4,12},{8,0},{12,4},{16,24},{20,28},{24,16},{28,20},{1,9},{5... | collective-permute-start | bytes 8257544 | tf_op jit(solution)/shard_map/ppermute | solution.py:413
  484.6 151.9 %copy-start.8 = (bf16[1,448,2048]{2,1,0:T(8,128)(2,1)S(1)}, bf16[1,448,2048]{2,1,0:T(8,128)(2,1)}, u32[]{:S(2)}) copy-start(bf16[1,448,2048]{2,1,0:T(8,128)(2,1)} %copy-done.7) | copy-start | bytes 5505028
  484.6 151.9 %copy-start.10 = (bf16[1,448,2048]{2,1,0:T(8,128)(2,1)S(1)}, bf16[1,448,2048]{2,1,0:T(8,128)(2,1)}, u32[]{:S(2)}) copy-start(bf16[1,448,2048]{2,1,0:T(8,128)(2,1)} %copy-done.9) | copy-start | bytes 5505028
  484.6 151.9 %copy-start.12 = (bf16[1,448,2048]{2,1,0:T(8,128)(2,1)S(1)}, bf16[1,448,2048]{2,1,0:T(8,128)(2,1)}, u32[]{:S(2)}) copy-start(bf16[1,448,2048]{2,1,0:T(8,128)(2,1)} %copy-done.11) | copy-start | bytes 5505028
  484.6 151.9 %copy-start.14 = (bf16[1,448,2048]{2,1,0:T(8,128)(2,1)S(1)}, bf16[1,448,2048]{2,1,0:T(8,128)(2,1)}, u32[]{:S(2)}) copy-start(bf16[1,448,2048]{2,1,0:T(8,128)(2,1)} %maximum_bitcast_fusion.1) | copy-start | bytes 5505028
  (127 other events, 595.4 us)
Sparse Core Ops, SparseCore 0:
  19.5 9.3 all-gather.7
  30.4 10.1 all-gather.9
  70.1 36.3 all-reduce.12
  122.9 34.6 all-reduce.14
  176.7 34.6 all-reduce.16
  232.4 34.6 all-reduce.18
  291.6 36.1 all-reduce.20
  351.1 34.9 all-reduce.22
  430.6 42.1 all-reduce.24

commit v2 on v1

v2 whole, which is shorter than its diff:
```python
import functools

import jax
import jax.numpy as jnp
from jax import lax
from jax.experimental import pallas as pl
from jax.experimental.pallas import tpu as pltpu
from jax.sharding import PartitionSpec as P

HD = 64
EPSILON = 1e-05
NEGATIVE = -1e30
MESH = pl.DeviceIdType.MESH
BF = jnp.bfloat16
F32 = jnp.float32
PAIR_BIT = 1


def flip(index, bit):
    weight = 1 << bit
    return index + weight - 2 * weight * lax.rem(index // weight, 2)


def bit_of(index, bit):
    return lax.rem(index // (1 << bit), 2)


def dot_nt(a, b):
    return lax.dot_general(a, b, (((1,), (1,)), ((), ())), preferred_element_type=F32)


def dot_tn(a, b):
    return lax.dot_general(a, b, (((0,), (0,)), ((), ())), preferred_element_type=F32)


def grads_kernel(
    bits,
    tiles,
    width,
    la_ref,
    lx_ref,
    ra_ref,
    rb_ref,
    small_ref,
    out_ref,
    small_out_ref,
    send0,
    recv0,
    keep0,
    both,
    sends,
    recvs,
    keeps,
    send_p,
    recv_p,
    keep_p,
    send_x,
    recv_x,
    small_cur,
    small_recv,
    sem0,
    sems,
    sem_p,
    sem_x,
    sem_s,
):
    b, s, t = lax.axis_index("batch"), lax.axis_index("seq"), lax.axis_index("tensor")
    halving = list(range(bits - 1, PAIR_BIT, -1))
    at_y = (flip(b, 0), s, t)
    at_p = (flip(b, PAIR_BIT), s, t)
    at_x = (b, 1 - s, t)
    at_h = [(flip(b, bit), s, t) for bit in halving]
    partners = [at_y, at_p, at_x] + at_h
    barrier = pltpu.get_barrier_semaphore()
    for partner in partners:
        pl.semaphore_signal(barrier, inc=1, device_id=partner, device_id_type=MESH)
    pl.semaphore_wait(barrier, len(partners))

    features = la_ref.shape[1]
    inner = ra_ref.shape[1] // width
    chunk = features // (1 << bits)
    half_count = 1 << (bits - 1)
    mine = bit_of(b, 0)

    def remote(src, dst, sem, partner):
        return pltpu.make_async_remote_copy(
            src_ref=src,
            dst_ref=dst,
            send_sem=sem.at[0],
            recv_sem=sem.at[1],
            device_id=partner,
            device_id_type=MESH,
        )

    def copy_y(i):
        return remote(send0.at[i], recv0.at[i], sem0.at[i], at_y)

    def copy_h(k, i):
        return remote(sends[k].at[i], recvs[k].at[i], sems[k].at[i], at_h[k])

    def copy_p(i):
        return remote(send_p.at[i], recv_p.at[i], sem_p.at[i], at_p)

    def copy_x(i):
        return remote(send_x.at[i], recv_x.at[i], sem_x.at[i], at_x)

    per = (tiles - inner - 1) // 2

    def product(i, side, put):
        def blocks(left, right):
            @pl.loop(0, half_count)
            def _(j):
                at = pl.ds(pl.multiple_of(j * chunk, chunk), chunk)
                if chunk % 128 == 0:
                    start = pl.multiple_of((2 * j + side) * chunk, chunk)
                    put(at, dot_tn(left(pl.ds(start, chunk)), right))
                else:
                    start = pl.multiple_of(2 * j * chunk, 2 * chunk)
                    both[...] = dot_tn(left(pl.ds(start, 2 * chunk)), right)
                    put(at, both[pl.ds(pl.multiple_of(side * chunk, chunk), chunk), :])

        @pl.when(i < inner)
        def _():
            cols = pl.ds(pl.multiple_of(i * width, width), width)
            blocks(lambda at: la_ref[:, at], ra_ref[:, cols])

        @pl.when(i >= inner)
        def _():
            k = i - inner
            cols = pl.ds(pl.multiple_of(k * width, width), width)
            op = (k + per - 1) // per
            blocks(lambda at: lx_ref[op, :, at], rb_ref[:, cols])

    small_cur[...] = small_ref[...]
    small_partners = [at_y] + at_h + [at_p]
    for k, partner in enumerate(small_partners):
        copy = remote(small_cur, small_recv.at[k], sem_s.at[k], partner)
        copy.start()

        if k == 0:

            @pl.loop(0, tiles)
            def _(i):
                def put(at, value):
                    send0[i, at, :] = value.astype(BF)

                product(i, 1 - mine, put)
                copy_y(i).start()

        copy.wait()
        small_cur[...] = small_cur[...] + small_recv[k]
    last = len(small_partners)
    copy = remote(small_cur, small_recv.at[last], sem_s.at[last], at_x)
    copy.start()
    copy.wait()
    small_out_ref[s] = small_cur[...]
    small_out_ref[1 - s] = small_recv[last]

    stages = len(halving)

    def split(i, k, total, rows):
        bit = bit_of(b, halving[k])
        half = rows // 2
        keeps[k][i] = total(pl.multiple_of(bit * half, half), half)
        sends[k][i] = total(pl.multiple_of((1 - bit) * half, half), half).astype(BF)
        copy_h(k, i).start()

    def stage_first(i):
        copy_y(i).wait()

        def put(at, value):
            keep0[at, :] = value + recv0[i, at, :].astype(F32)

        product(i, mine, put)
        split(i, 0, lambda at, n: keep0[pl.ds(at, n), :], half_count * chunk)

    def stage_next(k, i):
        copy_h(k, i).wait()

        def total(at, n):
            return keeps[k][i, pl.ds(at, n), :] + recvs[k][i, pl.ds(at, n), :].astype(F32)

        rows = (half_count * chunk) >> (k + 1)
        if k + 1 < stages:
            split(i, k + 1, total, rows)
        else:
            bit = bit_of(b, PAIR_BIT)
            keep_p[i] = total(pl.multiple_of(bit * chunk, chunk), chunk)
            send_p[i] = total(pl.multiple_of((1 - bit) * chunk, chunk), chunk).astype(BF)
            copy_p(i).start()

    def stage_pair(i):
        copy_p(i).wait()
        bit = bit_of(b, PAIR_BIT)
        half = chunk // 2
        mine_at = pl.multiple_of(s * half, half)
        other_at = pl.multiple_of((1 - s) * half, half)
        out_ref[i, s, bit] = keep_p[i, pl.ds(mine_at, half), :]
        out_ref[i, s, 1 - bit] = recv_p[i, pl.ds(mine_at, half), :].astype(F32)
        send_x[i, bit] = keep_p[i, pl.ds(other_at, half), :].astype(BF)
        send_x[i, 1 - bit] = recv_p[i, pl.ds(other_at, half), :]
        copy_x(i).start()

    def stage_last(i):
        copy_x(i).wait()
        out_ref[i, 1 - s] = recv_x[i].astype(F32)

    @pl.loop(0, tiles + stages + 2)
    def _(i):
        @pl.when(i < tiles)
        def _():
            stage_first(i)

        for k in range(stages):

            @pl.when((i >= k + 1) & (i < tiles + k + 1))
            def _():
                stage_next(k, i - (k + 1))

        @pl.when((i >= stages + 1) & (i < tiles + stages + 1))
        def _():
            stage_pair(i - (stages + 1))

        @pl.when(i >= stages + 2)
        def _():
            stage_last(i - (stages + 2))


def reduce_grads(la, lx, ra, rb, small, width):
    count = lax.axis_size("batch")
    bits = count.bit_length() - 1
    tiles = (ra.shape[1] + rb.shape[1]) // width
    features = la.shape[1]
    chunk = features // count
    rows = features // 2
    halving = bits - 1 - PAIR_BIT
    dma = pltpu.SemaphoreType.DMA
    pieces = [rows >> (k + 1) for k in range(halving)]
    scratch = [
        pltpu.VMEM((tiles, rows, width), BF),
        pltpu.VMEM((tiles, rows, width), BF),
        pltpu.VMEM((rows, width), F32),
        pltpu.VMEM((2 * chunk if chunk % 128 else 8, width), F32),
        [pltpu.VMEM((tiles, n, width), BF) for n in pieces],
        [pltpu.VMEM((tiles, n, width), BF) for n in pieces],
        [pltpu.VMEM((tiles, n, width), F32) for n in pieces],
        pltpu.VMEM((tiles, chunk, width), BF),
        pltpu.VMEM((tiles, chunk, width), BF),
        pltpu.VMEM((tiles, chunk, width), F32),
        pltpu.VMEM((tiles, 2, chunk // 2, width), BF),
        pltpu.VMEM((tiles, 2, chunk // 2, width), BF),
        pltpu.VMEM(small.shape, F32),
        pltpu.VMEM((bits + 1,) + small.shape, F32),
        dma((tiles, 2)),
        [dma((tiles, 2)) for _ in pieces],
        dma((tiles, 2)),
        dma((tiles, 2)),
        dma((bits + 1, 2)),
    ]
    vmem = pl.BlockSpec(memory_space=pltpu.VMEM)
    return pl.pallas_call(
        functools.partial(grads_kernel, bits, tiles, width),
        name="weight_grads",
        out_shape=(
            jax.ShapeDtypeStruct((tiles, 2, 2, chunk // 2, width), F32),
            jax.ShapeDtypeStruct((2,) + small.shape, F32),
        ),
        in_specs=[vmem] * 5,
        out_specs=(vmem, vmem),
        scratch_shapes=scratch,
        compiler_params=pltpu.CompilerParams(
            collective_id=1, has_side_effects=True, vmem_limit_bytes=62 * 2**20
        ),
    )(la, lx, ra, rb, small)


def chain_kernel(
    count_ref,
    vecu_ref,
    hid_hbm,
    dhid_hbm,
    emb_hbm,
    dsum_hbm,
    vec_hbm,
    wq_hbm,
    wk_hbm,
    wv_hbm,
    wo_hbm,
    wu_hbm,
    wd_hbm,
    hid_out,
    sum_out,
    gin_out,
    small_out,
    la_hbm,
    lx_hbm,
    ra_hbm,
    rb_hbm,
    wqkv,
    wo,
    wu,
    wd,
    rows,
    act1,
    qkv,
    probs,
    mix,
    mid,
    act2,
    actv,
    db,
    slope0,
    gd,
    gm,
    dmix,
    dqkv,
    dsum,
    vec,
    bias,
    stat,
    outacc,
    fsum,
    gsum,
    gx_send,
    gx_recv,
    ar_send,
    ar_core,
    ar_x,
    ar_full,
    ar_own,
    wsem,
    lsem,
    rsem,
):
    b, s, t = lax.axis_index("batch"), lax.axis_index("seq"), lax.axis_index("tensor")
    at_core = (b, s, 1 - t)
    at_x = (b, 1 - s, t)
    at_p = (flip(b, PAIR_BIT), s, t)
    zl = bit_of(b, PAIR_BIT)
    barrier = pltpu.get_barrier_semaphore()
    for partner in (at_core, at_x, at_p):
        pl.semaphore_signal(barrier, inc=1, device_id=partner, device_id_type=MESH)

    toks = hid_hbm.shape[1]
    slots = emb_hbm.shape[0]
    feats = rows.shape[1]
    half = feats // 2
    quarter = feats // 4
    span = 2 * toks
    s0, t0, t1, s1, p0 = 0, slots, slots + span, slots + 2 * span, 2 * slots + 2 * span
    own = slots + span
    end = p0 + slots
    nq = wo.shape[0]
    nu = wu.shape[1]
    my_cols = pl.ds(pl.multiple_of(t * half, half), half)
    its_cols = pl.ds(pl.multiple_of((1 - t) * half, half), half)
    my_toks = pl.multiple_of(s * toks, toks)
    its_toks = pl.multiple_of((1 - s) * toks, toks)
    my_quarter = pl.ds(pl.multiple_of(t * half + s * quarter, quarter), quarter)

    counter = {"l": 0, "r": 0}

    def local(src, dst):
        counter["l"] += 1
        copy = pltpu.make_async_copy(src, dst, lsem.at[counter["l"] - 1])
        copy.start()
        return copy

    def remote(src, dst, partner):
        counter["r"] += 1
        at = counter["r"] - 1
        copy = pltpu.make_async_remote_copy(
            src_ref=src,
            dst_ref=dst,
            send_sem=rsem.at[at, 0],
            recv_sem=rsem.at[at, 1],
            device_id=partner,
            device_id_type=MESH,
        )
        copy.start()
        return copy

    part = lambda ref, n, axis: (
        ref.at[:, pl.ds(pl.multiple_of(s * n, n), n)]
        if axis
        else ref.at[pl.ds(pl.multiple_of(s * n, n), n), :]
    )
    weights = []
    for at, (src, dst) in enumerate(
        (
            (part(wq_hbm, nq, 1), wqkv.at[:, pl.ds(0, nq)]),
            (part(wk_hbm, nq, 1), wqkv.at[:, pl.ds(nq, nq)]),
            (part(wv_hbm, nq, 1), wqkv.at[:, pl.ds(2 * nq, nq)]),
            (part(wo_hbm, nq, 0), wo),
            (part(wu_hbm, nu, 1), wu),
            (part(wd_hbm, nu, 0), wd),
        )
    ):
        copy = pltpu.make_async_copy(src, dst, wsem.at[at])
        weights.append(copy)

    firsts = [
        local(emb_hbm, rows.at[pl.ds(s0, slots), my_cols]),
        local(emb_hbm, rows.at[pl.ds(s1, slots), my_cols]),
        local(vec_hbm, vec.at[:, my_cols]),
    ]
    for seg, at in enumerate((t0, t1)):
        firsts.append(local(hid_hbm.at[seg], rows.at[pl.ds(at + my_toks, toks), my_cols]))
    laters = [local(dsum_hbm, dsum.at[:, my_cols])]
    for seg, at in enumerate((t0, t1)):
        laters.append(local(dhid_hbm.at[seg], gd.at[pl.ds(at + my_toks, toks), my_cols]))
    for copy in weights[:3]:
        copy.start()
    pl.semaphore_wait(barrier, 3)

    from_x, from_core, forwards = [], [], []
    for src, dst, at in (
        (hid_hbm.at[0], rows, t0),
        (hid_hbm.at[1], rows, t1),
        (dhid_hbm.at[0], gd, t0),
        (dhid_hbm.at[1], gd, t1),
    ):
        block = dst.at[pl.ds(at + my_toks, toks), my_cols]
        from_x.append((remote(src, block, at_x), dst, at))
    from_core.append(remote(emb_hbm, rows.at[pl.ds(s0, slots), my_cols], at_core))
    from_core.append(remote(emb_hbm, rows.at[pl.ds(s1, slots), my_cols], at_core))
    from_core.append(remote(vec_hbm, vec.at[:, my_cols], at_core))
    for src, dst, at in ((hid_hbm.at[0], rows, t0), (hid_hbm.at[1], rows, t1)):
        from_core.append(remote(src, dst.at[pl.ds(at + my_toks, toks), my_cols], at_core))
    late_core = [remote(dsum_hbm, dsum.at[:, my_cols], at_core)]
    for src, dst, at in ((dhid_hbm.at[0], gd, t0), (dhid_hbm.at[1], gd, t1)):
        late_core.append(remote(src, dst.at[pl.ds(at + my_toks, toks), my_cols], at_core))
    for copy in weights[3:]:
        copy.start()

    live_count = count_ref[0]
    row_live = (lax.broadcasted_iota(jnp.int32, (slots, 1), 0) < live_count).astype(F32)
    dqkv[pl.ds(p0, slots), pl.ds(0, nq)] = jnp.zeros((slots, nq), BF)
    bias[:, pl.ds(0, nq)] = vecu_ref[:, pl.ds(pl.multiple_of(s * nq, nq), nq)]
    bias[:, pl.ds(nq, nq)] = jnp.zeros((1, nq), F32)
    bias[:, pl.ds(2 * nq, nq)] = vecu_ref[:, pl.ds(pl.multiple_of((2 + s) * nq, nq), nq)]
    bias[:, pl.ds(3 * nq, nu)] = vecu_ref[:, pl.ds(pl.multiple_of(4 * nq + s * nu, nq), nu)]
    fsum[...] = jnp.zeros_like(fsum)
    gsum[...] = jnp.zeros_like(gsum)

    step = 16
    inverse = 1.0 / feats

    def row_loop(start, n, body):
        @pl.loop(0, n // step)
        def _(i):
            body(pl.ds(pl.multiple_of(start + i * step, step), step))

    def mean(x):
        return jnp.sum(x, axis=1, keepdims=True) * inverse

    def stats(x):
        m = mean(x)
        return m, lax.rsqrt(mean(x * x) - m * m + EPSILON)

    def norm1(start, n):
        def body(at):
            x = rows[at, :].astype(F32)
            m, r = stats(x)
            act1[at, :] = ((x - m) * r * vec[0:1, :] + vec[1:2, :]).astype(BF)
            stat[at, 0:1] = m
            stat[at, 1:2] = r

        row_loop(start, n, body)

    def norm_back(d, xhat, r, gain):
        q = d * gain
        return r * (q - mean(q) - xhat * mean(q * xhat))

    def fold(x):
        return jnp.sum(x.reshape(step // 8, 8, x.shape[1]), axis=0)

    wide = 512

    def col_loop(n, body):
        @pl.loop(0, n // wide)
        def _(j):
            body(pl.multiple_of(j * wide, wide))

    def project(at, n, lo, hi):
        def body(c):
            cols = pl.ds(pl.multiple_of(lo + c, wide), wide)
            x = jnp.dot(act1[pl.ds(at, n), :], wqkv[:, cols], preferred_element_type=F32)
            qkv[pl.ds(at, n), cols] = (x + bias[:, cols]).astype(BF)

        col_loop(hi - lo, body)

    class Total:
        def __init__(self, n, at, full, pieces, own_at=0):
            self.n, self.at, self.full, self.own_at = n, at, full, own_at
            self.pieces = pieces

        def mine(self, r, n):
            if self.full is None:
                return ar_own.at[pl.ds(self.own_at + r, n), :]
            return ar_full.at[pl.ds(self.full + r, n), my_cols]

        def start(self, product):
            at = pl.ds(self.at, self.n)

            def other(c):
                x = product(pl.multiple_of((1 - t) * half + c, wide), wide)
                ar_send[at, pl.ds(c, wide)] = x.astype(BF)

            col_loop(half, other)
            self.core = remote(ar_send.at[at, :], ar_core.at[at, :], at_core)

            def this(c):
                x = product(pl.multiple_of(t * half + c, wide), wide)
                if self.full is None:
                    ar_own[pl.ds(self.own_at, self.n), pl.ds(c, wide)] = x.astype(BF)
                else:
                    cols = pl.ds(pl.multiple_of(t * half + c, wide), wide)
                    ar_full[pl.ds(self.full, self.n), cols] = x.astype(BF)

            col_loop(half, this)

        def middle(self):
            self.core.wait()
            self.xs = []
            for base, n, scatter in self.pieces:
                at = pl.ds(self.at + base, n)
                ar_core[at, :] = (
                    self.mine(base, n)[...].astype(F32) + ar_core[at, :].astype(F32)
                ).astype(BF)
                if scatter:
                    src = ar_core.at[pl.ds(self.at + base + its_toks, toks), :]
                    dst = ar_x.at[pl.ds(self.at + base, toks), :]
                else:
                    src, dst = ar_core.at[at, :], ar_x.at[at, :]
                self.xs.append(remote(src, dst, at_x))

        def sums(self, base, n, scatter):
            if scatter:
                near = ar_core[pl.ds(self.at + base + my_toks, toks), :]
                far = ar_x[pl.ds(self.at + base, toks), :]
            else:
                near = ar_core[pl.ds(self.at + base, n), :]
                far = ar_x[pl.ds(self.at + base, n), :]
            return near.astype(F32) + far.astype(F32)

        def finish(self):
            self.backs = []
            for (base, n, scatter), copy in zip(self.pieces, self.xs):
                copy.wait()
                n = toks if scatter else n
                block = ar_full.at[pl.ds(self.full + base, n), my_cols]
                block[...] = self.sums(base, n, scatter).astype(BF)
                self.backs.append(remote(block, block, at_core))

        def done(self):
            for copy in self.backs:
                copy.wait()

    whole = lambda n: [(i, 64, False) for i in range(0, n, 64)]

    def out_product(at, n):
        return lambda c, w: jnp.dot(
            mix[pl.ds(at, n), :], wo[:, pl.ds(c, w)], preferred_element_type=F32
        )

    def down_product(at, n):
        return lambda c, w: jnp.dot(
            actv[pl.ds(at, n), :], wd[:, pl.ds(c, w)], preferred_element_type=F32
        )

    def up_back(at, n):
        return lambda c, w: dot_nt(db[pl.ds(at, n), :], wu[pl.ds(c, w), :])

    def in_back(at, n, lo):
        return lambda c, w: dot_nt(
            dqkv[pl.ds(at, n), pl.ds(lo, 3 * nq - lo)], wqkv[pl.ds(c, w), pl.ds(lo, 3 * nq - lo)]
        )

    def enter_ffn(total, at, n):
        def body(i):
            r = pl.ds(pl.multiple_of(at + i * step, step), step)
            f = pl.ds(pl.multiple_of(total.full + i * step, step), step)
            x = rows[r, :].astype(F32) + ar_full[f, :].astype(F32) + vec[4:5, :]
            m, rs = stats(x)
            mid[r, :] = x
            act2[r, :] = ((x - m) * rs * vec[2:3, :] + vec[3:4, :]).astype(BF)
            stat[r, 2:3] = m
            stat[r, 3:4] = rs

        pl.loop(0, n // step)(body)

    def gelu(v):
        c = 0.7978845608028654
        th = jnp.tanh(c * (v + 0.044715 * (v * v * v)))
        act = 0.5 * v * (1.0 + th)
        sl = 0.5 * (1.0 + th) + (0.5 * c) * v * (1.0 - th * th) * (1.0 + (3 * 0.044715) * v * v)
        return act, sl

    def ffn(at, n, back):
        r = pl.ds(at, n)

        def body(c):
            cols = pl.ds(c, wide)
            v = jnp.dot(act2[r, :], wu[:, cols], preferred_element_type=F32)
            act, sl = gelu(v + bias[:, pl.ds(pl.multiple_of(3 * nq + c, wide), wide)])
            actv[r, cols] = act.astype(BF)
            if back:
                db[r, cols] = (sl * dot_nt(gd[r, :], wd[cols, :])).astype(BF)
            else:
                slope0[:, cols] = sl

        col_loop(nu, body)

    def leave_ffn(total, at, n):
        def body(i):
            r = pl.ds(pl.multiple_of(at + i * step, step), step)
            f = pl.ds(pl.multiple_of(total.full + i * step, step), step)
            d = ar_full[f, :].astype(F32)
            xhat = (mid[r, :] - stat[r, 2:3]) * stat[r, 3:4]
            fsum[pl.ds(0, 8), :] = fsum[pl.ds(0, 8), :] + fold(d * xhat)
            fsum[pl.ds(8, 8), :] = fsum[pl.ds(8, 8), :] + fold(d)
            dm = gd[r, :].astype(F32) + norm_back(d, xhat, stat[r, 3:4], vec[2:3, :])
            mid[r, :] = dm
            gm[r, :] = dm.astype(BF)

        pl.loop(0, n // step)(body)

    def mix_back(at, n):
        dmix[pl.ds(at, n), :] = dot_nt(gm[pl.ds(at, n), :], wo[...]).astype(BF)

    pairs = nq // (2 * HD)
    scale = HD**-0.5

    def seen(seg, keys):
        q = lax.broadcasted_iota(jnp.int32, (own, keys), 0)
        k = lax.broadcasted_iota(jnp.int32, (own, keys), 1)
        if seg == 0:
            q = jnp.where(q < slots, q + span, q - slots)
            slot = k
            token = k >= slots
            k = jnp.where(token, k - slots, k + span)
            return (k <= q) & (token | (slot < live_count))
        token = k < span
        ahead = k >= own
        slot = jnp.where(ahead, k - own, k - span)
        return (ahead | (k <= q)) & (token | (slot < live_count))

    def lanes(n):
        first = (lax.broadcasted_iota(jnp.int32, (n, 2 * HD), 1) < HD).astype(F32)
        return first.astype(BF), (1.0 - first).astype(BF)

    def attend(seg):
        at, keys = (s0, own) if seg == 0 else (t1, own + slots)
        q_rows, k_rows = pl.ds(at, own), pl.ds(at, keys)

        @pl.loop(0, pairs)
        def _(j):
            col = lambda g: pl.ds(pl.multiple_of(g * nq + j * 2 * HD, 2 * HD), 2 * HD)
            q, k, v = qkv[q_rows, col(0)], qkv[k_rows, col(1)], qkv[k_rows, col(2)]
            first = lanes(keys)
            allowed = seen(seg, keys)
            got = jnp.zeros((own, 2 * HD), F32)
            for h in range(2):
                pick = first[h]
                sc = dot_nt(q, k * pick) * scale
                sc = jnp.where(allowed, sc, NEGATIVE)
                e = jnp.exp(sc - jnp.max(sc, axis=1, keepdims=True))
                p = (e / jnp.sum(e, axis=1, keepdims=True)).astype(BF)
                probs[seg, 2 * j + h, :, pl.ds(0, keys)] = p
                got += jnp.dot(p, v * pick, preferred_element_type=F32)
            mix[q_rows, pl.ds(pl.multiple_of(j * 2 * HD, 2 * HD), 2 * HD)] = got.astype(BF)

    def attend_back(seg):
        at, keys = (s0, own) if seg == 0 else (t1, own + slots)
        q_rows, k_rows = pl.ds(at, own), pl.ds(at, keys)

        @pl.loop(0, pairs)
        def _(j):
            col = lambda g: pl.ds(pl.multiple_of(g * nq + j * 2 * HD, 2 * HD), 2 * HD)
            q, k, v = qkv[q_rows, col(0)], qkv[k_rows, col(1)], qkv[k_rows, col(2)]
            d = dmix[q_rows, pl.ds(pl.multiple_of(j * 2 * HD, 2 * HD), 2 * HD)]
            first_k, first_q = lanes(keys), lanes(own)
            dq = jnp.zeros((own, 2 * HD), F32)
            dk = jnp.zeros((keys, 2 * HD), F32)
            dv = jnp.zeros((keys, 2 * HD), F32)
            for h in range(2):
                pick_k, pick_q = first_k[h], first_q[h]
                p = probs[seg, 2 * j + h, :, pl.ds(0, keys)]
                pf = p.astype(F32)
                dp = dot_nt(d, v * pick_k)
                ds = (pf * (dp - jnp.sum(pf * dp, axis=1, keepdims=True))).astype(BF)
                dq += jnp.dot(ds, k * pick_k, preferred_element_type=F32)
                dk += dot_tn(ds, q * pick_q)
                dv += dot_tn(p, d * pick_q)
            dqkv[q_rows, col(0)] = (dq * scale).astype(BF)
            dqkv[k_rows, col(1)] = (dk * scale).astype(BF)
            dqkv[k_rows, col(2)] = dv.astype(BF)

    stays, gifts, passed = [], [], []

    def share_feats(src, dst, at, n):
        stays.append(local(src.at[pl.ds(at, n), :], dst.at[0, pl.ds(at, n), :]))
        landing = dst.at[1, pl.ds(at, n), my_cols]
        gifts.append((remote(src.at[pl.ds(at, n), my_cols], landing, at_p), landing))

    def pass_on():
        while gifts:
            copy, landing = gifts.pop(0)
            copy.wait()
            if landing is not None:
                passed.append(remote(landing, landing, at_core))

    def share_units(src, col, n, dst, dst_col, at, rn):
        mine = pl.ds(pl.multiple_of(col + zl * n, n), n)
        its = pl.ds(pl.multiple_of(col + (1 - zl) * n, n), n)
        to = pl.ds(dst_col, n)
        stays.append(local(src.at[pl.ds(at, rn), mine], dst.at[0, pl.ds(at, rn), to]))
        gifts.append((remote(src.at[pl.ds(at, rn), its], dst.at[1, pl.ds(at, rn), to], at_p), None))

    hq, hu = nq // 2, nu // 2

    def share_qkv(at, n):
        for g in range(3):
            share_units(dqkv, g * nq, hq, ra_hbm, g * hq, at, n)

    share_mix = lambda at, n: share_units(mix, 0, hq, rb_hbm, 0, at, n)
    share_db = lambda at, n: share_units(db, 0, hu, rb_hbm, hq, at, n)
    share_actv = lambda at, n: share_units(actv, 0, hu, rb_hbm, hq + hu, at, n)

    for copy in firsts:
        copy.wait()
    for copy in from_core:
        copy.wait()
    for copy, dst, at in from_x[:2]:
        copy.wait()
        block = dst.at[pl.ds(at + its_toks, toks), my_cols]
        forwards.append(remote(block, block, at_core))
    for copy in forwards:
        copy.wait()
    norm1(0, p0)
    share_feats(act1, la_hbm, 0, p0)
    for copy in weights[:3]:
        copy.wait()
    project(0, p0, 0, 3 * nq)
    forwards = []
    for copy, dst, at in from_x[2:]:
        copy.wait()
        block = dst.at[pl.ds(at + its_toks, toks), my_cols]
        forwards.append(remote(block, block, at_core))
    attend(0)
    share_mix(0, own)
    for copy in weights[3:4]:
        copy.wait()
    T = span
    a1 = Total(slots, 0, 0, whole(slots))
    a2 = Total(T, 2 * slots, 2 * slots, whole(T))
    a1.start(out_product(s0, slots))
    a2.start(out_product(t0, T))
    a1.middle()
    a2.middle()
    for copy in forwards + laters + late_core:
        copy.wait()
    gd[pl.ds(s1, slots), :] = (dsum[pl.ds(slots, slots), :].astype(F32) * row_live).astype(BF)
    share_feats(gd, lx_hbm.at[2], t0, p0 - t0)
    a1.finish()
    a1.done()
    enter_ffn(a1, s0, slots)
    weights[4].wait()
    ffn(s0, slots, False)
    weights[5].wait()
    a3 = Total(slots, slots, slots, whole(slots))
    a3.start(down_product(s0, slots))
    a2.finish()
    a3.middle()
    a2.done()
    enter_ffn(a2, t0, T)
    outacc[0] = mid[pl.ds(t0 + my_toks, toks), my_cols]
    a3.finish()
    share_feats(act2, lx_hbm.at[1], s0, own)
    a3.done()

    def summary(i):
        r = pl.ds(pl.multiple_of(s0 + i * step, step), step)
        f = pl.ds(pl.multiple_of(a3.full + i * step, step), step)
        p = pl.ds(pl.multiple_of(p0 + i * step, step), step)
        x = mid[r, :] + ar_full[f, :].astype(F32) + vec[5:6, :]
        on = (lax.broadcasted_iota(jnp.int32, (step, 1), 0) + i * step < live_count).astype(F32)
        rows[p, :] = (x * on).astype(BF)

    pl.loop(0, slots // step)(summary)
    sum_out[0] = rows[pl.ds(p0, slots), my_cols]
    norm1(p0, slots)
    share_feats(act1, la_hbm, p0, slots)
    project(p0, slots, nq, 3 * nq)
    attend(1)
    share_mix(t1, own)
    a5 = Total(own, 2 * slots + T, 2 * slots + T, whole(own))
    a5.start(out_product(t1, own))
    ffn(t0, T, True)
    share_actv(s0, own)
    share_db(t0, T)
    a5.middle()
    a6 = Total(T, 2 * slots, 2 * slots, whole(T))
    a6.start(up_back(t0, T))
    a6.middle()
    a5.finish()
    a4 = Total(T, 2 * slots + T + 2 * own, None, [(0, T, True)], 0)
    a4.start(down_product(t0, T))
    a5.done()
    enter_ffn(a5, t1, own)
    outacc[1] = mid[pl.ds(t1 + my_toks, toks), my_cols]
    outacc[2] = mid[pl.ds(s1, slots), my_cols]
    share_feats(act2, lx_hbm.at[1], t1, own)
    ffn(t1, own, True)
    share_actv(t1, own)
    share_db(t1, own)
    a8 = Total(own, 2 * slots + T + own, 2 * slots + T + own, whole(own))
    a8.start(up_back(t1, own))
    a6.finish()
    a4.middle()
    a8.middle()
    a7 = Total(own, 2 * slots + 2 * T + 2 * own, None, [(0, T, True), (T, slots, False)], T)
    a7.start(down_product(t1, own))
    a7.middle()
    a6.done()
    leave_ffn(a6, t0, T)
    mix_back(t0, T)
    share_feats(gm, lx_hbm.at[0], t0, T)
    a8.finish()
    for copy in a4.xs:
        copy.wait()
    hid_out[0] = (outacc[0] + a4.sums(0, T, True) + vec[5:6, my_cols]).astype(BF)
    a8.done()
    leave_ffn(a8, t1, own)
    mix_back(t1, own)
    share_feats(gm, lx_hbm.at[0], t1, own)
    attend_back(1)
    share_qkv(t1, own + slots)
    a9 = Total(slots, 0, 0, whole(slots))
    a9.start(in_back(p0, slots, nq))
    a10 = Total(own, 2 * slots + T, 2 * slots + T, [(0, T, True), (T, slots, False)])
    a9.middle()
    a10.start(in_back(t1, own, 0))
    a9.finish()
    a10.middle()
    for copy in a7.xs:
        copy.wait()
    hid_out[1] = (outacc[1] + a7.sums(0, T, True) + vec[5:6, my_cols]).astype(BF)
    sum_out[1] = (
        (outacc[2] + a7.sums(T, slots, False) + vec[5:6, my_cols]) * row_live
    ).astype(BF)
    a9.done()
    first_only = (s == 0).astype(F32)

    def norm1_back(r, f, weight):
        d = ar_full[f, :].astype(F32)
        xhat = (rows[r, :].astype(F32) - stat[r, 0:1]) * stat[r, 1:2]
        gsum[pl.ds(0, 8), :] = gsum[pl.ds(0, 8), :] + fold(d * xhat) * weight
        gsum[pl.ds(8, 8), :] = gsum[pl.ds(8, 8), :] + fold(d) * weight
        return norm_back(d, xhat, stat[r, 1:2], vec[0:1, :])

    def prefix_back(i):
        r = pl.ds(pl.multiple_of(p0 + i * step, step), step)
        f = pl.ds(pl.multiple_of(a9.full + i * step, step), step)
        g = pl.ds(pl.multiple_of(s0 + i * step, step), step)
        on = (lax.broadcasted_iota(jnp.int32, (step, 1), 0) + i * step < live_count).astype(F32)
        d = norm1_back(r, f, first_only)
        gd[g, :] = ((dsum[pl.ds(pl.multiple_of(i * step, step), step), :].astype(F32) + d) * on).astype(BF)

    pl.loop(0, slots // step)(prefix_back)
    share_feats(gd, lx_hbm.at[2], s0, slots)

    def last_before(c):
        cols = pl.ds(c, wide)
        r = pl.ds(s0, slots)
        db[r, cols] = (slope0[:, cols] * dot_nt(gd[r, :], wd[cols, :])).astype(BF)

    col_loop(nu, last_before)
    share_db(s0, slots)
    a11 = Total(slots, slots, slots, whole(slots))
    a11.start(up_back(s0, slots))
    a10.finish()
    a11.middle()
    a10.done()

    def rows_back(total, seg):
        t_at, s_at = (t0, s0) if seg == 0 else (t1, s1)
        t_in, s_in = (slots, 0) if seg == 0 else (0, span)

        def tokens(i):
            r = pl.ds(pl.multiple_of(t_at + my_toks + i * step, step), step)
            f = pl.ds(pl.multiple_of(total.full + t_in + i * step, step), step)
            x = norm1_back(r, f, 1.0)
            mid[r, :] = mid[r, :] + x

        pl.loop(0, toks // step)(tokens)
        gin_out[seg] = mid[pl.ds(t_at + my_toks, toks), my_cols]

        def summaries(i):
            r = pl.ds(pl.multiple_of(s_at + i * step, step), step)
            f = pl.ds(pl.multiple_of(total.full + s_in + i * step, step), step)
            x = norm1_back(r, f, first_only) + mid[r, :]
            e = pl.ds(pl.multiple_of(i * step, step), step)
            emb_wide[e, :] = x if seg == 1 else emb_wide[e, :] + x

        pl.loop(0, slots // step)(summaries)

    emb_wide = slope0
    rows_back(a10, 1)
    a11.finish()
    a11.done()
    leave_ffn(a11, s0, slots)
    mix_back(s0, slots)
    share_feats(gm, lx_hbm.at[0], s0, slots)
    attend_back(0)
    share_qkv(0, own)
    a12 = Total(own, 2 * slots + T + own, 2 * slots + T + own, [(0, slots, False), (slots, T, True)])
    a12.start(in_back(s0, own, 0))
    a12.middle()
    ones = jnp.ones((8, p0), BF)
    column = lambda ref, cols: jnp.dot(ones, ref[pl.ds(0, p0), cols], preferred_element_type=F32)[0:1, :]
    base = slots
    small_out[base + 2 : base + 3, :] = column(gm, my_quarter)
    small_out[base + 5 : base + 6, :] = column(gd, my_quarter)
    small_out[base + 3 : base + 4, :] = jnp.sum(fsum[pl.ds(0, 8), my_quarter], axis=0, keepdims=True)
    small_out[base + 4 : base + 5, :] = jnp.sum(fsum[pl.ds(8, 8), my_quarter], axis=0, keepdims=True)
    small_out[base + 6 : base + 7, :] = column(dqkv, pl.ds(0, nq))
    small_out[base + 7 : base + 8, :] = column(dqkv, pl.ds(2 * nq, nq)) + jnp.sum(
        dqkv[pl.ds(p0, slots), pl.ds(2 * nq, nq)].astype(F32), axis=0, keepdims=True
    )
    for k in range(nu // quarter):
        small_out[base + 8 + k : base + 9 + k, :] = column(db, pl.ds(k * quarter, quarter))
    small_out[base + 12 : base + 16, :] = jnp.zeros((4, quarter), F32)
    pass_on()
    a12.finish()
    a12.done()
    rows_back(a12, 0)
    small_out[pl.ds(0, slots), :] = emb_wide[:, my_quarter]
    its_quarter = pl.ds(pl.multiple_of(t * half + (1 - s) * quarter, quarter), quarter)
    gx_send[0:1, :] = jnp.sum(gsum[pl.ds(0, 8), its_quarter], axis=0, keepdims=True)
    gx_send[1:2, :] = jnp.sum(gsum[pl.ds(8, 8), its_quarter], axis=0, keepdims=True)
    gx_send[2:8, :] = jnp.zeros((6, quarter), F32)
    copy = remote(gx_send, gx_recv, at_x)
    copy.wait()
    small_out[base : base + 1, :] = gx_recv[0:1, :] + jnp.sum(gsum[pl.ds(0, 8), my_quarter], axis=0, keepdims=True)
    small_out[base + 1 : base + 2, :] = gx_recv[1:2, :] + jnp.sum(gsum[pl.ds(8, 8), my_quarter], axis=0, keepdims=True)
    for copy in stays + passed:
        copy.wait()

def chain(count, vecu, hid, dhid, emb, dsum, vec, wq, wk, wv, wo, wu, wd):
    toks, slots = hid.shape[1], emb.shape[0]
    half = hid.shape[2]
    feats, quarter = 2 * half, half // 2
    nq, nu = wo.shape[0] // 2, wd.shape[0] // 2
    own = 2 * toks + slots
    main, end = 2 * own, 2 * own + slots
    sums = 2 * slots + 2 * toks + 2 * own
    vm = pltpu.VMEM
    sds = jax.ShapeDtypeStruct
    dma = pltpu.SemaphoreType.DMA
    scratch = [
        vm((feats, 3 * nq), BF),
        vm((nq, feats), BF),
        vm((feats, nu), BF),
        vm((nu, feats), BF),
        vm((end, feats), BF),
        vm((end, feats), BF),
        vm((end, 3 * nq), BF),
        vm((2, nq // HD, own, own + slots), BF),
        vm((main, nq), BF),
        vm((main, feats), F32),
        vm((main, feats), BF),
        vm((main, nu), BF),
        vm((main, nu), BF),
        vm((slots, nu), F32),
        vm((main, feats), BF),
        vm((main, feats), BF),
        vm((main, nq), BF),
        vm((end, 3 * nq), BF),
        vm((2 * slots, feats), BF),
        vm((8, feats), F32),
        vm((1, 3 * nq + nu), F32),
        vm((end, 128), F32),
        vm((3, toks, half), F32),
        vm((16, feats), F32),
        vm((16, feats), F32),
        vm((8, quarter), F32),
        vm((8, quarter), F32),
        vm((sums + 2 * toks + own, half), BF),
        vm((sums + 2 * toks + own, half), BF),
        vm((sums + 2 * toks + own, half), BF),
        vm((sums, feats), BF),
        vm((2 * toks + own, half), BF),
        dma((6,)),
        dma((48,)),
        dma((128, 2)),
    ]
    vmem = pl.BlockSpec(memory_space=pltpu.VMEM)
    hbm = pl.BlockSpec(memory_space=pl.ANY)
    smem = pl.BlockSpec(memory_space=pltpu.SMEM)
    return pl.pallas_call(
        chain_kernel,
        name="chain",
        out_shape=(
            sds((2, toks, half), BF),
            sds((2, slots, half), BF),
            sds((2, toks, half), F32),
            sds((slots + 16, quarter), F32),
            sds((2, end, feats), BF),
            sds((3, 2, main, feats), BF),
            sds((2, end, 3 * nq // 2), BF),
            sds((2, main, nq // 2 + nu), BF),
        ),
        in_specs=[smem, vmem] + [hbm] * 11,
        out_specs=(vmem,) * 4 + (hbm,) * 4,
        scratch_shapes=scratch,
        compiler_params=pltpu.CompilerParams(
            collective_id=2, has_side_effects=True, vmem_limit_bytes=62 * 2**20
        ),
    )(count, vecu, hid, dhid, emb, dsum, vec, wq, wk, wv, wo, wu, wd)


def local(
    hidden_in, summary_counts, summary_embed, ln1_gain, ln1_bias, w_query, b_query, w_key, w_value,
    b_value, w_out, b_out, ln2_gain, ln2_bias, w_up, b_up, w_down, b_down, d_hidden, d_summary,
):
    n = summary_embed.shape[0]
    pad = -n % 64
    emb = jnp.pad(summary_embed, ((0, pad), (0, 0)))
    dsum = jnp.pad(d_summary[0], ((0, 0), (0, pad), (0, 0))).reshape(-1, d_summary.shape[3])
    zero = jnp.zeros_like(ln1_gain)
    vec = jnp.stack([ln1_gain, ln1_bias, ln2_gain, ln2_bias, b_out, b_down, zero, zero]).astype(F32)
    vecu = jnp.concatenate([b_query, b_value, b_up]).astype(F32)[None]
    nq, nu = w_query.shape[1] // 2, w_up.shape[1] // 2
    hid, summaries, gin, small, la, lx, ra, rb = chain(
        summary_counts, vecu, hidden_in[0], d_hidden[0], emb, dsum, vec,
        w_query, w_key, w_value, w_out, w_up, w_down,
    )
    flat = lambda x: x.reshape(x.shape[:-3] + (-1, x.shape[-1]))
    width = nq // 2
    w, sm = reduce_grads(flat(la), flat(lx), flat(ra), flat(rb), small, width)

    def place(lo, hi):
        x = w[lo:hi]
        return x.transpose(3, 1, 2, 0, 4).reshape(x.shape[3], -1)

    per = nu // 2 // width
    gq, gk, gv, go = (place(i, i + 1) for i in range(4))
    gu, gdn = place(4, 4 + per), place(4 + per, 4 + 2 * per)
    sm = sm.transpose(1, 0, 2)
    at = n + pad
    fl = lambda r: sm[at + r].reshape(-1)
    bup = sm[at + 8 : at + 8 + nu // sm.shape[2]].transpose(1, 0, 2).reshape(-1)
    return (
        hid[None], summaries[None, :, :n], gin[None],
        sm[:n].reshape(n, -1), fl(0), fl(1), gq, fl(6), gk, gv, fl(7), go.T, fl(2),
        fl(3), fl(4), gu, bup, gdn.T, fl(5),
    )


def solution(mesh):
    return jax.shard_map(
        local,
        mesh=mesh,
        in_specs=(
            P("batch", None, "seq", "tensor"),
            P("batch"),
            P(None, "tensor"),
            P("tensor"),
            P("tensor"),
            P(None, "tensor"),
            P("tensor"),
            P(None, "tensor"),
            P(None, "tensor"),
            P("tensor"),
            P("tensor", None),
            P("tensor"),
            P("tensor"),
            P("tensor"),
            P(None, "tensor"),
            P("tensor"),
            P("tensor", None),
            P("tensor"),
            P("batch", None, "seq", "tensor"),
            P("batch", None, None, "tensor"),
        ),
        out_specs=(
            P("batch", None, "seq", "tensor"),
            P("batch", None, None, "tensor"),
            P("batch", None, "seq", "tensor"),
            P(None, "tensor"),
            P("tensor"),
            P("tensor"),
            P(("batch", "seq"), "tensor"),
            P("tensor"),
            P(("batch", "seq"), "tensor"),
            P(("batch", "seq"), "tensor"),
            P("tensor"),
            P("tensor", ("batch", "seq")),
            P("tensor"),
            P("tensor"),
            P("tensor"),
            P(("batch", "seq"), "tensor"),
            P("tensor"),
            P("tensor", ("batch", "seq")),
            P("tensor"),
        ),
        check_vma=False,
    )
```

time: 898 us -> 388 us (0.43)
  waiting for transfers between devices: 352 us -> 0 us
  Pallas kernels: 187 us -> 348 us
  matrix products: 100 us -> 0 us
  local copies, waits for them, and re-layouts: 118 us -> 36.9 us
  other arithmetic: 76.2 us -> 1.26 us
  blocking collectives: 35.3 us -> 0 us
  between operations: 16.4 us -> 1.4 us
    psum x7 -> x0, waiting for transfers between devices: 205 us -> none  [total4(): return lax.psum(x, ('seq', 'tensor'))]
    pallas_call x1 -> x2, Pallas kernels: 187 us -> 348 us  [the longest x1 196 us: reduce_grads(): pl.pallas_call(functools.partial(grads_kernel, bits, tiles, width), name=...]
    ppermute x2 -> x0, waiting for transfers between devices: 147 us -> none  [the longest x1 147 us: local(): take = lax.ppermute(give, 'batch', pair)]
    dot_general x34 -> x0, matrix products: 95.1 us -> none  [the longest x12 39.6 us: dot_nn(): return jnp.dot(a, b, preferred_element_type=F32)]
    all_gather x10 -> x0, blocking collectives: 35.3 us -> none  [the longest x2 20.5 us: local(): tokens = lambda x: full(lax.all_gather(x[0], 'seq', axis=1, tiled=True))]
    unnamed x291 -> x16, local copies, waits for them, and re-layouts: 38 us -> 10.4 us
    reduce_sum x12 -> x0, other arithmetic: 21.9 us -> none  [the longest x8 17.8 us: local(): jnp.sum(a, axis=0, keepdims=True)]
    transpose x1 -> x0, local copies, waits for them, and re-layouts: 20.8 us -> none  [local(): lhs = jnp.concatenate([lhs, lhs_take], 1).transpose(0, 2, 1)]
  transfers between devices with their start and end apart: 11 -> 0, of which waited for: 8 -> 0; matrix products, arithmetic and copies ran while one was open for 11% -> 0% of each run, Pallas kernels for 0% -> 0%
where the time goes in v2:
time: 388 us; the launch traced here: 387 us
  Pallas kernels  348 us (90%)
  local copies, waits for them, and re-layouts  36.9 us (10%)
    pallas_call x1, Pallas kernels, reduce_grads(): pl.pallas_call(functools.partial(grads_kernel, bits, tiles, width), name=...  196 us
    pallas_call x1, Pallas kernels, chain(): pl.pallas_call(chain_kernel, name='chain', out_shape=(sds((2, toks, half)...  152 us
    transpose x8, local copies, waits for them, and re-layouts, place(): return x.transpose(3, 1, 2, 0, 4).reshape(x.shape[3], -1)  14 us
    unnamed x16, local copies, waits for them, and re-layouts  10.4 us

profile of v2, /device:TPU:0, one launch (start us, length us, event | category | flops | bytes accessed | tf_op | source)
XLA Modules:
  0.0 387.1 jit_solution(16013336793837801142)
XLA Ops:
  7.5 0.7 concatenate.18
  8.8 1.6 pad.8.emb_hbm
  10.4 1.0 copy.54
  11.4 0.7 pad.9.clone
  12.1 151.5 %chain.1 = (bf16[2,64,1024]{2,1,0:T(8,128)(2,1)}, bf16[2,64,1024]{2,1,0:T(8,128)(2,1)}, f32[2,64,1024]{2,1,0:T(8,128)}, f32[80,512]{1,0:T(8,128)}, bf16[2,448,20...) custom-call(s32[1]{0:T(128)S(6)} %copy.59.count_ref, ...), custom_call_target="tpu_custom_call" | custom-call | tf_op jit(solution)/shard_map/chain/pallas_call | solution.py:1002
  163.6 1.0 slice_bitcast_fusion.6
  164.6 0.9 copy.49
  165.5 196.0 %weight_grads.1 = (f32[12,2,2,128,256]{4,3,2,1,0:T(8,128)}, f32[2,80,512]{2,1,0:T(8,128)}) custom-call(bf16[896,2048]{1,0:T(8,128)(2,1)} %bitcast.52, bf16[3,768,2048]{2,1,0:T(8,128)(2,1)} %bitcast.50, bf16[896,768]{1,0:T(8,128)(2,1)} %bitcast.58, bf16[768,2304]{1,0:T(8,128)(2,1)} %bitcast.53, f32[80,512]{1,0:T(8,128)} %get-tuple-element.36.small_ref), custom_call_target="tpu_custom_call" | custom-call | tf_op jit(solution)/shard_map/weight_grads/pallas_call | solution.py:261
  361.5 0.8 slice_bitcast_fusion.7
  362.9 1.9 fusion
  364.7 1.0 slice.68
  366.0 0.7 copy.55
  366.7 2.7 slice_bitcast_fusion.2
  369.4 3.9 %slice_bitcast_fusion = (f32[128,2,2,4,256]{4,0,2,1,3:T(8,128)S(1)}, f32[128,2,2,4,256]{4,0,2,1,3:T(8,128)}) fusion(f32[12,2,2,128,256]{4,3,2,1,0:T(8,128)} %get-tuple-element.38), kind=kLoop, calls=%fused_computation | loop fusion | bytes 8388608 | tf_op jit(solution)/shard_map/transpose | solution.py:1046
  373.3 1.8 copy.48
  375.1 2.0 copy.46
  377.1 1.2 copy.45
  378.4 1.0 copy.52
  379.6 1.0 copy.51
  380.8 1.0 copy.50
  381.8 2.0 copy.47
  383.8 1.8 copy.53
  385.6 0.7 copy.60
  386.3 0.8 copy.61
  (21 shorter events, 8.0 us)
Async XLA Ops:
  381.8 3.8 copy-start.1
  381.8 4.5 %copy-start = (f32[2,64,1024]{2,1,0:T(8,128)S(1)}, f32[2,64,1024]{2,1,0:T(8,128)}, u32[]{:S(2)}) copy-start(f32[2,64,1024]{2,1,0:T(8,128)} %get-tuple-element.31) | copy-start | bytes 1572868

commit v3 on v2

--- a/solution.py
+++ b/solution.py
@@ -23,6 +23,14 @@
 
 def bit_of(index, bit):
     return lax.rem(index // (1 << bit), 2)
+
+
+def dot_nt(a, b):
+    return lax.dot_general(a, b, (((1,), (1,)), ((), ())), preferred_element_type=F32)
+
+
+def dot_tn(a, b):
+    return lax.dot_general(a, b, (((0,), (0,)), ((), ())), preferred_element_type=F32)
 
 
 def dot_nt(a, b):
@@ -42,8 +50,15 @@
     ra_ref,
     rb_ref,
     small_ref,
-    out_ref,
-    small_out_ref,
+    gq_ref,
+    gk_ref,
+    gv_ref,
+    go_ref,
+    gu_ref,
+    gd_ref,
+    emb_ref,
+    vec_refs,
+    bup_ref,
     send0,
     recv0,
     keep0,
@@ -153,8 +168,18 @@
     copy = remote(small_cur, small_recv.at[last], sem_s.at[last], at_x)
     copy.start()
     copy.wait()
-    small_out_ref[s] = small_cur[...]
-    small_out_ref[1 - s] = small_recv[last]
+    used = emb_ref.shape[0]
+    quarter = small_ref.shape[1]
+    base = small_ref.shape[0] - 16
+    for side, ref in ((s, small_cur), (1 - s, small_recv.at[last])):
+        at = pl.ds(pl.multiple_of(side * quarter, quarter), quarter)
+        emb_ref[:, at] = ref[pl.ds(0, used), :]
+        for k, out in enumerate(vec_refs):
+            out[:, at] = ref[base + k : base + k + 1, :]
+        pieces = bup_ref.shape[1] // (2 * quarter)
+        for k in range(pieces):
+            at = pl.ds(pl.multiple_of((side * pieces + k) * quarter, quarter), quarter)
+            bup_ref[:, at] = ref[base + 8 + k : base + 9 + k, :]
 
     stages = len(halving)
 
@@ -189,21 +214,45 @@
             send_p[i] = total(pl.multiple_of((1 - bit) * chunk, chunk), chunk).astype(BF)
             copy_p(i).start()
 
+    def write(i, side, pair, value):
+        spot = pl.ds(pl.multiple_of((2 * side + pair) * width, width), width)
+        for k, ref in enumerate((gq_ref, gk_ref, gv_ref)):
+
+            @pl.when(i == k)
+            def _():
+                ref[:, spot] = value
+
+        @pl.when(i == inner)
+        def _():
+            go_ref[spot, :] = value.T
+
+        def unit(k):
+            return pl.ds(pl.multiple_of(((2 * side + pair) * per + k) * width, width), width)
+
+        @pl.when((i > inner) & (i <= inner + per))
+        def _():
+            gu_ref[:, unit(i - inner - 1)] = value
+
+        @pl.when(i > inner + per)
+        def _():
+            gd_ref[unit(i - inner - 1 - per), :] = value.T
+
     def stage_pair(i):
         copy_p(i).wait()
         bit = bit_of(b, PAIR_BIT)
         half = chunk // 2
         mine_at = pl.multiple_of(s * half, half)
         other_at = pl.multiple_of((1 - s) * half, half)
-        out_ref[i, s, bit] = keep_p[i, pl.ds(mine_at, half), :]
-        out_ref[i, s, 1 - bit] = recv_p[i, pl.ds(mine_at, half), :].astype(F32)
+        write(i, s, bit, keep_p[i, pl.ds(mine_at, half), :])
+        write(i, s, 1 - bit, recv_p[i, pl.ds(mine_at, half), :].astype(F32))
         send_x[i, bit] = keep_p[i, pl.ds(other_at, half), :].astype(BF)
         send_x[i, 1 - bit] = recv_p[i, pl.ds(other_at, half), :]
         copy_x(i).start()
 
     def stage_last(i):
         copy_x(i).wait()
-        out_ref[i, 1 - s] = recv_x[i].astype(F32)
+        for pair in range(2):
+            write(i, 1 - s, pair, recv_x[i, pair].astype(F32))
 
     @pl.loop(0, tiles + stages + 2)
     def _(i):
@@ -226,62 +275,53 @@
             stage_last(i - (stages + 2))
 
 
-def reduce_grads(la, lx, ra, rb, small, width):
-    count = lax.axis_size("batch")
-    bits = count.bit_length() - 1
-    tiles = (ra.shape[1] + rb.shape[1]) // width
-    features = la.shape[1]
-    chunk = features // count
-    rows = features // 2
-    halving = bits - 1 - PAIR_BIT
-    dma = pltpu.SemaphoreType.DMA
-    pieces = [rows >> (k + 1) for k in range(halving)]
-    scratch = [
-        pltpu.VMEM((tiles, rows, width), BF),
-        pltpu.VMEM((tiles, rows, width), BF),
-        pltpu.VMEM((rows, width), F32),
-        pltpu.VMEM((2 * chunk if chunk % 128 else 8, width), F32),
-        [pltpu.VMEM((tiles, n, width), BF) for n in pieces],
-        [pltpu.VMEM((tiles, n, width), BF) for n in pieces],
-        [pltpu.VMEM((tiles, n, width), F32) for n in pieces],
-        pltpu.VMEM((tiles, chunk, width), BF),
-        pltpu.VMEM((tiles, chunk, width), BF),
-        pltpu.VMEM((tiles, chunk, width), F32),
-        pltpu.VMEM((tiles, 2, chunk // 2, width), BF),
-        pltpu.VMEM((tiles, 2, chunk // 2, width), BF),
-        pltpu.VMEM(small.shape, F32),
-        pltpu.VMEM((bits + 1,) + small.shape, F32),
-        dma((tiles, 2)),
-        [dma((tiles, 2)) for _ in pieces],
-        dma((tiles, 2)),
-        dma((tiles, 2)),
-        dma((bits + 1, 2)),
-    ]
-    vmem = pl.BlockSpec(memory_space=pltpu.VMEM)
-    return pl.pallas_call(
-        functools.partial(grads_kernel, bits, tiles, width),
-        name="weight_grads",
-        out_shape=(
-            jax.ShapeDtypeStruct((tiles, 2, 2, chunk // 2, width), F32),
-            jax.ShapeDtypeStruct((2,) + small.shape, F32),
-        ),
-        in_specs=[vmem] * 5,
-        out_specs=(vmem, vmem),
-        scratch_shapes=scratch,
-        compiler_params=pltpu.CompilerParams(
-            collective_id=1, has_side_effects=True, vmem_limit_bytes=62 * 2**20
-        ),
-    )(la, lx, ra, rb, small)
+class Strips:
+    def __init__(self, refs, width):
+        self.width = width
+        self.free = [[ref, ref.shape[0], at, 0] for ref in refs for at in range(ref.shape[1] // width)]
+
+    def take(self, tiles, n, unit):
+        for k, (ref, height, at, used) in enumerate(self.free):
+            if height < n:
+                continue
+            if used + tiles * n <= height:
+                self.free[k][3] += tiles * n
+                return Slab(ref, at, used, tiles, n, unit, self.width)
+            per = height // n
+            need = -(-tiles // per)
+            run = self.free[k : k + need]
+            if len(run) == need and all(r[0] is ref and r[3] == 0 for r in run):
+                for r in run:
+                    r[3] = height
+                return Slab(ref, at, 0, per, n, unit, self.width)
+        raise ValueError("no room")
+
+
+class Slab:
+    def __init__(self, ref, strip, start, per, n, unit, width):
+        self.ref, self.strip, self.start, self.per = ref, strip, start, per
+        self.n, self.unit, self.width = n, unit, width
+
+    def at(self, i, lo, n):
+        first = pl.multiple_of(self.start + (i % self.per) * self.n + lo, self.unit)
+        col = pl.multiple_of((self.strip + i // self.per) * self.width, self.width)
+        return self.ref.at[pl.ds(first, n), pl.ds(col, self.width)]
+
+    def __call__(self, i):
+        return self.at(i, 0, self.n)
 
 
 def chain_kernel(
+    bits,
     count_ref,
-    vecu_ref,
+    emb_ref,
+    dsum_ref,
+    feat_refs,
+    bq_ref,
+    bv_ref,
+    bu_ref,
     hid_hbm,
     dhid_hbm,
-    emb_hbm,
-    dsum_hbm,
-    vec_hbm,
     wq_hbm,
     wk_hbm,
     wv_hbm,
@@ -291,11 +331,12 @@
     hid_out,
     sum_out,
     gin_out,
-    small_out,
+    small_final,
+    w_hbm,
     la_hbm,
-    lx_hbm,
+    lm_hbm,
     ra_hbm,
-    rb_hbm,
+    mx_hbm,
     wqkv,
     wo,
     wu,
@@ -328,21 +369,42 @@
     ar_x,
     ar_full,
     ar_own,
+    lxx,
+    rbx,
+    both,
+    small_out,
+    small_recv,
     wsem,
     lsem,
     rsem,
+    free,
+    sem_y,
+    sem_za,
+    sem_pa,
+    sem_xa,
+    sem_pb,
+    sem_zb,
+    sem_xb,
+    sem_oa,
+    sem_ob,
+    sem_s,
 ):
     b, s, t = lax.axis_index("batch"), lax.axis_index("seq"), lax.axis_index("tensor")
     at_core = (b, s, 1 - t)
     at_x = (b, 1 - s, t)
     at_p = (flip(b, PAIR_BIT), s, t)
-    zl = bit_of(b, PAIR_BIT)
+    at_y = (flip(b, 0), s, t)
+    halving = list(range(bits - 1, PAIR_BIT, -1))
+    at_h = [(flip(b, bit), s, t) for bit in halving]
+    zl, y = bit_of(b, PAIR_BIT), bit_of(b, 0)
     barrier = pltpu.get_barrier_semaphore()
-    for partner in (at_core, at_x, at_p):
+    partners = [at_core, at_x, at_p, at_y] + at_h
+    for partner in partners:
         pl.semaphore_signal(barrier, inc=1, device_id=partner, device_id_type=MESH)
 
     toks = hid_hbm.shape[1]
-    slots = emb_hbm.shape[0]
+    slots = slope0.shape[0]
+    used = emb_ref.shape[0]
     feats = rows.shape[1]
     half = feats // 2
     quarter = feats // 4
@@ -399,19 +461,23 @@
         copy = pltpu.make_async_copy(src, dst, wsem.at[at])
         weights.append(copy)
 
-    firsts = [
-        local(emb_hbm, rows.at[pl.ds(s0, slots), my_cols]),
-        local(emb_hbm, rows.at[pl.ds(s1, slots), my_cols]),
-        local(vec_hbm, vec.at[:, my_cols]),
-    ]
+    firsts = []
     for seg, at in enumerate((t0, t1)):
         firsts.append(local(hid_hbm.at[seg], rows.at[pl.ds(at + my_toks, toks), my_cols]))
-    laters = [local(dsum_hbm, dsum.at[:, my_cols])]
+    laters = []
     for seg, at in enumerate((t0, t1)):
         laters.append(local(dhid_hbm.at[seg], gd.at[pl.ds(at + my_toks, toks), my_cols]))
     for copy in weights[:3]:
         copy.start()
-    pl.semaphore_wait(barrier, 3)
+    for at in (s0, s1):
+        rows[pl.ds(at, slots), my_cols] = jnp.zeros((slots, half), BF)
+        rows[pl.ds(at, used), my_cols] = emb_ref[...]
+    for seg in range(2):
+        dsum[pl.ds(seg * slots, slots), my_cols] = jnp.zeros((slots, half), BF)
+        dsum[pl.ds(seg * slots, used), my_cols] = dsum_ref[0, seg]
+    for k, ref in enumerate(feat_refs):
+        vec[k : k + 1, my_cols] = ref[...].astype(F32)[None]
+    pl.semaphore_wait(barrier, len(partners))
 
     from_x, from_core, forwards = [], [], []
     for src, dst, at in (
@@ -422,12 +488,15 @@
     ):
         block = dst.at[pl.ds(at + my_toks, toks), my_cols]
         from_x.append((remote(src, block, at_x), dst, at))
-    from_core.append(remote(emb_hbm, rows.at[pl.ds(s0, slots), my_cols], at_core))
-    from_core.append(remote(emb_hbm, rows.at[pl.ds(s1, slots), my_cols], at_core))
-    from_core.append(remote(vec_hbm, vec.at[:, my_cols], at_core))
+    for block in (
+        rows.at[pl.ds(s0, slots), my_cols],
+        rows.at[pl.ds(s1, slots), my_cols],
+        vec.at[:, my_cols],
+    ):
+        from_core.append(remote(block, block, at_core))
     for src, dst, at in ((hid_hbm.at[0], rows, t0), (hid_hbm.at[1], rows, t1)):
         from_core.append(remote(src, dst.at[pl.ds(at + my_toks, toks), my_cols], at_core))
-    late_core = [remote(dsum_hbm, dsum.at[:, my_cols], at_core)]
+    late_core = [remote(dsum.at[:, my_cols], dsum.at[:, my_cols], at_core)]
     for src, dst, at in ((dhid_hbm.at[0], gd, t0), (dhid_hbm.at[1], gd, t1)):
         late_core.append(remote(src, dst.at[pl.ds(at + my_toks, toks), my_cols], at_core))
     for copy in weights[3:]:
@@ -436,10 +505,10 @@
     live_count = count_ref[0]
     row_live = (lax.broadcasted_iota(jnp.int32, (slots, 1), 0) < live_count).astype(F32)
     dqkv[pl.ds(p0, slots), pl.ds(0, nq)] = jnp.zeros((slots, nq), BF)
-    bias[:, pl.ds(0, nq)] = vecu_ref[:, pl.ds(pl.multiple_of(s * nq, nq), nq)]
     bias[:, pl.ds(nq, nq)] = jnp.zeros((1, nq), F32)
-    bias[:, pl.ds(2 * nq, nq)] = vecu_ref[:, pl.ds(pl.multiple_of((2 + s) * nq, nq), nq)]
-    bias[:, pl.ds(3 * nq, nu)] = vecu_ref[:, pl.ds(pl.multiple_of(4 * nq + s * nu, nq), nu)]
+    for ref, at, n in ((bq_ref, 0, nq), (bv_ref, 2 * nq, nq), (bu_ref, 3 * nq, nu)):
+        x = ref[...].astype(F32)[None]
+        bias[:, pl.ds(at, n)] = jnp.where(s == 0, x[:, :n], x[:, n:])
     fsum[...] = jnp.zeros_like(fsum)
     gsum[...] = jnp.zeros_like(gsum)
 
@@ -697,36 +766,299 @@
             dqkv[k_rows, col(1)] = (dk * scale).astype(BF)
             dqkv[k_rows, col(2)] = dv.astype(BF)
 
-    stays, gifts, passed = [], [], []
-
-    def share_feats(src, dst, at, n):
-        stays.append(local(src.at[pl.ds(at, n), :], dst.at[0, pl.ds(at, n), :]))
-        landing = dst.at[1, pl.ds(at, n), my_cols]
-        gifts.append((remote(src.at[pl.ds(at, n), my_cols], landing, at_p), landing))
-
-    def pass_on():
-        while gifts:
+    gifts_a, gifts_b, passed = [], [], []
+    hu = nu // 2
+
+    def share_feats_a(op, src, at, n):
+        landing = lxx.at[op, pl.ds(at, n), my_cols]
+        gifts_a.append((remote(src.at[pl.ds(at, n), my_cols], landing, at_p), landing))
+
+    def share_units_a(src, col, at, n):
+        its = pl.ds(pl.multiple_of((1 - zl) * hu, hu), hu)
+        landing = rbx.at[pl.ds(at, n), pl.ds(col, hu)]
+        gifts_a.append((remote(src.at[pl.ds(at, n), its], landing, at_p), None))
+
+    def share_feats_b(src, dst, at, n):
+        landing = dst.at[pl.ds(at, n), my_cols]
+        gifts_b.append((remote(src.at[pl.ds(at, n), my_cols], landing, at_y), landing))
+
+    def share_units_b(src, dst, at, n):
+        gifts_b.append((remote(src.at[pl.ds(at, n), :], dst.at[pl.ds(at, n), :], at_y), None))
+
+    def pass_on(gifts, most=1000):
+        while gifts and most:
+            most -= 1
             copy, landing = gifts.pop(0)
             copy.wait()
             if landing is not None:
                 passed.append(remote(landing, landing, at_core))
 
-    def share_units(src, col, n, dst, dst_col, at, rn):
-        mine = pl.ds(pl.multiple_of(col + zl * n, n), n)
-        its = pl.ds(pl.multiple_of(col + (1 - zl) * n, n), n)
-        to = pl.ds(dst_col, n)
-        stays.append(local(src.at[pl.ds(at, rn), mine], dst.at[0, pl.ds(at, rn), to]))
-        gifts.append((remote(src.at[pl.ds(at, rn), its], dst.at[1, pl.ds(at, rn), to], at_p), None))
-
-    hq, hu = nq // 2, nu // 2
-
-    def share_qkv(at, n):
-        for g in range(3):
-            share_units(dqkv, g * nq, hq, ra_hbm, g * hq, at, n)
-
-    share_mix = lambda at, n: share_units(mix, 0, hq, rb_hbm, 0, at, n)
-    share_db = lambda at, n: share_units(db, 0, hu, rb_hbm, hq, at, n)
-    share_actv = lambda at, n: share_units(actv, 0, hu, rb_hbm, hq + hu, at, n)
+    def pass_end():
+        while passed:
+            passed.pop(0).wait()
+
+    share_qkv = lambda at, n: share_units_b(dqkv, ra_hbm, at, n)
+    share_mix = lambda at, n: share_units_b(mix, mx_hbm, at, n)
+    share_actv = lambda at, n: share_units_a(actv, 0, at, n)
+    share_db = lambda at, n: share_units_a(db, hu, at, n)
+
+    width = nq // 2
+    chunk = feats >> bits
+    near = chunk // 2
+    chunks = 1 << (bits - 1)
+    per = hu // width
+    tiles_a, tiles_b = 2 * per, 4 * nq // width
+    nh = len(halving)
+    strips = Strips([wu, wd], width)
+    recv_y = strips.take(tiles_a, chunks * chunk, near)
+    send_y = strips.take(tiles_a, chunks * chunk, near)
+    recv_za = [strips.take(tiles_a, chunks * chunk >> (k + 1), near) for k in range(nh)]
+    recv_pb = strips.take(tiles_b, chunks * chunk // 2, near)
+    recv_zb = [strips.take(tiles_b, chunks * chunk >> (k + 2), near) for k in range(nh)]
+    recv_pa = strips.take(tiles_a, chunk, near)
+    recv_xa = strips.take(tiles_a, chunk, near)
+    recv_xb = strips.take(tiles_b, near, near)
+    strips = Strips([wqkv, wo], width)
+    send_za = [strips.take(tiles_a, chunks * chunk >> (k + 1), near) for k in range(nh)]
+    send_pb = strips.take(tiles_b, chunks * chunk // 2, near)
+    send_zb = [strips.take(tiles_b, chunks * chunk >> (k + 2), near) for k in range(nh)]
+    send_pa = strips.take(tiles_a, chunk, near)
+
+    def linked(src, dst, sem, partner):
+        return pltpu.make_async_remote_copy(
+            src_ref=src,
+            dst_ref=dst,
+            send_sem=sem.at[0],
+            recv_sem=sem.at[1],
+            device_id=partner,
+            device_id_type=MESH,
+        )
+
+    copy_y = lambda i: linked(send_y(i), recv_y(i), sem_y.at[i], at_y)
+    copy_za = lambda k, i: linked(send_za[k](i), recv_za[k](i), sem_za.at[k, i], at_h[k])
+    copy_pa = lambda i: linked(send_pa(i), recv_pa(i), sem_pa.at[i], at_p)
+    copy_pb = lambda i: linked(send_pb(i), recv_pb(i), sem_pb.at[i], at_p)
+    copy_zb = lambda k, i: linked(send_zb[k](i), recv_zb[k](i), sem_zb.at[k, i], at_h[k])
+
+    def block_product(l1, l2, r1, r2, c):
+        def dots(cols):
+            return dot_tn(l1(cols), r1) + dot_tn(l2(cols), r2)
+
+        if chunk % 128 == 0:
+            return dots(pl.ds(pl.multiple_of(c * chunk, chunk), chunk))
+        both[...] = dots(pl.ds(pl.multiple_of((c // 2) * 2 * chunk, 2 * chunk), 2 * chunk))
+        return both[pl.ds(pl.multiple_of((c % 2) * chunk, chunk), chunk), :]
+
+    def products_a(i, parts):
+        for op, (left, right) in enumerate(((gd, actv), (act2, db))):
+
+            @pl.when(i // per == op)
+            def _():
+                mine = pl.ds(pl.multiple_of(zl * hu + (i - op * per) * width, width), width)
+                its = pl.ds(pl.multiple_of(i * width, width), width)
+                r1, r2 = right[:, mine], rbx[:, its]
+                for n, which, put, after in parts:
+
+                    @pl.loop(0, n)
+                    def _(j):
+                        l2 = lambda cols: lxx[op, :, cols]
+                        put(j, block_product(lambda cols: left[:, cols], l2, r1, r2, which(j)))
+
+                    after()
+
+    def products_b(i, parts):
+        groups = 3 * nq // width
+        for late in range(2):
+
+            @pl.when(i // groups == late)
+            def _():
+                cols = pl.ds(pl.multiple_of((i - late * groups) * width, width), width)
+                r1, r2 = (mix[:, cols], dmix[:, cols]) if late else (dqkv[:, cols], qkv[:, cols])
+                l1 = (lambda at: gm[:, at]) if late else (lambda at: act1[:, at])
+                l2 = (lambda at: ar_full[pl.ds(0, p0), at]) if late else (lambda at: rows[:, at])
+                for n, which, put, after in parts:
+
+                    @pl.loop(0, n)
+                    def _(j):
+                        put(j, block_product(l1, l2, r1, r2, which(j)))
+
+                    after()
+
+    def rows_at(slab, i, lo, n):
+        return slab.at(i, lo, n)
+
+    def a_first(i):
+        def put(j, v):
+            send_y.at(i, j * chunk, chunk)[...] = v.astype(BF)
+
+        products_a(i, [(chunks, lambda j: 2 * j + 1 - y, put, lambda: copy_y(i).start())])
+
+    def a_second(i):
+        copy_y(i).wait()
+        bit = bit_of(b, halving[0])
+        n = chunks // 2
+
+        def total(j, v, at):
+            return (v + recv_y.at(i, at * chunk, chunk)[...].astype(F32)).astype(BF)
+
+        def give(j, v):
+            send_za[0].at(i, j * chunk, chunk)[...] = total(j, v, (1 - bit) * n + j)
+
+        def keep(j, v):
+            x = total(j, v, bit * n + j)
+            recv_y.at(i, j * chunk, chunk)[...] = x
+
+        products_a(
+            i,
+            [
+                (n, lambda j: 2 * ((1 - bit) * n + j) + y, give, lambda: copy_za(0, i).start()),
+                (n, lambda j: 2 * (bit * n + j) + y, keep, lambda: None),
+            ],
+        )
+
+    def halve(i, k, kept, at, recv, n, give, copy, start):
+        def total(c):
+            x = kept.at(i, (at + c) * chunk, chunk)[...].astype(F32)
+            return (x + recv.at(i, c * chunk, chunk)[...].astype(F32)).astype(BF)
+
+        bit = start
+        for j in range(n // 2):
+            give.at(i, j * chunk, chunk)[...] = total((1 - bit) * (n // 2) + j)
+        copy().start()
+        for j in range(n // 2):
+            x = total(bit * (n // 2) + j)
+            kept.at(i, (at + n + j) * chunk, chunk)[...] = x
+
+    ends_a = [0]
+    for k in range(nh + 1):
+        ends_a.append(ends_a[-1] + (chunks >> (k + 1)))
+
+    def a_third(k, i):
+        copy_za(k, i).wait()
+        n = chunks >> (k + 1)
+        if k + 1 < nh:
+            bit = bit_of(b, halving[k + 1])
+            halve(i, k, recv_y, ends_a[k], recv_za[k], n, send_za[k + 1], lambda: copy_za(k + 1, i), bit)
+        else:
+            halve(i, k, recv_y, ends_a[k], recv_za[k], n, send_pa, lambda: copy_pa(i), zl)
+
+    my_near = pl.multiple_of(s * near, near)
+    its_near = pl.multiple_of((1 - s) * near, near)
+    kept_a = lambda i, at: recv_y.at(i, ends_a[nh] * chunk + at, near)
+
+    def copies_xa(i):
+        return [
+            linked(kept_a(i, its_near), recv_xa.at(i, zl * near, near), sem_xa.at[i, 0], at_x),
+            linked(
+                recv_pa.at(i, its_near, near),
+                recv_xa.at(i, (1 - zl) * near, near),
+                sem_xa.at[i, 1],
+                at_x,
+            ),
+        ]
+
+    def outs_a(i):
+        def to(side, pair):
+            col = 8 * nq + (1 - i // per) * 2 * nu + side * nu + pair * hu + (i % per) * width
+            return w_hbm.at[:, pl.ds(pl.multiple_of(col, width), width)]
+
+        pieces = [
+            (kept_a(i, my_near), to(s, zl)),
+            (recv_pa.at(i, my_near, near), to(s, 1 - zl)),
+            (recv_xa.at(i, 0, near), to(1 - s, 0)),
+            (recv_xa.at(i, near, near), to(1 - s, 1)),
+        ]
+        return [pltpu.make_async_copy(src, dst, sem_oa.at[i, k]) for k, (src, dst) in enumerate(pieces)]
+
+    def a_fourth(i):
+        copy_pa(i).wait()
+        for copy in copies_xa(i) + outs_a(i)[:2]:
+            copy.start()
+
+    def a_fifth(i):
+        for copy in copies_xa(i):
+            copy.wait()
+        for copy in outs_a(i)[2:]:
+            copy.start()
+
+    def b_first(i):
+        n = chunks // 2
+
+        def put(j, v):
+            send_pb.at(i, j * chunk, chunk)[...] = v.astype(BF)
+
+        products_b(i, [(n, lambda j: 2 * (2 * j + 1 - zl) + y, put, lambda: copy_pb(i).start())])
+
+    def b_second(i):
+        copy_pb(i).wait()
+        bit = bit_of(b, halving[0])
+        n = chunks // 4
+
+        def total(v, at):
+            return (v + recv_pb.at(i, at * chunk, chunk)[...].astype(F32)).astype(BF)
+
+        def give(j, v):
+            send_zb[0].at(i, j * chunk, chunk)[...] = total(v, (1 - bit) * n + j)
+
+        def keep(j, v):
+            x = total(v, bit * n + j)
+            recv_pb.at(i, j * chunk, chunk)[...] = x
+
+        products_b(
+            i,
+            [
+                (n, lambda j: 2 * (2 * ((1 - bit) * n + j) + zl) + y, give, lambda: copy_zb(0, i).start()),
+                (n, lambda j: 2 * (2 * (bit * n + j) + zl) + y, keep, lambda: None),
+            ],
+        )
+
+    ends_b = [0]
+    for k in range(nh):
+        ends_b.append(ends_b[-1] + (chunks >> (k + 2)))
+    kept_b = lambda i, at: recv_pb.at(i, ends_b[nh] * chunk + at, near)
+
+    def copy_xb(i):
+        return linked(kept_b(i, its_near), recv_xb(i), sem_xb.at[i], at_x)
+
+    def outs_b(i):
+        def to(side):
+            col = (i // 2) * 2 * nq + side * nq + (i % 2) * width
+            return w_hbm.at[:, pl.ds(pl.multiple_of(col, width), width)]
+
+        return [
+            pltpu.make_async_copy(kept_b(i, my_near), to(s), sem_ob.at[i, 0]),
+            pltpu.make_async_copy(recv_xb(i), to(1 - s), sem_ob.at[i, 1]),
+        ]
+
+    def b_third(k, i):
+        copy_zb(k, i).wait()
+        n = chunks >> (k + 2)
+        if k + 1 < nh:
+            bit = bit_of(b, halving[k + 1])
+            halve(i, k, recv_pb, ends_b[k], recv_zb[k], n, send_zb[k + 1], lambda: copy_zb(k + 1, i), bit)
+        else:
+            x = recv_pb.at(i, ends_b[k] * chunk, chunk)[...].astype(F32) + recv_zb[k](i)[...].astype(F32)
+            recv_pb.at(i, ends_b[nh] * chunk, chunk)[...] = x.astype(BF)
+            copy_xb(i).start()
+            outs_b(i)[0].start()
+
+    def b_fourth(i):
+        copy_xb(i).wait()
+        outs_b(i)[1].start()
+
+    small_partners = [at_y] + at_h + [at_p, at_x]
+
+    def small_step(k):
+        copy = lambda k: linked(small_out, small_recv.at[k], sem_s.at[k], small_partners[k])
+        if k > 0:
+            copy(k - 1).wait()
+            if k < len(small_partners):
+                small_out[...] = small_out[...] + small_recv[k - 1]
+        if k < len(small_partners):
+            copy(k).start()
+        else:
+            small_final[s] = small_out[...]
+            small_final[1 - s] = small_recv[k - 1]
 
     for copy in firsts:
         copy.wait()
@@ -739,7 +1071,7 @@
     for copy in forwards:
         copy.wait()
     norm1(0, p0)
-    share_feats(act1, la_hbm, 0, p0)
+    share_feats_b(act1, la_hbm, 0, p0)
     for copy in weights[:3]:
         copy.wait()
     project(0, p0, 0, 3 * nq)
@@ -762,7 +1094,7 @@
     for copy in forwards + laters + late_core:
         copy.wait()
     gd[pl.ds(s1, slots), :] = (dsum[pl.ds(slots, slots), :].astype(F32) * row_live).astype(BF)
-    share_feats(gd, lx_hbm.at[2], t0, p0 - t0)
+    share_feats_a(0, gd, t0, p0 - t0)
     a1.finish()
     a1.done()
     enter_ffn(a1, s0, slots)
@@ -777,7 +1109,7 @@
     enter_ffn(a2, t0, T)
     outacc[0] = mid[pl.ds(t0 + my_toks, toks), my_cols]
     a3.finish()
-    share_feats(act2, lx_hbm.at[1], s0, own)
+    share_feats_a(1, act2, s0, own)
     a3.done()
 
     def summary(i):
@@ -791,7 +1123,7 @@
     pl.loop(0, slots // step)(summary)
     sum_out[0] = rows[pl.ds(p0, slots), my_cols]
     norm1(p0, slots)
-    share_feats(act1, la_hbm, p0, slots)
+    share_feats_b(act1, la_hbm, p0, slots)
     project(p0, slots, nq, 3 * nq)
     attend(1)
     share_mix(t1, own)
@@ -811,7 +1143,7 @@
     enter_ffn(a5, t1, own)
     outacc[1] = mid[pl.ds(t1 + my_toks, toks), my_cols]
     outacc[2] = mid[pl.ds(s1, slots), my_cols]
-    share_feats(act2, lx_hbm.at[1], t1, own)
+    share_feats_a(1, act2, t1, own)
     ffn(t1, own, True)
     share_actv(t1, own)
     share_db(t1, own)
@@ -826,7 +1158,7 @@
     a6.done()
     leave_ffn(a6, t0, T)
     mix_back(t0, T)
-    share_feats(gm, lx_hbm.at[0], t0, T)
+    share_feats_b(gm, lm_hbm, t0, T)
     a8.finish()
     for copy in a4.xs:
         copy.wait()
@@ -834,7 +1166,7 @@
     a8.done()
     leave_ffn(a8, t1, own)
     mix_back(t1, own)
-    share_feats(gm, lx_hbm.at[0], t1, own)
+    share_feats_b(gm, lm_hbm, t1, own)
     attend_back(1)
     share_qkv(t1, own + slots)
     a9 = Total(slots, 0, 0, whole(slots))
@@ -869,7 +1201,7 @@
         gd[g, :] = ((dsum[pl.ds(pl.multiple_of(i * step, step), step), :].astype(F32) + d) * on).astype(BF)
 
     pl.loop(0, slots // step)(prefix_back)
-    share_feats(gd, lx_hbm.at[2], s0, slots)
+    share_feats_a(0, gd, s0, slots)
 
     def last_before(c):
         cols = pl.ds(c, wide)
@@ -880,6 +1212,9 @@
     share_db(s0, slots)
     a11 = Total(slots, slots, slots, whole(slots))
     a11.start(up_back(s0, slots))
+    askers = [at_x, at_p, at_y] + at_h
+    for k, partner in enumerate(askers):
+        pl.semaphore_signal(free.at[k], inc=1, device_id=partner, device_id_type=MESH)
     a10.finish()
     a11.middle()
     a10.done()
@@ -908,16 +1243,23 @@
 
     emb_wide = slope0
     rows_back(a10, 1)
+    pass_on(gifts_a)
     a11.finish()
+    pass_end()
+    for k in range(len(askers)):
+        pl.semaphore_wait(free.at[k], 1)
+    a_first(0)
     a11.done()
     leave_ffn(a11, s0, slots)
     mix_back(s0, slots)
-    share_feats(gm, lx_hbm.at[0], s0, slots)
+    a_first(1)
+    share_feats_b(gm, lm_hbm, s0, slots)
     attend_back(0)
     share_qkv(0, own)
     a12 = Total(own, 2 * slots + T + own, 2 * slots + T + own, [(0, slots, False), (slots, T, True)])
     a12.start(in_back(s0, own, 0))
     a12.middle()
+    a_first(2)
     ones = jnp.ones((8, p0), BF)
     column = lambda ref, cols: jnp.dot(ones, ref[pl.ds(0, p0), cols], preferred_element_type=F32)[0:1, :]
     base = slots
@@ -932,7 +1274,7 @@
     for k in range(nu // quarter):
         small_out[base + 8 + k : base + 9 + k, :] = column(db, pl.ds(k * quarter, quarter))
     small_out[base + 12 : base + 16, :] = jnp.zeros((4, quarter), F32)
-    pass_on()
+    pass_on(gifts_b)
     a12.finish()
     a12.done()
     rows_back(a12, 0)
@@ -945,17 +1287,70 @@
     copy.wait()
     small_out[base : base + 1, :] = gx_recv[0:1, :] + jnp.sum(gsum[pl.ds(0, 8), my_quarter], axis=0, keepdims=True)
     small_out[base + 1 : base + 2, :] = gx_recv[1:2, :] + jnp.sum(gsum[pl.ds(8, 8), my_quarter], axis=0, keepdims=True)
-    for copy in stays + passed:
+    small_step(0)
+    pass_end()
+    stage = [
+        local(la_hbm, rows),
+        local(lm_hbm, ar_full.at[pl.ds(0, p0), :]),
+        local(ra_hbm, qkv),
+        local(mx_hbm, dmix),
+    ]
+    for copy in stage:
         copy.wait()
 
-def chain(count, vecu, hid, dhid, emb, dsum, vec, wq, wk, wv, wo, wu, wd):
-    toks, slots = hid.shape[1], emb.shape[0]
+    lead = 3
+
+    def turn(it, lag, count, stage):
+        @pl.when((it >= lag) & (it < lag + count))
+        def _():
+            stage(it - lag)
+
+    turns = max(tiles_a + nh + 3, tiles_b + nh + 4)
+
+    @pl.loop(0, turns)
+    def _(it):
+        @pl.when(it < tiles_a - lead)
+        def _():
+            a_first(it + lead)
+
+        turn(it, 0, tiles_b, b_first)
+        turn(it, 0, tiles_a, a_second)
+        turn(it, 2, tiles_b, b_second)
+        for k in range(nh):
+            turn(it, k + 1, tiles_a, functools.partial(a_third, k))
+        turn(it, nh + 1, tiles_a, a_fourth)
+        turn(it, nh + 2, tiles_a, a_fifth)
+        for k in range(nh):
+            turn(it, k + 3, tiles_b, functools.partial(b_third, k))
+        turn(it, nh + 3, tiles_b, b_fourth)
+        for k in range(1, len(small_partners) + 1):
+
+            @pl.when(it == 2 * k)
+            def _():
+                small_step(k)
+
+    @pl.loop(0, tiles_a)
+    def _(i):
+        for copy in outs_a(i):
+            copy.wait()
+
+    @pl.loop(0, tiles_b)
+    def _(i):
+        for copy in outs_b(i):
+            copy.wait()
+
+def chain(count, emb, dsum, feat_vecs, bq, bv, bu, hid, dhid, wq, wk, wv, wo, wu, wd):
+    bits = lax.axis_size("batch").bit_length() - 1
+    toks, slots = hid.shape[1], emb.shape[0] + -emb.shape[0] % 64
     half = hid.shape[2]
     feats, quarter = 2 * half, half // 2
     nq, nu = wo.shape[0] // 2, wd.shape[0] // 2
     own = 2 * toks + slots
     main, end = 2 * own, 2 * own + slots
     sums = 2 * slots + 2 * toks + 2 * own
+    chunk = feats >> bits
+    nh = bits - 2
+    ta, tb = 2 * nu // nq, 8
     vm = pltpu.VMEM
     sds = jax.ShapeDtypeStruct
     dma = pltpu.SemaphoreType.DMA
@@ -992,70 +1387,117 @@
         vm((sums + 2 * toks + own, half), BF),
         vm((sums, feats), BF),
         vm((2 * toks + own, half), BF),
+        vm((2, main, feats), BF),
+        vm((main, nu), BF),
+        vm((2 * chunk if chunk % 128 else 8, nq // 2), F32),
+        vm((slots + 16, quarter), F32),
+        vm((bits + 1, slots + 16, quarter), F32),
         dma((6,)),
-        dma((48,)),
+        dma((16,)),
         dma((128, 2)),
+        pltpu.SemaphoreType.REGULAR((3 + nh,)),
+        dma((ta, 2)),
+        dma((nh, ta, 2)),
+        dma((ta, 2)),
+        dma((ta, 2, 2)),
+        dma((tb, 2)),
+        dma((nh, tb, 2)),
+        dma((tb, 2)),
+        dma((ta, 4)),
+        dma((tb, 2)),
+        dma((bits + 1, 2)),
     ]
     vmem = pl.BlockSpec(memory_space=pltpu.VMEM)
     hbm = pl.BlockSpec(memory_space=pl.ANY)
     smem = pl.BlockSpec(memory_space=pltpu.SMEM)
     return pl.pallas_call(
-        chain_kernel,
-        name="chain",
+        functools.partial(chain_kernel, bits),
+        name="layer",
         out_shape=(
             sds((2, toks, half), BF),
             sds((2, slots, half), BF),
             sds((2, toks, half), F32),
-            sds((slots + 16, quarter), F32),
-            sds((2, end, feats), BF),
-            sds((3, 2, main, feats), BF),
-            sds((2, end, 3 * nq // 2), BF),
-            sds((2, main, nq // 2 + nu), BF),
+            sds((2, slots + 16, quarter), F32),
+            sds((chunk // 2, 8 * nq + 4 * nu), BF),
+            sds((end, feats), BF),
+            sds((main, feats), BF),
+            sds((end, 3 * nq), BF),
+            sds((main, nq), BF),
         ),
-        in_specs=[smem, vmem] + [hbm] * 11,
-        out_specs=(vmem,) * 4 + (hbm,) * 4,
+        in_specs=[smem, vmem, vmem, [vmem] * 6, vmem, vmem, vmem] + [hbm] * 8,
+        out_specs=(vmem,) * 4 + (hbm,) * 5,
         scratch_shapes=scratch,
         compiler_params=pltpu.CompilerParams(
-            collective_id=2, has_side_effects=True, vmem_limit_bytes=62 * 2**20
+            collective_id=2, has_side_effects=True, vmem_limit_bytes=63 * 2**20
         ),
-    )(count, vecu, hid, dhid, emb, dsum, vec, wq, wk, wv, wo, wu, wd)
+    )(count, emb, dsum, feat_vecs, bq, bv, bu, hid, dhid, wq, wk, wv, wo, wu, wd)
+
+
+def place_kernel(hid, sums, gin, small, w, hid_o, sum_o, gin_o, emb_o, vec_o, bup_o, q_o, k_o, v_o, o_o, u_o, d_o):
+    hid_o[0] = hid[...]
+    used = sum_o.shape[2]
+    sum_o[0] = sums[:, :used, :]
+    gin_o[0] = gin[...]
+    quarter = small.shape[2]
+    base = small.shape[1] - 16
+    nu = bup_o.shape[0] // 2
+    for side in range(2):
+        at = pl.ds(side * quarter, quarter)
+        emb_o[:, at] = small[side, :used, :]
+        for k, ref in enumerate(vec_o):
+            ref[at] = small[side, base + k]
+        for k in range(nu // quarter):
+            bup_o[pl.ds(side * nu + k * quarter, quarter)] = small[side, base + 8 + k]
+    n = q_o.shape[1]
+    for k, ref in enumerate((q_o, k_o, v_o)):
+        ref[...] = w[:, k * n : (k + 1) * n].astype(F32)
+    o_o[...] = w[:, 3 * n : 4 * n].astype(F32).T
+    u_o[...] = w[:, 4 * n : 4 * n + 2 * nu].astype(F32)
+    d_o[...] = w[:, 4 * n + 2 * nu :].astype(F32).T
+
+
+def place(hid, sums, gin, small, w, used):
+    sds = jax.ShapeDtypeStruct
+    _, toks, half = hid.shape
+    rows = w.shape[0]
+    nu = (w.shape[1] - 4 * half) // 4
+    vmem = pl.BlockSpec(memory_space=pltpu.VMEM)
+    return pl.pallas_call(
+        place_kernel,
+        name="place",
+        out_shape=(
+            sds((1, 2, toks, half), BF),
+            sds((1, 2, used, half), BF),
+            sds((1, 2, toks, half), F32),
+            sds((used, half), F32),
+            [sds((half,), F32)] * 8,
+            sds((2 * nu,), F32),
+            sds((rows, half), F32),
+            sds((rows, half), F32),
+            sds((rows, half), F32),
+            sds((half, rows), F32),
+            sds((rows, 2 * nu), F32),
+            sds((2 * nu, rows), F32),
+        ),
+        in_specs=[vmem] * 5,
+        out_specs=(vmem,) * 4 + ([vmem] * 8,) + (vmem,) * 7,
+        compiler_params=pltpu.CompilerParams(vmem_limit_bytes=32 * 2**20),
+    )(hid, sums, gin, small, w)
 
 
 def local(
     hidden_in, summary_counts, summary_embed, ln1_gain, ln1_bias, w_query, b_query, w_key, w_value,
     b_value, w_out, b_out, ln2_gain, ln2_bias, w_up, b_up, w_down, b_down, d_hidden, d_summary,
 ):
-    n = summary_embed.shape[0]
-    pad = -n % 64
-    emb = jnp.pad(summary_embed, ((0, pad), (0, 0)))
-    dsum = jnp.pad(d_summary[0], ((0, 0), (0, pad), (0, 0))).reshape(-1, d_summary.shape[3])
-    zero = jnp.zeros_like(ln1_gain)
-    vec = jnp.stack([ln1_gain, ln1_bias, ln2_gain, ln2_bias, b_out, b_down, zero, zero]).astype(F32)
-    vecu = jnp.concatenate([b_query, b_value, b_up]).astype(F32)[None]
-    nq, nu = w_query.shape[1] // 2, w_up.shape[1] // 2
-    hid, summaries, gin, small, la, lx, ra, rb = chain(
-        summary_counts, vecu, hidden_in[0], d_hidden[0], emb, dsum, vec,
-        w_query, w_key, w_value, w_out, w_up, w_down,
+    got = chain(
+        summary_counts, summary_embed, d_summary,
+        [ln1_gain, ln1_bias, ln2_gain, ln2_bias, b_out, b_down], b_query, b_value, b_up,
+        hidden_in[0], d_hidden[0], w_query, w_key, w_value, w_out, w_up, w_down,
     )
-    flat = lambda x: x.reshape(x.shape[:-3] + (-1, x.shape[-1]))
-    width = nq // 2
-    w, sm = reduce_grads(flat(la), flat(lx), flat(ra), flat(rb), small, width)
-
-    def place(lo, hi):
-        x = w[lo:hi]
-        return x.transpose(3, 1, 2, 0, 4).reshape(x.shape[3], -1)
-
-    per = nu // 2 // width
-    gq, gk, gv, go = (place(i, i + 1) for i in range(4))
-    gu, gdn = place(4, 4 + per), place(4 + per, 4 + 2 * per)
-    sm = sm.transpose(1, 0, 2)
-    at = n + pad
-    fl = lambda r: sm[at + r].reshape(-1)
-    bup = sm[at + 8 : at + 8 + nu // sm.shape[2]].transpose(1, 0, 2).reshape(-1)
+    hid, sums, gin, emb, vecs, bup, gq, gk, gv, go, gu, gd = place(*got[:5], summary_embed.shape[0])
     return (
-        hid[None], summaries[None, :, :n], gin[None],
-        sm[:n].reshape(n, -1), fl(0), fl(1), gq, fl(6), gk, gv, fl(7), go.T, fl(2),
-        fl(3), fl(4), gu, bup, gdn.T, fl(5),
+        hid, sums, gin, emb, vecs[0], vecs[1], gq, vecs[6], gk, gv,
+        vecs[7], go, vecs[2], vecs[3], vecs[4], gu, bup, gd, vecs[5],
     )
 
 

time: 388 us -> 342 us (0.88)
  local copies, waits for them, and re-layouts: 36.9 us -> 8.35 us
  Pallas kernels: 348 us -> 332 us
    pallas_call x2, Pallas kernels: 348 us -> 332 us  [the longest x1 328 us: chain(): pl.pallas_call(functools.partial(chain_kernel, bits), name='layer', out_s...]
    transpose x8 -> x0, local copies, waits for them, and re-layouts: 14 us -> none  [place(): return x.transpose(3, 1, 2, 0, 4).reshape(x.shape[3], -1)]
    another operation x8 -> x0, local copies, waits for them, and re-layouts: 4.17 us -> none  [local(): jnp.stack([ln1_gain, ln1_bias, ln2_gain, ln2_bias, b_out, b_down, zero, z...]
    unnamed x16 -> x12, local copies, waits for them, and re-layouts: 10.4 us -> 8.35 us
where the time goes in v3:
time: 342 us; the launch traced here: 341 us
  Pallas kernels  332 us (97%)
  local copies, waits for them, and re-layouts  8.35 us (2%)
    pallas_call x1, Pallas kernels, chain(): pl.pallas_call(functools.partial(chain_kernel, bits), name='layer', out_s...  328 us
    unnamed x12, local copies, waits for them, and re-layouts  8.35 us

profile of v3, /device:TPU:0, one launch (start us, length us, event | category | flops | bytes accessed | tf_op | source)
XLA Modules:
  0.0 341.3 jit_solution(13611857410918132086)
XLA Ops:
  1.3 1.7 copy.39.dsum_ref
  3.0 328.2 %layer.1 = (bf16[2,64,1024]{2,1,0:T(8,128)(2,1)}, bf16[2,64,1024]{2,1,0:T(8,128)(2,1)}, f32[2,64,1024]{2,1,0:T(8,128)}, f32[2,80,512]{2,1,0:T(8,128)}, bf16[128,...) custom-call(s32[1]{0:T(128)S(6)} %copy.41.count_ref, ...), custom_call_target="tpu_custom_call" | custom-call | tf_op jit(solution)/shard_map/layer/pallas_call | solution.py:1413
  331.1 0.0 copy-start
  331.1 1.9 copy-done
  333.0 0.0 copy-start.1
  333.0 1.0 copy-done.1
  334.1 0.0 copy-start.2
  334.1 1.0 copy-done.2
  335.0 0.0 copy-start.3
  335.0 0.9 copy-done.3
  336.0 0.0 copy-start.4
  336.0 0.9 copy-done.4
  336.9 3.4 %place.1 = (bf16[1,2,64,1024]{3,2,1,0:T(8,128)(2,1)}, bf16[1,2,50,1024]{3,2,1,0:T(8,128)(2,1)S(1)}, f32[1,2,64,1024]{3,2,1,0:T(8,128)}, f32[50,1024]{1,0:T(8,128...) custom-call(bf16[2,64,1024]{2,1,0:T(8,128)(2,1)S(1)} %copy-done.3, ...), custom_call_target="tpu_custom_call" | custom-call | tf_op jit(solution)/shard_map/place/pallas_call | solution.py:1465
  340.4 0.9 copy.40
Async XLA Ops:
  331.1 1.9 copy-start
  333.0 1.0 copy-start.1
  334.1 1.0 copy-start.2
  335.0 0.9 copy-start.3
  336.0 0.9 copy-start.4

commit v4 on v3

--- a/solution.py
+++ b/solution.py
@@ -474,29 +474,31 @@
         rows[pl.ds(at, used), my_cols] = emb_ref[...]
     for seg in range(2):
         dsum[pl.ds(seg * slots, slots), my_cols] = jnp.zeros((slots, half), BF)
-        dsum[pl.ds(seg * slots, used), my_cols] = dsum_ref[0, seg]
+        dsum[pl.ds(seg * slots, used), my_cols] = dsum_ref[:, seg, :]
     for k, ref in enumerate(feat_refs):
         vec[k : k + 1, my_cols] = ref[...].astype(F32)[None]
     pl.semaphore_wait(barrier, len(partners))
 
-    from_x, from_core, forwards = [], [], []
-    for src, dst, at in (
-        (hid_hbm.at[0], rows, t0),
-        (hid_hbm.at[1], rows, t1),
-        (dhid_hbm.at[0], gd, t0),
-        (dhid_hbm.at[1], gd, t1),
-    ):
-        block = dst.at[pl.ds(at + my_toks, toks), my_cols]
-        from_x.append((remote(src, block, at_x), dst, at))
-    for block in (
-        rows.at[pl.ds(s0, slots), my_cols],
-        rows.at[pl.ds(s1, slots), my_cols],
-        vec.at[:, my_cols],
-    ):
-        from_core.append(remote(block, block, at_core))
-    for src, dst, at in ((hid_hbm.at[0], rows, t0), (hid_hbm.at[1], rows, t1)):
-        from_core.append(remote(src, dst.at[pl.ds(at + my_toks, toks), my_cols], at_core))
-    late_core = [remote(dsum.at[:, my_cols], dsum.at[:, my_cols], at_core)]
+    def in_x(src, dst, at):
+        return remote(src, dst.at[pl.ds(at + my_toks, toks), my_cols], at_x)
+
+    def in_core(block):
+        return remote(block, block, at_core)
+
+    def in_pass(dst, at):
+        return in_core(dst.at[pl.ds(at + its_toks, toks), my_cols])
+
+    x_hid = [in_x(hid_hbm.at[0], rows, t0)]
+    from_core = [
+        in_core(rows.at[pl.ds(s0, slots), my_cols]),
+        in_core(vec.at[:, my_cols]),
+        remote(hid_hbm.at[0], rows.at[pl.ds(t0 + my_toks, toks), my_cols], at_core),
+    ]
+    late_core = [
+        in_core(rows.at[pl.ds(s1, slots), my_cols]),
+        remote(hid_hbm.at[1], rows.at[pl.ds(t1 + my_toks, toks), my_cols], at_core),
+        in_core(dsum.at[:, my_cols]),
+    ]
     for src, dst, at in ((dhid_hbm.at[0], gd, t0), (dhid_hbm.at[1], gd, t1)):
         late_core.append(remote(src, dst.at[pl.ds(at + my_toks, toks), my_cols], at_core))
     for copy in weights[3:]:
@@ -626,6 +628,19 @@
             for copy in self.backs:
                 copy.wait()
 
+        def flow(self, body):
+            self.backs = []
+            for k, ((base, n, _), copy) in enumerate(zip(self.pieces, self.xs)):
+                copy.wait()
+                block = ar_full.at[pl.ds(self.full + base, n), my_cols]
+                block[...] = self.sums(base, n, False).astype(BF)
+                self.backs.append(remote(block, block, at_core))
+                if k:
+                    self.backs[k - 1].wait()
+                    body(*self.pieces[k - 1][:2])
+            self.backs[-1].wait()
+            body(*self.pieces[-1][:2])
+
     whole = lambda n: [(i, 64, False) for i in range(0, n, 64)]
 
     def out_product(at, n):
@@ -646,10 +661,10 @@
             dqkv[pl.ds(at, n), pl.ds(lo, 3 * nq - lo)], wqkv[pl.ds(c, w), pl.ds(lo, 3 * nq - lo)]
         )
 
-    def enter_ffn(total, at, n):
+    def enter_ffn(total, at, n, base=0):
         def body(i):
-            r = pl.ds(pl.multiple_of(at + i * step, step), step)
-            f = pl.ds(pl.multiple_of(total.full + i * step, step), step)
+            r = pl.ds(pl.multiple_of(at + base + i * step, step), step)
+            f = pl.ds(pl.multiple_of(total.full + base + i * step, step), step)
             x = rows[r, :].astype(F32) + ar_full[f, :].astype(F32) + vec[4:5, :]
             m, rs = stats(x)
             mid[r, :] = x
@@ -666,25 +681,28 @@
         sl = 0.5 * (1.0 + th) + (0.5 * c) * v * (1.0 - th * th) * (1.0 + (3 * 0.044715) * v * v)
         return act, sl
 
-    def ffn(at, n, back):
+    def ffn(at, n, back, lo, hi):
         r = pl.ds(at, n)
 
         def body(c):
+            c = pl.multiple_of(lo + c, wide)
             cols = pl.ds(c, wide)
             v = jnp.dot(act2[r, :], wu[:, cols], preferred_element_type=F32)
             act, sl = gelu(v + bias[:, pl.ds(pl.multiple_of(3 * nq + c, wide), wide)])
             actv[r, cols] = act.astype(BF)
-            if back:
+            if back == 1:
                 db[r, cols] = (sl * dot_nt(gd[r, :], wd[cols, :])).astype(BF)
+            elif back == 2:
+                db[r, cols] = (sl * db[r, cols].astype(F32)).astype(BF)
             else:
                 slope0[:, cols] = sl
 
-        col_loop(nu, body)
-
-    def leave_ffn(total, at, n):
+        col_loop(hi - lo, body)
+
+    def leave_ffn(total, at, n, base=0):
         def body(i):
-            r = pl.ds(pl.multiple_of(at + i * step, step), step)
-            f = pl.ds(pl.multiple_of(total.full + i * step, step), step)
+            r = pl.ds(pl.multiple_of(at + base + i * step, step), step)
+            f = pl.ds(pl.multiple_of(total.full + base + i * step, step), step)
             d = ar_full[f, :].astype(F32)
             xhat = (mid[r, :] - stat[r, 2:3]) * stat[r, 3:4]
             fsum[pl.ds(0, 8), :] = fsum[pl.ds(0, 8), :] + fold(d * xhat)
@@ -768,6 +786,8 @@
 
     gifts_a, gifts_b, passed = [], [], []
     hu = nu // 2
+    chunk = feats >> bits
+    chunks = 1 << (bits - 1)
 
     def share_feats_a(op, src, at, n):
         landing = lxx.at[op, pl.ds(at, n), my_cols]
@@ -779,8 +799,14 @@
         gifts_a.append((remote(src.at[pl.ds(at, n), its], landing, at_p), None))
 
     def share_feats_b(src, dst, at, n):
-        landing = dst.at[pl.ds(at, n), my_cols]
-        gifts_b.append((remote(src.at[pl.ds(at, n), my_cols], landing, at_y), landing))
+        some = [(my_cols, my_cols)]
+        if chunk % 128 == 0:
+            block = lambda c: pl.ds(pl.multiple_of(c * chunk, chunk), chunk)
+            some = [2 * (t * chunks // 2 + m) for m in range(chunks // 2)]
+            some = [(block(c + 1 - y), block(c + y)) for c in some]
+        for out, back in some:
+            copy = remote(src.at[pl.ds(at, n), out], dst.at[pl.ds(at, n), out], at_y)
+            gifts_b.append((copy, dst.at[pl.ds(at, n), back]))
 
     def share_units_b(src, dst, at, n):
         gifts_b.append((remote(src.at[pl.ds(at, n), :], dst.at[pl.ds(at, n), :], at_y), None))
@@ -803,9 +829,7 @@
     share_db = lambda at, n: share_units_a(db, hu, at, n)
 
     width = nq // 2
-    chunk = feats >> bits
     near = chunk // 2
-    chunks = 1 << (bits - 1)
     per = hu // width
     tiles_a, tiles_b = 2 * per, 4 * nq // width
     nh = len(halving)
@@ -867,15 +891,15 @@
                     after()
 
     def products_b(i, parts):
-        groups = 3 * nq // width
-        for late in range(2):
-
-            @pl.when(i // groups == late)
+        groups = nq // width
+        for op in range(2):
+
+            @pl.when(jnp.minimum(i // groups, 1) == op)
             def _():
-                cols = pl.ds(pl.multiple_of((i - late * groups) * width, width), width)
-                r1, r2 = (mix[:, cols], dmix[:, cols]) if late else (dqkv[:, cols], qkv[:, cols])
-                l1 = (lambda at: gm[:, at]) if late else (lambda at: act1[:, at])
-                l2 = (lambda at: ar_full[pl.ds(0, p0), at]) if late else (lambda at: rows[:, at])
+                cols = pl.ds(pl.multiple_of((i - op * groups) * width, width), width)
+                r1, r2 = (dqkv[:, cols], qkv[:, cols]) if op else (mix[:, cols], dmix[:, cols])
+                l1 = (lambda at: act1[:, at]) if op else (lambda at: gm[:, at])
+                l2 = (lambda at: rows[:, at]) if op else (lambda at: ar_full[pl.ds(0, p0), at])
                 for n, which, put, after in parts:
 
                     @pl.loop(0, n)
@@ -957,7 +981,7 @@
             ),
         ]
 
-    def outs_a(i):
+    def outs_a(i, picks):
         def to(side, pair):
             col = 8 * nq + (1 - i // per) * 2 * nu + side * nu + pair * hu + (i % per) * width
             return w_hbm.at[:, pl.ds(pl.multiple_of(col, width), width)]
@@ -968,17 +992,17 @@
             (recv_xa.at(i, 0, near), to(1 - s, 0)),
             (recv_xa.at(i, near, near), to(1 - s, 1)),
         ]
-        return [pltpu.make_async_copy(src, dst, sem_oa.at[i, k]) for k, (src, dst) in enumerate(pieces)]
+        return [pltpu.make_async_copy(*pieces[k], sem_oa.at[i, k]) for k in picks]
 
     def a_fourth(i):
         copy_pa(i).wait()
-        for copy in copies_xa(i) + outs_a(i)[:2]:
+        for copy in copies_xa(i) + outs_a(i, (0, 1)):
             copy.start()
 
     def a_fifth(i):
         for copy in copies_xa(i):
             copy.wait()
-        for copy in outs_a(i)[2:]:
+        for copy in outs_a(i, (2, 3)):
             copy.start()
 
     def b_first(i):
@@ -1020,15 +1044,15 @@
     def copy_xb(i):
         return linked(kept_b(i, its_near), recv_xb(i), sem_xb.at[i], at_x)
 
-    def outs_b(i):
+    def outs_b(i, picks):
         def to(side):
-            col = (i // 2) * 2 * nq + side * nq + (i % 2) * width
+            groups = nq // width
+            op = (i // groups + 3) % 4
+            col = op * 2 * nq + side * nq + (i % groups) * width
             return w_hbm.at[:, pl.ds(pl.multiple_of(col, width), width)]
 
-        return [
-            pltpu.make_async_copy(kept_b(i, my_near), to(s), sem_ob.at[i, 0]),
-            pltpu.make_async_copy(recv_xb(i), to(1 - s), sem_ob.at[i, 1]),
-        ]
+        pieces = [(kept_b(i, my_near), to(s)), (recv_xb(i), to(1 - s))]
+        return [pltpu.make_async_copy(*pieces[k], sem_ob.at[i, k]) for k in picks]
 
     def b_third(k, i):
         copy_zb(k, i).wait()
@@ -1040,11 +1064,11 @@
             x = recv_pb.at(i, ends_b[k] * chunk, chunk)[...].astype(F32) + recv_zb[k](i)[...].astype(F32)
             recv_pb.at(i, ends_b[nh] * chunk, chunk)[...] = x.astype(BF)
             copy_xb(i).start()
-            outs_b(i)[0].start()
+            outs_b(i, (0,))[0].start()
 
     def b_fourth(i):
         copy_xb(i).wait()
-        outs_b(i)[1].start()
+        outs_b(i, (1,))[0].start()
 
     small_partners = [at_y] + at_h + [at_p, at_x]
 
@@ -1060,26 +1084,20 @@
             small_final[s] = small_out[...]
             small_final[1 - s] = small_recv[k - 1]
 
-    for copy in firsts:
+    for copy in firsts + from_core:
         copy.wait()
-    for copy in from_core:
-        copy.wait()
-    for copy, dst, at in from_x[:2]:
-        copy.wait()
-        block = dst.at[pl.ds(at + its_toks, toks), my_cols]
-        forwards.append(remote(block, block, at_core))
-    for copy in forwards:
-        copy.wait()
-    norm1(0, p0)
-    share_feats_b(act1, la_hbm, 0, p0)
+    norm1(s0, slots)
+    norm1(t0 + my_toks, toks)
+    x_hid[0].wait()
+    forward = in_pass(rows, t0)
+    x_hid.append(in_x(hid_hbm.at[1], rows, t1))
+    x_dhid = [in_x(dhid_hbm.at[0], gd, t0), in_x(dhid_hbm.at[1], gd, t1)]
+    forward.wait()
+    norm1(t0 + its_toks, toks)
+    share_feats_b(act1, la_hbm, 0, own)
     for copy in weights[:3]:
         copy.wait()
-    project(0, p0, 0, 3 * nq)
-    forwards = []
-    for copy, dst, at in from_x[2:]:
-        copy.wait()
-        block = dst.at[pl.ds(at + its_toks, toks), my_cols]
-        forwards.append(remote(block, block, at_core))
+    project(0, own, 0, 3 * nq)
     attend(0)
     share_mix(0, own)
     for copy in weights[3:4]:
@@ -1091,15 +1109,27 @@
     a2.start(out_product(t0, T))
     a1.middle()
     a2.middle()
-    for copy in forwards + laters + late_core:
+    x_hid[1].wait()
+    forward = in_pass(rows, t1)
+    for copy in late_core + laters:
         copy.wait()
-    gd[pl.ds(s1, slots), :] = (dsum[pl.ds(slots, slots), :].astype(F32) * row_live).astype(BF)
-    share_feats_a(0, gd, t0, p0 - t0)
+    forward.wait()
+    norm1(t1, own)
+    share_feats_b(act1, la_hbm, t1, own)
+    project(t1, own, 0, 3 * nq)
     a1.finish()
     a1.done()
     enter_ffn(a1, s0, slots)
     weights[4].wait()
-    ffn(s0, slots, False)
+    forwards = []
+    for copy, at in zip(x_dhid, (t0, t1)):
+        copy.wait()
+        forwards.append(in_pass(gd, at))
+    gd[pl.ds(s1, slots), :] = (dsum[pl.ds(slots, slots), :].astype(F32) * row_live).astype(BF)
+    ffn(s0, slots, 0, 0, nu)
+    for copy in forwards:
+        copy.wait()
+    share_feats_a(0, gd, t0, p0 - t0)
     weights[5].wait()
     a3 = Total(slots, slots, slots, whole(slots))
     a3.start(down_product(s0, slots))
@@ -1108,6 +1138,12 @@
     a2.done()
     enter_ffn(a2, t0, T)
     outacc[0] = mid[pl.ds(t0 + my_toks, toks), my_cols]
+
+    def early_before(c):
+        cols, r = pl.ds(c, wide), pl.ds(t1, own)
+        db[r, cols] = dot_nt(gd[r, :], wd[cols, :]).astype(BF)
+
+    col_loop(nu, early_before)
     a3.finish()
     share_feats_a(1, act2, s0, own)
     a3.done()
@@ -1129,44 +1165,38 @@
     share_mix(t1, own)
     a5 = Total(own, 2 * slots + T, 2 * slots + T, whole(own))
     a5.start(out_product(t1, own))
-    ffn(t0, T, True)
+    ffn(t0, T, 1, 0, nu // 4)
+    a5.middle()
+    ffn(t0, T, 1, nu // 4, nu)
     share_actv(s0, own)
     share_db(t0, T)
-    a5.middle()
     a6 = Total(T, 2 * slots, 2 * slots, whole(T))
     a6.start(up_back(t0, T))
     a6.middle()
-    a5.finish()
     a4 = Total(T, 2 * slots + T + 2 * own, None, [(0, T, True)], 0)
     a4.start(down_product(t0, T))
-    a5.done()
-    enter_ffn(a5, t1, own)
+    a5.flow(lambda base, n: enter_ffn(a5, t1, n, base))
+    a4.middle()
     outacc[1] = mid[pl.ds(t1 + my_toks, toks), my_cols]
     outacc[2] = mid[pl.ds(s1, slots), my_cols]
     share_feats_a(1, act2, t1, own)
-    ffn(t1, own, True)
+    ffn(t1, own, 2, 0, nu)
     share_actv(t1, own)
-    share_db(t1, own)
     a8 = Total(own, 2 * slots + T + own, 2 * slots + T + own, whole(own))
     a8.start(up_back(t1, own))
     a6.finish()
-    a4.middle()
     a8.middle()
     a7 = Total(own, 2 * slots + 2 * T + 2 * own, None, [(0, T, True), (T, slots, False)], T)
     a7.start(down_product(t1, own))
-    a7.middle()
     a6.done()
     leave_ffn(a6, t0, T)
     mix_back(t0, T)
     share_feats_b(gm, lm_hbm, t0, T)
-    a8.finish()
-    for copy in a4.xs:
-        copy.wait()
-    hid_out[0] = (outacc[0] + a4.sums(0, T, True) + vec[5:6, my_cols]).astype(BF)
-    a8.done()
-    leave_ffn(a8, t1, own)
+    a8.flow(lambda base, n: leave_ffn(a8, t1, n, base))
+    a7.middle()
     mix_back(t1, own)
     share_feats_b(gm, lm_hbm, t1, own)
+    early_b = len(gifts_b)
     attend_back(1)
     share_qkv(t1, own + slots)
     a9 = Total(slots, 0, 0, whole(slots))
@@ -1174,10 +1204,12 @@
     a10 = Total(own, 2 * slots + T, 2 * slots + T, [(0, T, True), (T, slots, False)])
     a9.middle()
     a10.start(in_back(t1, own, 0))
+    pass_on(gifts_b, early_b)
     a9.finish()
     a10.middle()
-    for copy in a7.xs:
+    for copy in a4.xs + a7.xs:
         copy.wait()
+    hid_out[0] = (outacc[0] + a4.sums(0, T, True) + vec[5:6, my_cols]).astype(BF)
     hid_out[1] = (outacc[1] + a7.sums(0, T, True) + vec[5:6, my_cols]).astype(BF)
     sum_out[1] = (
         (outacc[2] + a7.sums(T, slots, False) + vec[5:6, my_cols]) * row_live
@@ -1202,6 +1234,8 @@
 
     pl.loop(0, slots // step)(prefix_back)
     share_feats_a(0, gd, s0, slots)
+    late_gifts = 1 + len(gifts_a)
+    share_db(t1, own)
 
     def last_before(c):
         cols = pl.ds(c, wide)
@@ -1217,7 +1251,12 @@
         pl.semaphore_signal(free.at[k], inc=1, device_id=partner, device_id_type=MESH)
     a10.finish()
     a11.middle()
+    pass_on(gifts_a, late_gifts - 1)
     a10.done()
+    pass_end()
+    for k in range(len(askers)):
+        pl.semaphore_wait(free.at[k], 1)
+    a_first(0)
 
     def rows_back(total, seg):
         t_at, s_at = (t0, s0) if seg == 0 else (t1, s1)
@@ -1243,23 +1282,28 @@
 
     emb_wide = slope0
     rows_back(a10, 1)
-    pass_on(gifts_a)
     a11.finish()
-    pass_end()
-    for k in range(len(askers)):
-        pl.semaphore_wait(free.at[k], 1)
-    a_first(0)
     a11.done()
     leave_ffn(a11, s0, slots)
     mix_back(s0, slots)
-    a_first(1)
     share_feats_b(gm, lm_hbm, s0, slots)
     attend_back(0)
-    share_qkv(0, own)
+    a_first(1)
     a12 = Total(own, 2 * slots + T + own, 2 * slots + T + own, [(0, slots, False), (slots, T, True)])
     a12.start(in_back(s0, own, 0))
+    pass_on(gifts_b)
     a12.middle()
-    a_first(2)
+    stage = [
+        local(ra_hbm.at[pl.ds(t1, own + slots), :], qkv.at[pl.ds(t1, own + slots), :]),
+        local(mx_hbm, dmix),
+    ]
+    pass_end()
+    stage.append(local(lm_hbm, ar_full.at[pl.ds(0, p0), :]))
+    a_second(0)
+    for copy in stage:
+        copy.wait()
+    b_first(0)
+    b_first(1)
     ones = jnp.ones((8, p0), BF)
     column = lambda ref, cols: jnp.dot(ones, ref[pl.ds(0, p0), cols], preferred_element_type=F32)[0:1, :]
     base = slots
@@ -1274,7 +1318,6 @@
     for k in range(nu // quarter):
         small_out[base + 8 + k : base + 9 + k, :] = column(db, pl.ds(k * quarter, quarter))
     small_out[base + 12 : base + 16, :] = jnp.zeros((4, quarter), F32)
-    pass_on(gifts_b)
     a12.finish()
     a12.done()
     rows_back(a12, 0)
@@ -1287,56 +1330,55 @@
     copy.wait()
     small_out[base : base + 1, :] = gx_recv[0:1, :] + jnp.sum(gsum[pl.ds(0, 8), my_quarter], axis=0, keepdims=True)
     small_out[base + 1 : base + 2, :] = gx_recv[1:2, :] + jnp.sum(gsum[pl.ds(8, 8), my_quarter], axis=0, keepdims=True)
+    stage = [local(la_hbm, rows)]
     small_step(0)
-    pass_end()
-    stage = [
-        local(la_hbm, rows),
-        local(lm_hbm, ar_full.at[pl.ds(0, p0), :]),
-        local(ra_hbm, qkv),
-        local(mx_hbm, dmix),
-    ]
+    pass_on(gifts_a)
+    a_second(1)
+    share_qkv(0, own)
+    b_second(0)
+    b_second(1)
+    a_first(2)
+    a_third(0, 0)
+    pass_on(gifts_b)
+    stage.append(local(ra_hbm.at[pl.ds(s0, own), :], qkv.at[pl.ds(s0, own), :]))
+    a_first(3)
     for copy in stage:
         copy.wait()
 
-    lead = 3
-
-    def turn(it, lag, count, stage):
-        @pl.when((it >= lag) & (it < lag + count))
+    def turn(it, lag, first, count, stage):
+        @pl.when((it >= first + lag) & (it < lag + count))
         def _():
             stage(it - lag)
 
-    turns = max(tiles_a + nh + 3, tiles_b + nh + 4)
+    turns = max(tiles_a + 2 * nh + 2, tiles_b + 2 * nh + 1)
 
     @pl.loop(0, turns)
     def _(it):
-        @pl.when(it < tiles_a - lead)
-        def _():
-            a_first(it + lead)
-
-        turn(it, 0, tiles_b, b_first)
-        turn(it, 0, tiles_a, a_second)
-        turn(it, 2, tiles_b, b_second)
+        turn(it, -4, 4, tiles_a, a_first)
+        turn(it, -2, 2, tiles_b, b_first)
+        turn(it, -2, 2, tiles_a, a_second)
+        turn(it, -1, 2, tiles_b, b_second)
         for k in range(nh):
-            turn(it, k + 1, tiles_a, functools.partial(a_third, k))
-        turn(it, nh + 1, tiles_a, a_fourth)
-        turn(it, nh + 2, tiles_a, a_fifth)
+            turn(it, 2 * k, 0 if k else 1, tiles_a, functools.partial(a_third, k))
+        turn(it, 2 * nh, 0, tiles_a, a_fourth)
+        turn(it, 2 * nh + 2, 0, tiles_a, a_fifth)
         for k in range(nh):
-            turn(it, k + 3, tiles_b, functools.partial(b_third, k))
-        turn(it, nh + 3, tiles_b, b_fourth)
+            turn(it, 1 + 2 * k, 0, tiles_b, functools.partial(b_third, k))
+        turn(it, 1 + 2 * nh, 0, tiles_b, b_fourth)
         for k in range(1, len(small_partners) + 1):
 
-            @pl.when(it == 2 * k)
+            @pl.when(it == 2 * k - 1)
             def _():
                 small_step(k)
 
     @pl.loop(0, tiles_a)
     def _(i):
-        for copy in outs_a(i):
+        for copy in outs_a(i, range(4)):
             copy.wait()
 
     @pl.loop(0, tiles_b)
     def _(i):
-        for copy in outs_b(i):
+        for copy in outs_b(i, range(2)):
             copy.wait()
 
 def chain(count, emb, dsum, feat_vecs, bq, bv, bu, hid, dhid, wq, wk, wv, wo, wu, wd):
@@ -1393,8 +1435,8 @@
         vm((slots + 16, quarter), F32),
         vm((bits + 1, slots + 16, quarter), F32),
         dma((6,)),
-        dma((16,)),
-        dma((128, 2)),
+        dma((24,)),
+        dma((192, 2)),
         pltpu.SemaphoreType.REGULAR((3 + nh,)),
         dma((ta, 2)),
         dma((nh, ta, 2)),
@@ -1435,8 +1477,9 @@
 
 def place_kernel(hid, sums, gin, small, w, hid_o, sum_o, gin_o, emb_o, vec_o, bup_o, q_o, k_o, v_o, o_o, u_o, d_o):
     hid_o[0] = hid[...]
-    used = sum_o.shape[2]
-    sum_o[0] = sums[:, :used, :]
+    used = sum_o.shape[0]
+    for seg in range(2):
+        sum_o[:, seg, :] = sums[seg, :used, :]
     gin_o[0] = gin[...]
     quarter = small.shape[2]
     base = small.shape[1] - 16
@@ -1467,7 +1510,7 @@
         name="place",
         out_shape=(
             sds((1, 2, toks, half), BF),
-            sds((1, 2, used, half), BF),
+            sds((used, 2, half), BF),
             sds((1, 2, toks, half), F32),
             sds((used, half), F32),
             [sds((half,), F32)] * 8,
@@ -1481,7 +1524,7 @@
         ),
         in_specs=[vmem] * 5,
         out_specs=(vmem,) * 4 + ([vmem] * 8,) + (vmem,) * 7,
-        compiler_params=pltpu.CompilerParams(vmem_limit_bytes=32 * 2**20),
+        compiler_params=pltpu.CompilerParams(vmem_limit_bytes=60 * 2**20),
     )(hid, sums, gin, small, w)
 
 
@@ -1490,13 +1533,13 @@
     b_value, w_out, b_out, ln2_gain, ln2_bias, w_up, b_up, w_down, b_down, d_hidden, d_summary,
 ):
     got = chain(
-        summary_counts, summary_embed, d_summary,
+        summary_counts, summary_embed, d_summary[0].transpose(1, 0, 2),
         [ln1_gain, ln1_bias, ln2_gain, ln2_bias, b_out, b_down], b_query, b_value, b_up,
         hidden_in[0], d_hidden[0], w_query, w_key, w_value, w_out, w_up, w_down,
     )
     hid, sums, gin, emb, vecs, bup, gq, gk, gv, go, gu, gd = place(*got[:5], summary_embed.shape[0])
     return (
-        hid, sums, gin, emb, vecs[0], vecs[1], gq, vecs[6], gk, gv,
+        hid, sums.transpose(1, 0, 2)[None], gin, emb, vecs[0], vecs[1], gq, vecs[6], gk, gv,
         vecs[7], go, vecs[2], vecs[3], vecs[4], gu, bup, gd, vecs[5],
     )
 

time: 342 us -> 287 us (0.84)
  Pallas kernels: 332 us -> 286 us
  local copies, waits for them, and re-layouts: 8.35 us -> 0 us
    pallas_call x1, Pallas kernels: 328 us -> 280 us  [chain(): pl.pallas_call(functools.partial(chain_kernel, bits), name='layer', out_s...]
    unnamed x12 -> x0, local copies, waits for them, and re-layouts: 8.35 us -> none
where the time goes in v4:
time: 287 us
  Pallas kernels  286 us (100%)
    pallas_call x1, Pallas kernels, chain(): pl.pallas_call(functools.partial(chain_kernel, bits), name='layer', out_s...  280 us
    pallas_call x1, Pallas kernels, place(): pl.pallas_call(place_kernel, name='place', out_shape=(sds((1, 2, toks, ha...  5.8 us

profile of v4, /device:TPU:0, one launch (start us, length us, event | category | flops | bytes accessed | tf_op | source)
XLA Modules:
  0.0 287.1 jit_solution(7121501250134268177)
XLA Ops:
  1.3 279.8 %layer.1 = (bf16[2,64,1024]{2,1,0:T(8,128)(2,1)}, bf16[2,64,1024]{2,1,0:T(8,128)(2,1)}, f32[2,64,1024]{2,1,0:T(8,128)}, f32[2,80,512]{2,1,0:T(8,128)}, bf16[128,...) custom-call(s32[1]{0:T(128)S(6)} %copy.39.count_ref, ...), custom_call_target="tpu_custom_call" | custom-call | tf_op jit(solution)/shard_map/layer/pallas_call | solution.py:1455
  281.2 5.8 %place.1 = (bf16[1,2,64,1024]{3,2,1,0:T(8,128)(2,1)}, bf16[50,2,1024]{2,1,0:T(2,128)(2,1)}, f32[1,2,64,1024]{3,2,1,0:T(8,128)}, f32[50,1024]{1,0:T(8,128)}, f32[...) custom-call(bf16[2,64,1024]{2,1,0:T(8,128)(2,1)} %get-tuple-element., ...), custom_call_target="tpu_custom_call" | custom-call | tf_op jit(solution)/shard_map/place/pallas_call | solution.py:1508

commit v5 on v4

--- a/solution.py
+++ b/solution.py
@@ -31,248 +31,6 @@
 
 def dot_tn(a, b):
     return lax.dot_general(a, b, (((0,), (0,)), ((), ())), preferred_element_type=F32)
-
-
-def dot_nt(a, b):
-    return lax.dot_general(a, b, (((1,), (1,)), ((), ())), preferred_element_type=F32)
-
-
-def dot_tn(a, b):
-    return lax.dot_general(a, b, (((0,), (0,)), ((), ())), preferred_element_type=F32)
-
-
-def grads_kernel(
-    bits,
-    tiles,
-    width,
-    la_ref,
-    lx_ref,
-    ra_ref,
-    rb_ref,
-    small_ref,
-    gq_ref,
-    gk_ref,
-    gv_ref,
-    go_ref,
-    gu_ref,
-    gd_ref,
-    emb_ref,
-    vec_refs,
-    bup_ref,
-    send0,
-    recv0,
-    keep0,
-    both,
-    sends,
-    recvs,
-    keeps,
-    send_p,
-    recv_p,
-    keep_p,
-    send_x,
-    recv_x,
-    small_cur,
-    small_recv,
-    sem0,
-    sems,
-    sem_p,
-    sem_x,
-    sem_s,
-):
-    b, s, t = lax.axis_index("batch"), lax.axis_index("seq"), lax.axis_index("tensor")
-    halving = list(range(bits - 1, PAIR_BIT, -1))
-    at_y = (flip(b, 0), s, t)
-    at_p = (flip(b, PAIR_BIT), s, t)
-    at_x = (b, 1 - s, t)
-    at_h = [(flip(b, bit), s, t) for bit in halving]
-    partners = [at_y, at_p, at_x] + at_h
-    barrier = pltpu.get_barrier_semaphore()
-    for partner in partners:
-        pl.semaphore_signal(barrier, inc=1, device_id=partner, device_id_type=MESH)
-    pl.semaphore_wait(barrier, len(partners))
-
-    features = la_ref.shape[1]
-    inner = ra_ref.shape[1] // width
-    chunk = features // (1 << bits)
-    half_count = 1 << (bits - 1)
-    mine = bit_of(b, 0)
-
-    def remote(src, dst, sem, partner):
-        return pltpu.make_async_remote_copy(
-            src_ref=src,
-            dst_ref=dst,
-            send_sem=sem.at[0],
-            recv_sem=sem.at[1],
-            device_id=partner,
-            device_id_type=MESH,
-        )
-
-    def copy_y(i):
-        return remote(send0.at[i], recv0.at[i], sem0.at[i], at_y)
-
-    def copy_h(k, i):
-        return remote(sends[k].at[i], recvs[k].at[i], sems[k].at[i], at_h[k])
-
-    def copy_p(i):
-        return remote(send_p.at[i], recv_p.at[i], sem_p.at[i], at_p)
-
-    def copy_x(i):
-        return remote(send_x.at[i], recv_x.at[i], sem_x.at[i], at_x)
-
-    per = (tiles - inner - 1) // 2
-
-    def product(i, side, put):
-        def blocks(left, right):
-            @pl.loop(0, half_count)
-            def _(j):
-                at = pl.ds(pl.multiple_of(j * chunk, chunk), chunk)
-                if chunk % 128 == 0:
-                    start = pl.multiple_of((2 * j + side) * chunk, chunk)
-                    put(at, dot_tn(left(pl.ds(start, chunk)), right))
-                else:
-                    start = pl.multiple_of(2 * j * chunk, 2 * chunk)
-                    both[...] = dot_tn(left(pl.ds(start, 2 * chunk)), right)
-                    put(at, both[pl.ds(pl.multiple_of(side * chunk, chunk), chunk), :])
-
-        @pl.when(i < inner)
-        def _():
-            cols = pl.ds(pl.multiple_of(i * width, width), width)
-            blocks(lambda at: la_ref[:, at], ra_ref[:, cols])
-
-        @pl.when(i >= inner)
-        def _():
-            k = i - inner
-            cols = pl.ds(pl.multiple_of(k * width, width), width)
-            op = (k + per - 1) // per
-            blocks(lambda at: lx_ref[op, :, at], rb_ref[:, cols])
-
-    small_cur[...] = small_ref[...]
-    small_partners = [at_y] + at_h + [at_p]
-    for k, partner in enumerate(small_partners):
-        copy = remote(small_cur, small_recv.at[k], sem_s.at[k], partner)
-        copy.start()
-
-        if k == 0:
-
-            @pl.loop(0, tiles)
-            def _(i):
-                def put(at, value):
-                    send0[i, at, :] = value.astype(BF)
-
-                product(i, 1 - mine, put)
-                copy_y(i).start()
-
-        copy.wait()
-        small_cur[...] = small_cur[...] + small_recv[k]
-    last = len(small_partners)
-    copy = remote(small_cur, small_recv.at[last], sem_s.at[last], at_x)
-    copy.start()
-    copy.wait()
-    used = emb_ref.shape[0]
-    quarter = small_ref.shape[1]
-    base = small_ref.shape[0] - 16
-    for side, ref in ((s, small_cur), (1 - s, small_recv.at[last])):
-        at = pl.ds(pl.multiple_of(side * quarter, quarter), quarter)
-        emb_ref[:, at] = ref[pl.ds(0, used), :]
-        for k, out in enumerate(vec_refs):
-            out[:, at] = ref[base + k : base + k + 1, :]
-        pieces = bup_ref.shape[1] // (2 * quarter)
-        for k in range(pieces):
-            at = pl.ds(pl.multiple_of((side * pieces + k) * quarter, quarter), quarter)
-            bup_ref[:, at] = ref[base + 8 + k : base + 9 + k, :]
-
-    stages = len(halving)
-
-    def split(i, k, total, rows):
-        bit = bit_of(b, halving[k])
-        half = rows // 2
-        keeps[k][i] = total(pl.multiple_of(bit * half, half), half)
-        sends[k][i] = total(pl.multiple_of((1 - bit) * half, half), half).astype(BF)
-        copy_h(k, i).start()
-
-    def stage_first(i):
-        copy_y(i).wait()
-
-        def put(at, value):
-            keep0[at, :] = value + recv0[i, at, :].astype(F32)
-
-        product(i, mine, put)
-        split(i, 0, lambda at, n: keep0[pl.ds(at, n), :], half_count * chunk)
-
-    def stage_next(k, i):
-        copy_h(k, i).wait()
-
-        def total(at, n):
-            return keeps[k][i, pl.ds(at, n), :] + recvs[k][i, pl.ds(at, n), :].astype(F32)
-
-        rows = (half_count * chunk) >> (k + 1)
-        if k + 1 < stages:
-            split(i, k + 1, total, rows)
-        else:
-            bit = bit_of(b, PAIR_BIT)
-            keep_p[i] = total(pl.multiple_of(bit * chunk, chunk), chunk)
-            send_p[i] = total(pl.multiple_of((1 - bit) * chunk, chunk), chunk).astype(BF)
-            copy_p(i).start()
-
-    def write(i, side, pair, value):
-        spot = pl.ds(pl.multiple_of((2 * side + pair) * width, width), width)
-        for k, ref in enumerate((gq_ref, gk_ref, gv_ref)):
-
-            @pl.when(i == k)
-            def _():
-                ref[:, spot] = value
-
-        @pl.when(i == inner)
-        def _():
-            go_ref[spot, :] = value.T
-
-        def unit(k):
-            return pl.ds(pl.multiple_of(((2 * side + pair) * per + k) * width, width), width)
-
-        @pl.when((i > inner) & (i <= inner + per))
-        def _():
-            gu_ref[:, unit(i - inner - 1)] = value
-
-        @pl.when(i > inner + per)
-        def _():
-            gd_ref[unit(i - inner - 1 - per), :] = value.T
-
-    def stage_pair(i):
-        copy_p(i).wait()
-        bit = bit_of(b, PAIR_BIT)
-        half = chunk // 2
-        mine_at = pl.multiple_of(s * half, half)
-        other_at = pl.multiple_of((1 - s) * half, half)
-        write(i, s, bit, keep_p[i, pl.ds(mine_at, half), :])
-        write(i, s, 1 - bit, recv_p[i, pl.ds(mine_at, half), :].astype(F32))
-        send_x[i, bit] = keep_p[i, pl.ds(other_at, half), :].astype(BF)
-        send_x[i, 1 - bit] = recv_p[i, pl.ds(other_at, half), :]
-        copy_x(i).start()
-
-    def stage_last(i):
-        copy_x(i).wait()
-        for pair in range(2):
-            write(i, 1 - s, pair, recv_x[i, pair].astype(F32))
-
-    @pl.loop(0, tiles + stages + 2)
-    def _(i):
-        @pl.when(i < tiles)
-        def _():
-            stage_first(i)
-
-        for k in range(stages):
-
-            @pl.when((i >= k + 1) & (i < tiles + k + 1))
-            def _():
-                stage_next(k, i - (k + 1))
-
-        @pl.when((i >= stages + 1) & (i < tiles + stages + 1))
-        def _():
-            stage_pair(i - (stages + 1))
-
-        @pl.when(i >= stages + 2)
-        def _():
-            stage_last(i - (stages + 2))
 
 
 class Strips:
@@ -293,6 +51,7 @@
             if len(run) == need and all(r[0] is ref and r[3] == 0 for r in run):
                 for r in run:
                     r[3] = height
+                run[-1][3] = (tiles - per * (need - 1)) * n
                 return Slab(ref, at, 0, per, n, unit, self.width)
         raise ValueError("no room")
 
@@ -330,13 +89,16 @@
     wd_hbm,
     hid_out,
     sum_out,
-    gin_out,
+    gin_hbm,
     small_final,
     w_hbm,
     la_hbm,
     lm_hbm,
     ra_hbm,
     mx_hbm,
+    ye_hbm,
+    ls_hbm,
+    rs_hbm,
     wqkv,
     wo,
     wu,
@@ -373,7 +135,6 @@
     rbx,
     both,
     small_out,
-    small_recv,
     wsem,
     lsem,
     rsem,
@@ -388,6 +149,7 @@
     sem_oa,
     sem_ob,
     sem_s,
+    early,
 ):
     b, s, t = lax.axis_index("batch"), lax.axis_index("seq"), lax.axis_index("tensor")
     at_core = (b, s, 1 - t)
@@ -397,6 +159,9 @@
     halving = list(range(bits - 1, PAIR_BIT, -1))
     at_h = [(flip(b, bit), s, t) for bit in halving]
     zl, y = bit_of(b, PAIR_BIT), bit_of(b, 0)
+    halving_down = list(range(bits - 2, 0, -1))
+    at_d = (flip(b, bits - 1), s, t)
+    zd = bit_of(b, bits - 1)
     barrier = pltpu.get_barrier_semaphore()
     partners = [at_core, at_x, at_p, at_y] + at_h
     for partner in partners:
@@ -628,9 +393,11 @@
             for copy in self.backs:
                 copy.wait()
 
-        def flow(self, body):
+        def flow(self, body, before_last=lambda: None):
             self.backs = []
             for k, ((base, n, _), copy) in enumerate(zip(self.pieces, self.xs)):
+                if k == len(self.pieces) - 1:
+                    before_last()
                 copy.wait()
                 block = ar_full.at[pl.ds(self.full + base, n), my_cols]
                 block[...] = self.sums(base, n, False).astype(BF)
@@ -791,20 +558,24 @@
 
     def share_feats_a(op, src, at, n):
         landing = lxx.at[op, pl.ds(at, n), my_cols]
-        gifts_a.append((remote(src.at[pl.ds(at, n), my_cols], landing, at_p), landing))
-
-    def share_units_a(src, col, at, n):
-        its = pl.ds(pl.multiple_of((1 - zl) * hu, hu), hu)
-        landing = rbx.at[pl.ds(at, n), pl.ds(col, hu)]
-        gifts_a.append((remote(src.at[pl.ds(at, n), its], landing, at_p), None))
+        partner = at_d if op else at_p
+        gifts_a.append((remote(src.at[pl.ds(at, n), my_cols], landing, partner), landing))
+
+    def share_units_a(op, src, at, n):
+        side = zd if op else zl
+        its = pl.ds(pl.multiple_of((1 - side) * hu, hu), hu)
+        landing = rbx.at[pl.ds(at, n), pl.ds(op * hu, hu)]
+        partner = at_d if op else at_p
+        gifts_a.append((remote(src.at[pl.ds(at, n), its], landing, partner), None))
+
+    y_blocks = [(my_cols, my_cols)]
+    if chunk % 128 == 0:
+        block = lambda c: pl.ds(pl.multiple_of(c * chunk, chunk), chunk)
+        y_blocks = [2 * (t * chunks // 2 + m) for m in range(chunks // 2)]
+        y_blocks = [(block(c + 1 - y), block(c + y)) for c in y_blocks]
 
     def share_feats_b(src, dst, at, n):
-        some = [(my_cols, my_cols)]
-        if chunk % 128 == 0:
-            block = lambda c: pl.ds(pl.multiple_of(c * chunk, chunk), chunk)
-            some = [2 * (t * chunks // 2 + m) for m in range(chunks // 2)]
-            some = [(block(c + 1 - y), block(c + y)) for c in some]
-        for out, back in some:
+        for out, back in y_blocks:
             copy = remote(src.at[pl.ds(at, n), out], dst.at[pl.ds(at, n), out], at_y)
             gifts_b.append((copy, dst.at[pl.ds(at, n), back]))
 
@@ -823,24 +594,44 @@
         while passed:
             passed.pop(0).wait()
 
-    share_qkv = lambda at, n: share_units_b(dqkv, ra_hbm, at, n)
+    def share_thin(src, dst, at, n, partner):
+        block = dst.at[pl.ds(at, n), my_quarter]
+        return remote(src.at[pl.ds(at, n), my_quarter], block, partner)
+
+    gifts_q, thin_act1, thin_act2 = [], [], []
+    hq = nq // 2
+
+    def share_qkv(at, n):
+        for g in range(3):
+            its = pl.ds(pl.multiple_of(g * nq + (1 - zl) * hq, hq), hq)
+            landing = ra_hbm.at[pl.ds(at, n), pl.ds(g * hq, hq)]
+            gifts_q.append(remote(dqkv.at[pl.ds(at, n), its], landing, at_p))
+
     share_mix = lambda at, n: share_units_b(mix, mx_hbm, at, n)
-    share_actv = lambda at, n: share_units_a(actv, 0, at, n)
-    share_db = lambda at, n: share_units_a(db, hu, at, n)
+    share_actv = lambda at, n: share_units_a(0, actv, at, n)
+    share_db = lambda at, n: share_units_a(1, db, at, n)
 
     width = nq // 2
     near = chunk // 2
     per = hu // width
-    tiles_a, tiles_b = 2 * per, 4 * nq // width
+    tiles_a, tiles_b = 2 * per + 3, nq // width
+    assert per == 4 and hq == width
+
+    def kind_of(i):
+        later = (i // per + 1) // 2
+        return 1 - later, later * (i % 2), (1 - later) * i + later * ((i - per) // 2)
+
+
     nh = len(halving)
     strips = Strips([wu, wd], width)
     recv_y = strips.take(tiles_a, chunks * chunk, near)
-    send_y = strips.take(tiles_a, chunks * chunk, near)
+    slots_y = 4
+    send_y = strips.take(slots_y, chunks * chunk, near)
     recv_za = [strips.take(tiles_a, chunks * chunk >> (k + 1), near) for k in range(nh)]
     recv_pb = strips.take(tiles_b, chunks * chunk // 2, near)
     recv_zb = [strips.take(tiles_b, chunks * chunk >> (k + 2), near) for k in range(nh)]
-    recv_pa = strips.take(tiles_a, chunk, near)
-    recv_xa = strips.take(tiles_a, chunk, near)
+    recv_px = strips.take(tiles_a, 2 * chunk, near)
+    send_zd = strips.take(per, chunks * chunk // 2, near)
     recv_xb = strips.take(tiles_b, near, near)
     strips = Strips([wqkv, wo], width)
     send_za = [strips.take(tiles_a, chunks * chunk >> (k + 1), near) for k in range(nh)]
@@ -858,99 +649,142 @@
             device_id_type=MESH,
         )
 
-    copy_y = lambda i: linked(send_y(i), recv_y(i), sem_y.at[i], at_y)
-    copy_za = lambda k, i: linked(send_za[k](i), recv_za[k](i), sem_za.at[k, i], at_h[k])
-    copy_pa = lambda i: linked(send_pa(i), recv_pa(i), sem_pa.at[i], at_p)
+    copy_y = lambda i: linked(send_y(i % slots_y), recv_y(i), sem_y.at[i], at_y)
+    def by_kind(i, far, close):
+        down, inner, _ = kind_of(i)
+        return close + (1 - down - inner) * (far - close)
+
+    def copy_za(k, i, down=False):
+        to = by_kind(i, flip(b, halving_down[k]), flip(b, halving[k]))
+        src = send_zd if down else send_za[k]
+        return linked(src(i), recv_za[k](i), sem_za.at[k, i], (to, s, t))
+
+    def copy_pa(i):
+        to = by_kind(i, at_d[0], at_p[0])
+        return linked(send_pa(i), recv_px.at(i, 0, chunk), sem_pa.at[i], (to, s, t))
+
+    def place_bit(j, k, value):
+        low = 1 << k
+        return (j // low) * 2 * low + value * low + j % low
+
     copy_pb = lambda i: linked(send_pb(i), recv_pb(i), sem_pb.at[i], at_p)
     copy_zb = lambda k, i: linked(send_zb[k](i), recv_zb[k](i), sem_zb.at[k, i], at_h[k])
 
-    def block_product(l1, l2, r1, r2, c):
+    def block_product(lefts, rights, c):
         def dots(cols):
-            return dot_tn(l1(cols), r1) + dot_tn(l2(cols), r2)
+            x = dot_tn(lefts[0](cols), rights[0])
+            for left, right in zip(lefts[1:], rights[1:]):
+                x = x + dot_tn(left(cols), right)
+            return x
 
         if chunk % 128 == 0:
             return dots(pl.ds(pl.multiple_of(c * chunk, chunk), chunk))
         both[...] = dots(pl.ds(pl.multiple_of((c // 2) * 2 * chunk, 2 * chunk), 2 * chunk))
         return both[pl.ds(pl.multiple_of((c % 2) * chunk, chunk), chunk), :]
 
-    def products_a(i, parts):
-        for op, (left, right) in enumerate(((gd, actv), (act2, db))):
-
-            @pl.when(i // per == op)
+    main = p0
+
+    def products_a(i, parts, early=False):
+        down, inner, k = kind_of(i)
+        tile = lambda c: pl.ds(pl.multiple_of(c, width), width)
+        cases = (
+            (gd, lxx.at[0], actv, zl * hu + k * width, rbx, k * width),
+            (act2, lxx.at[1], db, zd * hu + k * width, rbx, hu + k * width),
+            (act1, rows, dqkv, k * nq + zl * hq, qkv, k * width),
+        )
+        for op, (near_l, far_l, near_r, near_at, far_r, far_at) in enumerate(cases):
+
+            @pl.when((1 - down) * (1 + inner) == op)
             def _():
-                mine = pl.ds(pl.multiple_of(zl * hu + (i - op * per) * width, width), width)
-                its = pl.ds(pl.multiple_of(i * width, width), width)
-                r1, r2 = right[:, mine], rbx[:, its]
-                for n, which, put, after in parts:
+                at = pl.ds(slots, main - slots) if early and op == 0 else slice(None)
+                rights = [near_r[at, tile(near_at)], far_r[at, tile(far_at)]]
+                lefts = [lambda cols: near_l[at, cols], lambda cols: far_l[at, cols]]
+                if op == 0 and not early:
+                    rights.append(ar_own[pl.ds(0, 2 * slots), tile(k * width)])
+                    lefts.append(lambda cols: dsum[:, cols])
+                for n, which, put, after in parts(op):
 
                     @pl.loop(0, n)
                     def _(j):
-                        l2 = lambda cols: lxx[op, :, cols]
-                        put(j, block_product(lambda cols: left[:, cols], l2, r1, r2, which(j)))
+                        put(j, block_product(lefts, rights, which(j)))
 
                     after()
 
     def products_b(i, parts):
-        groups = nq // width
-        for op in range(2):
-
-            @pl.when(jnp.minimum(i // groups, 1) == op)
-            def _():
-                cols = pl.ds(pl.multiple_of((i - op * groups) * width, width), width)
-                r1, r2 = (dqkv[:, cols], qkv[:, cols]) if op else (mix[:, cols], dmix[:, cols])
-                l1 = (lambda at: act1[:, at]) if op else (lambda at: gm[:, at])
-                l2 = (lambda at: rows[:, at]) if op else (lambda at: ar_full[pl.ds(0, p0), at])
-                for n, which, put, after in parts:
-
-                    @pl.loop(0, n)
-                    def _(j):
-                        put(j, block_product(l1, l2, r1, r2, which(j)))
-
-                    after()
-
-    def rows_at(slab, i, lo, n):
-        return slab.at(i, lo, n)
+        cols = pl.ds(pl.multiple_of(i * width, width), width)
+        r1, r2 = mix[:, cols], dmix[:, cols]
+        l1, l2 = (lambda at: gm[:, at]), (lambda at: ar_full[pl.ds(0, p0), at])
+        for n, which, put, after in parts:
+
+            @pl.loop(0, n)
+            def _(j):
+                put(j, block_product((l1, l2), (r1, r2), which(j)))
+
+            after()
+
+    def copy_early(i):
+        return linked(early.at[i % 2], ye_hbm.at[i], sem_y.at[i], at_y)
+
+    def a_early(i):
+        def put(j, v):
+            early[i % 2, pl.ds(pl.multiple_of(j * chunk, chunk), chunk), :] = v.astype(BF)
+
+        if i >= 2:
+            copy_early(i - 2).wait_send()
+        part = (chunks, lambda j: 2 * j + 1 - y, put, lambda: copy_early(i).start())
+        products_a(i, lambda op: [part], True)
+
+    def early_in(i):
+        if i >= 2:
+            copy_early(i).wait_send()
+        copy_early(i).wait_recv()
+        return local(ye_hbm.at[i], recv_y(i))
 
     def a_first(i):
         def put(j, v):
-            send_y.at(i, j * chunk, chunk)[...] = v.astype(BF)
-
-        products_a(i, [(chunks, lambda j: 2 * j + 1 - y, put, lambda: copy_y(i).start())])
-
-    def a_second(i):
-        copy_y(i).wait()
-        bit = bit_of(b, halving[0])
+            send_y.at(i % slots_y, j * chunk, chunk)[...] = v.astype(BF)
+
+        part = (chunks, lambda j: 2 * j + 1 - y, put, lambda: copy_y(i).start())
+        products_a(i, lambda op: [part])
+
+    def a_second(i, came=None):
+        (copy_y(i) if came is None else came).wait()
         n = chunks // 2
 
-        def total(j, v, at):
-            return (v + recv_y.at(i, at * chunk, chunk)[...].astype(F32)).astype(BF)
-
-        def give(j, v):
-            send_za[0].at(i, j * chunk, chunk)[...] = total(j, v, (1 - bit) * n + j)
-
-        def keep(j, v):
-            x = total(j, v, bit * n + j)
-            recv_y.at(i, j * chunk, chunk)[...] = x
-
-        products_a(
-            i,
-            [
-                (n, lambda j: 2 * ((1 - bit) * n + j) + y, give, lambda: copy_za(0, i).start()),
-                (n, lambda j: 2 * (bit * n + j) + y, keep, lambda: None),
-            ],
-        )
-
-    def halve(i, k, kept, at, recv, n, give, copy, start):
+        def parts(op):
+            bit = bit_of(b, (halving_down if op == 1 else halving)[0])
+            k = bits - 3 if op == 1 else bits - 2
+            other = lambda j: place_bit(j, k, 1 - bit)
+            mine = lambda j: place_bit(j, k, bit)
+
+            def total(v, at):
+                return (v + recv_y.at(i, at * chunk, chunk)[...].astype(F32)).astype(BF)
+
+            def give(j, v):
+                give_to = send_za[0] if op else send_zd
+                give_to.at(i, j * chunk, chunk)[...] = total(v, other(j))
+
+            def keep(j, v):
+                x = total(v, mine(j))
+                recv_y.at(i, j * chunk, chunk)[...] = x
+
+            return [
+                (n, lambda j: 2 * other(j) + y, give, lambda: copy_za(0, i, op == 0).start()),
+                (n, lambda j: 2 * mine(j) + y, keep, lambda: None),
+            ]
+
+        products_a(i, parts)
+
+    def halve(i, kept, at, recv, n, give, copy, k, bit):
         def total(c):
             x = kept.at(i, (at + c) * chunk, chunk)[...].astype(F32)
             return (x + recv.at(i, c * chunk, chunk)[...].astype(F32)).astype(BF)
 
-        bit = start
         for j in range(n // 2):
-            give.at(i, j * chunk, chunk)[...] = total((1 - bit) * (n // 2) + j)
+            give.at(i, j * chunk, chunk)[...] = total(place_bit(j, k, 1 - bit))
         copy().start()
         for j in range(n // 2):
-            x = total(bit * (n // 2) + j)
+            x = total(place_bit(j, k, bit))
             kept.at(i, (at + n + j) * chunk, chunk)[...] = x
 
     ends_a = [0]
@@ -960,22 +794,30 @@
     def a_third(k, i):
         copy_za(k, i).wait()
         n = chunks >> (k + 1)
-        if k + 1 < nh:
-            bit = bit_of(b, halving[k + 1])
-            halve(i, k, recv_y, ends_a[k], recv_za[k], n, send_za[k + 1], lambda: copy_za(k + 1, i), bit)
-        else:
-            halve(i, k, recv_y, ends_a[k], recv_za[k], n, send_pa, lambda: copy_pa(i), zl)
+        if k + 1 == nh:
+            side = by_kind(i, zd, zl)
+            halve(i, recv_y, ends_a[k], recv_za[k], n, send_pa, lambda: copy_pa(i), 0, side)
+            return
+        for op in range(2):
+
+            @pl.when(by_kind(i, 1, 0) == op)
+            def _():
+                bit = bit_of(b, (halving_down if op else halving)[k + 1])
+                at = bits - 4 - k if op else bits - 3 - k
+                after = lambda: copy_za(k + 1, i)
+                halve(i, recv_y, ends_a[k], recv_za[k], n, send_za[k + 1], after, at, bit)
 
     my_near = pl.multiple_of(s * near, near)
     its_near = pl.multiple_of((1 - s) * near, near)
     kept_a = lambda i, at: recv_y.at(i, ends_a[nh] * chunk + at, near)
 
     def copies_xa(i):
+        side = by_kind(i, zd, zl)
         return [
-            linked(kept_a(i, its_near), recv_xa.at(i, zl * near, near), sem_xa.at[i, 0], at_x),
+            linked(kept_a(i, its_near), recv_px.at(i, chunk + side * near, near), sem_xa.at[i, 0], at_x),
             linked(
-                recv_pa.at(i, its_near, near),
-                recv_xa.at(i, (1 - zl) * near, near),
+                recv_px.at(i, its_near, near),
+                recv_px.at(i, chunk + (1 - side) * near, near),
                 sem_xa.at[i, 1],
                 at_x,
             ),
@@ -983,14 +825,16 @@
 
     def outs_a(i, picks):
         def to(side, pair):
-            col = 8 * nq + (1 - i // per) * 2 * nu + side * nu + pair * hu + (i % per) * width
+            down, inner, k = kind_of(i)
+            ffn_col = 8 * nq + down * 2 * nu + side * nu + pair * hu + k * width
+            col = (1 - inner) * ffn_col + inner * (k * 2 * nq + side * nq + pair * hq)
             return w_hbm.at[:, pl.ds(pl.multiple_of(col, width), width)]
 
         pieces = [
-            (kept_a(i, my_near), to(s, zl)),
-            (recv_pa.at(i, my_near, near), to(s, 1 - zl)),
-            (recv_xa.at(i, 0, near), to(1 - s, 0)),
-            (recv_xa.at(i, near, near), to(1 - s, 1)),
+            (kept_a(i, my_near), to(s, by_kind(i, zd, zl))),
+            (recv_px.at(i, my_near, near), to(s, 1 - by_kind(i, zd, zl))),
+            (recv_px.at(i, chunk, near), to(1 - s, 0)),
+            (recv_px.at(i, chunk + near, near), to(1 - s, 1)),
         ]
         return [pltpu.make_async_copy(*pieces[k], sem_oa.at[i, k]) for k in picks]
 
@@ -1046,9 +890,7 @@
 
     def outs_b(i, picks):
         def to(side):
-            groups = nq // width
-            op = (i // groups + 3) % 4
-            col = op * 2 * nq + side * nq + (i % groups) * width
+            col = 6 * nq + side * nq + i * width
             return w_hbm.at[:, pl.ds(pl.multiple_of(col, width), width)]
 
         pieces = [(kept_b(i, my_near), to(s)), (recv_xb(i), to(1 - s))]
@@ -1059,7 +901,8 @@
         n = chunks >> (k + 2)
         if k + 1 < nh:
             bit = bit_of(b, halving[k + 1])
-            halve(i, k, recv_pb, ends_b[k], recv_zb[k], n, send_zb[k + 1], lambda: copy_zb(k + 1, i), bit)
+            after = lambda: copy_zb(k + 1, i)
+            halve(i, recv_pb, ends_b[k], recv_zb[k], n, send_zb[k + 1], after, bits - 4 - k, bit)
         else:
             x = recv_pb.at(i, ends_b[k] * chunk, chunk)[...].astype(F32) + recv_zb[k](i)[...].astype(F32)
             recv_pb.at(i, ends_b[nh] * chunk, chunk)[...] = x.astype(BF)
@@ -1072,17 +915,21 @@
 
     small_partners = [at_y] + at_h + [at_p, at_x]
 
+    def small_in(k):
+        at = pl.ds((k // 2) * small_out.shape[0], small_out.shape[0])
+        return outacc.at[at, pl.ds((k % 2) * quarter, quarter)]
+
     def small_step(k):
-        copy = lambda k: linked(small_out, small_recv.at[k], sem_s.at[k], small_partners[k])
+        copy = lambda k: linked(small_out, small_in(k), sem_s.at[k], small_partners[k])
         if k > 0:
             copy(k - 1).wait()
             if k < len(small_partners):
-                small_out[...] = small_out[...] + small_recv[k - 1]
+                small_out[...] = small_out[...] + small_in(k - 1)[...]
         if k < len(small_partners):
             copy(k).start()
         else:
             small_final[s] = small_out[...]
-            small_final[1 - s] = small_recv[k - 1]
+            small_final[1 - s] = small_in(k - 1)[...]
 
     for copy in firsts + from_core:
         copy.wait()
@@ -1094,7 +941,7 @@
     x_dhid = [in_x(dhid_hbm.at[0], gd, t0), in_x(dhid_hbm.at[1], gd, t1)]
     forward.wait()
     norm1(t0 + its_toks, toks)
-    share_feats_b(act1, la_hbm, 0, own)
+    thin_act1.append(share_thin(act1, la_hbm, 0, own, at_p))
     for copy in weights[:3]:
         copy.wait()
     project(0, own, 0, 3 * nq)
@@ -1115,7 +962,7 @@
         copy.wait()
     forward.wait()
     norm1(t1, own)
-    share_feats_b(act1, la_hbm, t1, own)
+    thin_act1.append(share_thin(act1, la_hbm, t1, own, at_p))
     project(t1, own, 0, 3 * nq)
     a1.finish()
     a1.done()
@@ -1137,7 +984,7 @@
     a3.middle()
     a2.done()
     enter_ffn(a2, t0, T)
-    outacc[0] = mid[pl.ds(t0 + my_toks, toks), my_cols]
+    outacc[pl.ds(0 * toks, toks), :] = mid[pl.ds(t0 + my_toks, toks), my_cols]
 
     def early_before(c):
         cols, r = pl.ds(c, wide), pl.ds(t1, own)
@@ -1145,7 +992,7 @@
 
     col_loop(nu, early_before)
     a3.finish()
-    share_feats_a(1, act2, s0, own)
+    thin_act2.append(share_thin(act2, lxx.at[1], s0, own, at_d))
     a3.done()
 
     def summary(i):
@@ -1159,7 +1006,7 @@
     pl.loop(0, slots // step)(summary)
     sum_out[0] = rows[pl.ds(p0, slots), my_cols]
     norm1(p0, slots)
-    share_feats_b(act1, la_hbm, p0, slots)
+    thin_act1.append(share_thin(act1, la_hbm, p0, slots, at_p))
     project(p0, slots, nq, 3 * nq)
     attend(1)
     share_mix(t1, own)
@@ -1169,7 +1016,8 @@
     a5.middle()
     ffn(t0, T, 1, nu // 4, nu)
     share_actv(s0, own)
-    share_db(t0, T)
+    side = pl.ds(pl.multiple_of(zl * hu, hu), hu)
+    rs_own = remote(actv.at[pl.ds(s0, slots), side], rs_hbm.at[pl.ds(0, slots), :], at_y)
     a6 = Total(T, 2 * slots, 2 * slots, whole(T))
     a6.start(up_back(t0, T))
     a6.middle()
@@ -1177,9 +1025,9 @@
     a4.start(down_product(t0, T))
     a5.flow(lambda base, n: enter_ffn(a5, t1, n, base))
     a4.middle()
-    outacc[1] = mid[pl.ds(t1 + my_toks, toks), my_cols]
-    outacc[2] = mid[pl.ds(s1, slots), my_cols]
-    share_feats_a(1, act2, t1, own)
+    outacc[pl.ds(1 * toks, toks), :] = mid[pl.ds(t1 + my_toks, toks), my_cols]
+    outacc[pl.ds(2 * toks, toks), :] = mid[pl.ds(s1, slots), my_cols]
+    pass_on(gifts_a, 1)
     ffn(t1, own, 2, 0, nu)
     share_actv(t1, own)
     a8 = Total(own, 2 * slots + T + own, 2 * slots + T + own, whole(own))
@@ -1192,27 +1040,35 @@
     leave_ffn(a6, t0, T)
     mix_back(t0, T)
     share_feats_b(gm, lm_hbm, t0, T)
-    a8.flow(lambda base, n: leave_ffn(a8, t1, n, base))
+
+    def begin_down():
+        pass_on(gifts_a)
+        pass_end()
+        a_early(0)
+        thin_act2.append(share_thin(act2, lxx.at[1], t1, own, at_d))
+        share_db(t0, T)
+        share_db(t1, own)
+
+    a8.flow(lambda base, n: leave_ffn(a8, t1, n, base), begin_down)
+    far = rbx.at[pl.ds(s0, slots), pl.ds(0, hu)]
+    rs_far = remote(far, rs_hbm.at[pl.ds(slots, slots), :], at_y)
     a7.middle()
     mix_back(t1, own)
     share_feats_b(gm, lm_hbm, t1, own)
-    early_b = len(gifts_b)
     attend_back(1)
-    share_qkv(t1, own + slots)
     a9 = Total(slots, 0, 0, whole(slots))
     a9.start(in_back(p0, slots, nq))
     a10 = Total(own, 2 * slots + T, 2 * slots + T, [(0, T, True), (T, slots, False)])
     a9.middle()
     a10.start(in_back(t1, own, 0))
-    pass_on(gifts_b, early_b)
     a9.finish()
     a10.middle()
     for copy in a4.xs + a7.xs:
         copy.wait()
-    hid_out[0] = (outacc[0] + a4.sums(0, T, True) + vec[5:6, my_cols]).astype(BF)
-    hid_out[1] = (outacc[1] + a7.sums(0, T, True) + vec[5:6, my_cols]).astype(BF)
+    hid_out[0] = (outacc[pl.ds(0 * toks, toks), :] + a4.sums(0, T, True) + vec[5:6, my_cols]).astype(BF)
+    hid_out[1] = (outacc[pl.ds(1 * toks, toks), :] + a7.sums(0, T, True) + vec[5:6, my_cols]).astype(BF)
     sum_out[1] = (
-        (outacc[2] + a7.sums(T, slots, False) + vec[5:6, my_cols]) * row_live
+        (outacc[pl.ds(2 * toks, toks), :] + a7.sums(T, slots, False) + vec[5:6, my_cols]) * row_live
     ).astype(BF)
     a9.done()
     first_only = (s == 0).astype(F32)
@@ -1233,9 +1089,13 @@
         gd[g, :] = ((dsum[pl.ds(pl.multiple_of(i * step, step), step), :].astype(F32) + d) * on).astype(BF)
 
     pl.loop(0, slots // step)(prefix_back)
+    before_gifts = len(gifts_a)
     share_feats_a(0, gd, s0, slots)
-    late_gifts = 1 + len(gifts_a)
-    share_db(t1, own)
+    late_gifts = gifts_a.pop(before_gifts)
+    ls_near = [
+        remote(gd.at[pl.ds(s0, slots), out], ls_hbm.at[pl.ds(0, slots), out], at_y)
+        for out, _ in y_blocks
+    ]
 
     def last_before(c):
         cols = pl.ds(c, wide)
@@ -1251,12 +1111,15 @@
         pl.semaphore_signal(free.at[k], inc=1, device_id=partner, device_id_type=MESH)
     a10.finish()
     a11.middle()
-    pass_on(gifts_a, late_gifts - 1)
+    late_gifts[0].wait()
+    share_qkv(t1, own + slots)
+    passed.append(remote(late_gifts[1], late_gifts[1], at_core))
+    ls_far = [
+        remote(lxx.at[0, pl.ds(s0, slots), out], ls_hbm.at[pl.ds(slots, slots), out], at_y)
+        for out, _ in y_blocks
+    ]
     a10.done()
-    pass_end()
-    for k in range(len(askers)):
-        pl.semaphore_wait(free.at[k], 1)
-    a_first(0)
+    gin_copies = []
 
     def rows_back(total, seg):
         t_at, s_at = (t0, s0) if seg == 0 else (t1, s1)
@@ -1269,7 +1132,7 @@
             mid[r, :] = mid[r, :] + x
 
         pl.loop(0, toks // step)(tokens)
-        gin_out[seg] = mid[pl.ds(t_at + my_toks, toks), my_cols]
+        gin_copies.append(local(mid.at[pl.ds(t_at + my_toks, toks), my_cols], gin_hbm.at[seg]))
 
         def summaries(i):
             r = pl.ds(pl.multiple_of(s_at + i * step, step), step)
@@ -1281,25 +1144,51 @@
         pl.loop(0, slots // step)(summaries)
 
     emb_wide = slope0
+    for copy in [rs_own, rs_far]:
+        copy.wait()
+    for copy in ls_near:
+        copy.wait()
+    for copy in ls_far:
+        copy.wait()
+    ls_core = remote(ls_hbm.at[:, my_cols], ls_hbm.at[:, my_cols], at_core)
+    rs_in = local(rs_hbm, ar_own.at[pl.ds(0, 2 * slots), :])
+    came = [early_in(0)]
+    a_early(1)
     rows_back(a10, 1)
+    pass_end()
+    ls_core.wait()
+    ls_in = local(ls_hbm, dsum)
     a11.finish()
+    for k in range(len(askers)):
+        pl.semaphore_wait(free.at[k], 1)
     a11.done()
+    rs_in.wait()
+    ls_in.wait()
+    a_second(0, came[0])
+    for copy in thin_act1:
+        copy.wait()
+    x_act1 = remote(la_hbm.at[:, my_quarter], la_hbm.at[:, my_quarter], at_x)
     leave_ffn(a11, s0, slots)
     mix_back(s0, slots)
     share_feats_b(gm, lm_hbm, s0, slots)
+    a_early(2)
     attend_back(0)
-    a_first(1)
+    share_qkv(0, own)
     a12 = Total(own, 2 * slots + T + own, 2 * slots + T + own, [(0, slots, False), (slots, T, True)])
     a12.start(in_back(s0, own, 0))
+    a12.middle()
+    x_act1.wait()
+    core_act1 = remote(la_hbm.at[:, my_cols], la_hbm.at[:, my_cols], at_core)
+    a_second(1, early_in(1))
+    a_early(3)
+    for copy in thin_act2:
+        copy.wait()
+    to_x = remote(lxx.at[1, :, my_quarter], lxx.at[1, :, my_quarter], at_x)
     pass_on(gifts_b)
-    a12.middle()
-    stage = [
-        local(ra_hbm.at[pl.ds(t1, own + slots), :], qkv.at[pl.ds(t1, own + slots), :]),
-        local(mx_hbm, dmix),
-    ]
+    stage = [local(mx_hbm, dmix)]
     pass_end()
     stage.append(local(lm_hbm, ar_full.at[pl.ds(0, p0), :]))
-    a_second(0)
+    a12.finish()
     for copy in stage:
         copy.wait()
     b_first(0)
@@ -1318,7 +1207,6 @@
     for k in range(nu // quarter):
         small_out[base + 8 + k : base + 9 + k, :] = column(db, pl.ds(k * quarter, quarter))
     small_out[base + 12 : base + 16, :] = jnp.zeros((4, quarter), F32)
-    a12.finish()
     a12.done()
     rows_back(a12, 0)
     small_out[pl.ds(0, slots), :] = emb_wide[:, my_quarter]
@@ -1330,46 +1218,53 @@
     copy.wait()
     small_out[base : base + 1, :] = gx_recv[0:1, :] + jnp.sum(gsum[pl.ds(0, 8), my_quarter], axis=0, keepdims=True)
     small_out[base + 1 : base + 2, :] = gx_recv[1:2, :] + jnp.sum(gsum[pl.ds(8, 8), my_quarter], axis=0, keepdims=True)
-    stage = [local(la_hbm, rows)]
     small_step(0)
+    to_x.wait()
+    to_core = remote(lxx.at[1, :, my_cols], lxx.at[1, :, my_cols], at_core)
     pass_on(gifts_a)
-    a_second(1)
-    share_qkv(0, own)
-    b_second(0)
-    b_second(1)
-    a_first(2)
+    to_core.wait()
+    a_first(4)
+    a_second(2, early_in(2))
+    for copy in gifts_q:
+        copy.wait()
+    core_act1.wait()
+    stage = [local(la_hbm, rows), local(ra_hbm, qkv.at[:, pl.ds(0, 3 * hq)])]
     a_third(0, 0)
-    pass_on(gifts_b)
-    stage.append(local(ra_hbm.at[pl.ds(s0, own), :], qkv.at[pl.ds(s0, own), :]))
-    a_first(3)
     for copy in stage:
         copy.wait()
+    a_second(3, early_in(3))
+    a_first(5)
+    a_third(0, 1)
 
     def turn(it, lag, first, count, stage):
         @pl.when((it >= first + lag) & (it < lag + count))
         def _():
             stage(it - lag)
 
-    turns = max(tiles_a + 2 * nh + 2, tiles_b + 2 * nh + 1)
+    turns = tiles_a + 2 * nh
 
     @pl.loop(0, turns)
     def _(it):
-        turn(it, -4, 4, tiles_a, a_first)
-        turn(it, -2, 2, tiles_b, b_first)
-        turn(it, -2, 2, tiles_a, a_second)
-        turn(it, -1, 2, tiles_b, b_second)
+        turn(it, -4, 4, tiles_a, a_second)
+        turn(it, -6, 6, tiles_a, a_first)
+        turn(it, 1, 0, tiles_b, b_second)
         for k in range(nh):
-            turn(it, 2 * k, 0 if k else 1, tiles_a, functools.partial(a_third, k))
-        turn(it, 2 * nh, 0, tiles_a, a_fourth)
-        turn(it, 2 * nh + 2, 0, tiles_a, a_fifth)
+            turn(it, 2 * k - 2, 0 if k else 2, tiles_a, functools.partial(a_third, k))
+        turn(it, 2 * nh - 2, 0, tiles_a, a_fourth)
+        turn(it, 2 * nh, 0, tiles_a, a_fifth)
         for k in range(nh):
-            turn(it, 1 + 2 * k, 0, tiles_b, functools.partial(b_third, k))
-        turn(it, 1 + 2 * nh, 0, tiles_b, b_fourth)
+            turn(it, 3 + 2 * k, 0, tiles_b, functools.partial(b_third, k))
+        turn(it, 3 + 2 * nh, 0, tiles_b, b_fourth)
         for k in range(1, len(small_partners) + 1):
 
             @pl.when(it == 2 * k - 1)
             def _():
                 small_step(k)
+
+    assert counter["l"] <= lsem.shape[0] and counter["r"] <= rsem.shape[0]
+
+    for copy in gin_copies:
+        copy.wait()
 
     @pl.loop(0, tiles_a)
     def _(i):
@@ -1392,7 +1287,7 @@
     sums = 2 * slots + 2 * toks + 2 * own
     chunk = feats >> bits
     nh = bits - 2
-    ta, tb = 2 * nu // nq, 8
+    ta, tb = 2 * nu // nq + 3, 2
     vm = pltpu.VMEM
     sds = jax.ShapeDtypeStruct
     dma = pltpu.SemaphoreType.DMA
@@ -1419,7 +1314,7 @@
         vm((8, feats), F32),
         vm((1, 3 * nq + nu), F32),
         vm((end, 128), F32),
-        vm((3, toks, half), F32),
+        vm((max(3 * toks, (slots + 16) * ((bits + 2) // 2)), half), F32),
         vm((16, feats), F32),
         vm((16, feats), F32),
         vm((8, quarter), F32),
@@ -1433,10 +1328,9 @@
         vm((main, nu), BF),
         vm((2 * chunk if chunk % 128 else 8, nq // 2), F32),
         vm((slots + 16, quarter), F32),
-        vm((bits + 1, slots + 16, quarter), F32),
         dma((6,)),
-        dma((24,)),
-        dma((192, 2)),
+        dma((16,)),
+        dma((113, 2)),
         pltpu.SemaphoreType.REGULAR((3 + nh,)),
         dma((ta, 2)),
         dma((nh, ta, 2)),
@@ -1448,6 +1342,7 @@
         dma((ta, 4)),
         dma((tb, 2)),
         dma((bits + 1, 2)),
+        vm((2, feats // 2, nq // 2), BF),
     ]
     vmem = pl.BlockSpec(memory_space=pltpu.VMEM)
     hbm = pl.BlockSpec(memory_space=pl.ANY)
@@ -1463,11 +1358,14 @@
             sds((chunk // 2, 8 * nq + 4 * nu), BF),
             sds((end, feats), BF),
             sds((main, feats), BF),
-            sds((end, 3 * nq), BF),
+            sds((end, 3 * nq // 2), BF),
             sds((main, nq), BF),
+            sds((4, feats // 2, nq // 2), BF),
+            sds((2 * slots, feats), BF),
+            sds((2 * slots, nu // 2), BF),
         ),
         in_specs=[smem, vmem, vmem, [vmem] * 6, vmem, vmem, vmem] + [hbm] * 8,
-        out_specs=(vmem,) * 4 + (hbm,) * 5,
+        out_specs=(vmem, vmem, hbm, vmem) + (hbm,) * 8,
         scratch_shapes=scratch,
         compiler_params=pltpu.CompilerParams(
             collective_id=2, has_side_effects=True, vmem_limit_bytes=63 * 2**20

time: 287 us -> 264 us (0.920)
  Pallas kernels: 286 us -> 262 us
    pallas_call x1, Pallas kernels: 280 us -> 256 us  [chain(): pl.pallas_call(functools.partial(chain_kernel, bits), name='layer', out_s...]
where the time goes in v5:
time: 264 us
  Pallas kernels  262 us (99%)
    pallas_call x1, Pallas kernels, chain(): pl.pallas_call(functools.partial(chain_kernel, bits), name='layer', out_s...  256 us
    pallas_call x1, Pallas kernels, place(): pl.pallas_call(place_kernel, name='place', out_shape=(sds((1, 2, toks, ha...  5.8 us

profile of v5, /device:TPU:0, one launch (start us, length us, event | category | flops | bytes accessed | tf_op | source)
XLA Modules:
  0.0 263.8 jit_solution(11897565827167348503)
XLA Ops:
  1.3 256.5 %layer.1 = (bf16[2,64,1024]{2,1,0:T(8,128)(2,1)}, bf16[2,64,1024]{2,1,0:T(8,128)(2,1)}, f32[2,64,1024]{2,1,0:T(8,128)}, f32[2,80,512]{2,1,0:T(8,128)}, bf16[128,...) custom-call(s32[1]{0:T(128)S(6)} %copy.39.count_ref, ...), custom_call_target="tpu_custom_call" | custom-call | tf_op jit(solution)/shard_map/layer/pallas_call | solution.py:1350
  257.8 5.8 %place.1 = (bf16[1,2,64,1024]{3,2,1,0:T(8,128)(2,1)}, bf16[50,2,1024]{2,1,0:T(2,128)(2,1)}, f32[1,2,64,1024]{3,2,1,0:T(8,128)}, f32[50,1024]{1,0:T(8,128)}, f32[...) custom-call(bf16[2,64,1024]{2,1,0:T(8,128)(2,1)} %get-tuple-element., ...), custom_call_target="tpu_custom_call" | custom-call | tf_op jit(solution)/shard_map/place/pallas_call | solution.py:1406

commit v6 on v5

--- a/solution.py
+++ b/solution.py
@@ -150,6 +150,10 @@
     sem_ob,
     sem_s,
     early,
+    emb_v,
+    dsum_v,
+    vecs_v,
+    isem,
 ):
     b, s, t = lax.axis_index("batch"), lax.axis_index("seq"), lax.axis_index("tensor")
     at_core = (b, s, 1 - t)
@@ -162,6 +166,16 @@
     halving_down = list(range(bits - 2, 0, -1))
     at_d = (flip(b, bits - 1), s, t)
     zd = bit_of(b, bits - 1)
+    count = len(feat_refs)
+    small_ins = [(emb_ref, emb_v), (dsum_ref, dsum_v)]
+    small_ins += list(zip(list(feat_refs) + [bq_ref, bv_ref, bu_ref], vecs_v))
+    small_ins = [
+        pltpu.make_async_copy(src, dst, isem.at[k]) for k, (src, dst) in enumerate(small_ins)
+    ]
+    for copy in small_ins:
+        copy.start()
+    feat_refs, (bq_ref, bv_ref, bu_ref) = vecs_v[:count], vecs_v[count:]
+    emb_ref, dsum_ref = emb_v, dsum_v
     barrier = pltpu.get_barrier_semaphore()
     partners = [at_core, at_x, at_p, at_y] + at_h
     for partner in partners:
@@ -234,6 +248,8 @@
         laters.append(local(dhid_hbm.at[seg], gd.at[pl.ds(at + my_toks, toks), my_cols]))
     for copy in weights[:3]:
         copy.start()
+    for copy in small_ins:
+        copy.wait()
     for at in (s0, s1):
         rows[pl.ds(at, slots), my_cols] = jnp.zeros((slots, half), BF)
         rows[pl.ds(at, used), my_cols] = emb_ref[...]
@@ -1343,6 +1359,10 @@
         dma((tb, 2)),
         dma((bits + 1, 2)),
         vm((2, feats // 2, nq // 2), BF),
+        vm(emb.shape, BF),
+        vm(dsum.shape, BF),
+        [vm(v.shape, BF) for v in feat_vecs + [bq, bv, bu]],
+        dma((len(feat_vecs) + 5,)),
     ]
     vmem = pl.BlockSpec(memory_space=pltpu.VMEM)
     hbm = pl.BlockSpec(memory_space=pl.ANY)
@@ -1364,7 +1384,7 @@
             sds((2 * slots, feats), BF),
             sds((2 * slots, nu // 2), BF),
         ),
-        in_specs=[smem, vmem, vmem, [vmem] * 6, vmem, vmem, vmem] + [hbm] * 8,
+        in_specs=[smem, hbm, hbm, [hbm] * 6, hbm, hbm, hbm] + [hbm] * 8,
         out_specs=(vmem, vmem, hbm, vmem) + (hbm,) * 8,
         scratch_shapes=scratch,
         compiler_params=pltpu.CompilerParams(
@@ -1373,28 +1393,64 @@
     )(count, emb, dsum, feat_vecs, bq, bv, bu, hid, dhid, wq, wk, wv, wo, wu, wd)
 
 
-def place_kernel(hid, sums, gin, small, w, hid_o, sum_o, gin_o, emb_o, vec_o, bup_o, q_o, k_o, v_o, o_o, u_o, d_o):
-    hid_o[0] = hid[...]
+def place_kernel(
+    hid, sums, gin, small, w, hid_o, sum_o, gin_o, emb_o, vec_o, bup_o, q_o, k_o, v_o, o_o, u_o, d_o,
+    hid_v, sum_v, gin_v, small_v, w_v, wide_v, tall_v, sem,
+):
+    n, wide = q_o.shape[1], u_o.shape[1]
+    sections = [(k * n, n) for k in range(4)] + [(4 * n, wide), (4 * n + wide, wide)]
+    copy = pltpu.make_async_copy
+    ins = []
+    for k, (at, m) in enumerate(sections):
+        cols = pl.ds(at, m)
+        ins.append(copy(w.at[:, cols], w_v.at[:, cols], sem.at[k]))
+    plain = ((hid, hid_v), (gin, gin_v), (sums, sum_v), (small, small_v))
+    plain = [copy(src, dst, sem.at[6 + k]) for k, (src, dst) in enumerate(plain)]
+    order = (5, 4, 3, 0, 1, 2)
+    for k in order:
+        ins[k].start()
+    for c in plain:
+        c.start()
+    outs = []
+
+    def send(src, dst):
+        c = copy(src, dst, sem.at[10 + len(outs)])
+        c.start()
+        outs.append(c)
+
+    for k in order:
+        at, m = sections[k]
+        cols = pl.ds(at, m)
+        ins[k].wait()
+        x = w_v[:, cols].astype(F32)
+        if k in (3, 5):
+            there = tall_v.at[pl.ds(0, m), :] if k == 5 else tall_v.at[pl.ds(wide, m), :]
+            there[...] = x.T
+        else:
+            there = wide_v.at[:, cols]
+            there[...] = x
+        send(there, (q_o, k_o, v_o, o_o, u_o, d_o)[k])
+    for c in plain[:2]:
+        c.wait()
+    send(hid_v, hid_o.at[0])
+    send(gin_v, gin_o.at[0])
+    for c in plain[2:]:
+        c.wait()
     used = sum_o.shape[0]
     for seg in range(2):
-        sum_o[:, seg, :] = sums[seg, :used, :]
-    gin_o[0] = gin[...]
-    quarter = small.shape[2]
-    base = small.shape[1] - 16
+        sum_o[:, seg, :] = sum_v[seg, :used, :]
+    quarter = small_v.shape[2]
+    base = small_v.shape[1] - 16
     nu = bup_o.shape[0] // 2
     for side in range(2):
         at = pl.ds(side * quarter, quarter)
-        emb_o[:, at] = small[side, :used, :]
+        emb_o[:, at] = small_v[side, :used, :]
         for k, ref in enumerate(vec_o):
-            ref[at] = small[side, base + k]
+            ref[at] = small_v[side, base + k]
         for k in range(nu // quarter):
-            bup_o[pl.ds(side * nu + k * quarter, quarter)] = small[side, base + 8 + k]
-    n = q_o.shape[1]
-    for k, ref in enumerate((q_o, k_o, v_o)):
-        ref[...] = w[:, k * n : (k + 1) * n].astype(F32)
-    o_o[...] = w[:, 3 * n : 4 * n].astype(F32).T
-    u_o[...] = w[:, 4 * n : 4 * n + 2 * nu].astype(F32)
-    d_o[...] = w[:, 4 * n + 2 * nu :].astype(F32).T
+            bup_o[pl.ds(side * nu + k * quarter, quarter)] = small_v[side, base + 8 + k]
+    for c in outs:
+        c.wait()
 
 
 def place(hid, sums, gin, small, w, used):
@@ -1403,6 +1459,8 @@
     rows = w.shape[0]
     nu = (w.shape[1] - 4 * half) // 4
     vmem = pl.BlockSpec(memory_space=pltpu.VMEM)
+    hbm = pl.BlockSpec(memory_space=pl.ANY)
+    vm = pltpu.VMEM
     return pl.pallas_call(
         place_kernel,
         name="place",
@@ -1420,8 +1478,18 @@
             sds((rows, 2 * nu), F32),
             sds((2 * nu, rows), F32),
         ),
-        in_specs=[vmem] * 5,
-        out_specs=(vmem,) * 4 + ([vmem] * 8,) + (vmem,) * 7,
+        in_specs=[hbm] * 5,
+        out_specs=(hbm, vmem, hbm, vmem, [vmem] * 8, vmem) + (hbm,) * 6,
+        scratch_shapes=[
+            vm(hid.shape, BF),
+            vm(sums.shape, BF),
+            vm(gin.shape, F32),
+            vm(small.shape, F32),
+            vm(w.shape, BF),
+            vm((rows, 4 * half + 2 * nu), F32),
+            vm((2 * nu + half, rows), F32),
+            pltpu.SemaphoreType.DMA((18,)),
+        ],
         compiler_params=pltpu.CompilerParams(vmem_limit_bytes=60 * 2**20),
     )(hid, sums, gin, small, w)
 

time: 264 us -> 263 us (level)
  no operation moved by 1% of the time
where the time goes in v6:
time: 263 us
  Pallas kernels  261 us (99%)
    pallas_call x1, Pallas kernels, chain(): pl.pallas_call(functools.partial(chain_kernel, bits), name='layer', out_s...  256 us
    pallas_call x1, Pallas kernels, place(): pl.pallas_call(place_kernel, name='place', out_shape=(sds((1, 2, toks, ha...  5.41 us

profile of v6, /device:TPU:0, one launch (start us, length us, event | category | flops | bytes accessed | tf_op | source)
XLA Modules:
  0.0 262.7 jit_solution(10899135890053386725)
XLA Ops:
  1.3 255.8 %layer.1 = (bf16[2,64,1024]{2,1,0:T(8,128)(2,1)}, bf16[2,64,1024]{2,1,0:T(8,128)(2,1)}, f32[2,64,1024]{2,1,0:T(8,128)}, f32[2,80,512]{2,1,0:T(8,128)}, bf16[128,...) custom-call(s32[1]{0:T(128)S(6)} %copy.39.count_ref, ...), custom_call_target="tpu_custom_call" | custom-call | tf_op jit(solution)/shard_map/layer/pallas_call | solution.py:1370
  257.1 5.4 %place.1 = (bf16[1,2,64,1024]{3,2,1,0:T(8,128)(2,1)}, bf16[50,2,1024]{2,1,0:T(2,128)(2,1)}, f32[1,2,64,1024]{3,2,1,0:T(8,128)}, f32[50,1024]{1,0:T(8,128)}, f32[...) custom-call(bf16[2,64,1024]{2,1,0:T(8,128)(2,1)} %get-tuple-element., ...), custom_call_target="tpu_custom_call" | custom-call | tf_op jit(solution)/shard_map/place/pallas_call | solution.py:1464

commit v7 on v6

--- a/solution.py
+++ b/solution.py
@@ -1006,8 +1006,9 @@
         cols, r = pl.ds(c, wide), pl.ds(t1, own)
         db[r, cols] = dot_nt(gd[r, :], wd[cols, :]).astype(BF)
 
-    col_loop(nu, early_before)
+    col_loop(3 * nu // 4, early_before)
     a3.finish()
+    early_before(pl.multiple_of(3 * nu // 4, wide))
     thin_act2.append(share_thin(act2, lxx.at[1], s0, own, at_d))
     a3.done()
 

time: 263 us -> 262 us (level)
  no operation moved by 1% of the time
where the time goes in v7:
time: 262 us
  Pallas kernels  260 us (99%)
    pallas_call x1, Pallas kernels, chain(): pl.pallas_call(functools.partial(chain_kernel, bits), name='layer', out_s...  255 us
    pallas_call x1, Pallas kernels, place(): pl.pallas_call(place_kernel, name='place', out_shape=(sds((1, 2, toks, ha...  5.41 us

profile of v7, /device:TPU:0, one launch (start us, length us, event | category | flops | bytes accessed | tf_op | source)
XLA Modules:
  0.0 261.8 jit_solution(14658077768157688739)
XLA Ops:
  1.3 254.9 %layer.1 = (bf16[2,64,1024]{2,1,0:T(8,128)(2,1)}, bf16[2,64,1024]{2,1,0:T(8,128)(2,1)}, f32[2,64,1024]{2,1,0:T(8,128)}, f32[2,80,512]{2,1,0:T(8,128)}, bf16[128,...) custom-call(s32[1]{0:T(128)S(6)} %copy.39.count_ref, ...), custom_call_target="tpu_custom_call" | custom-call | tf_op jit(solution)/shard_map/layer/pallas_call | solution.py:1371
  256.2 5.4 %place.1 = (bf16[1,2,64,1024]{3,2,1,0:T(8,128)(2,1)}, bf16[50,2,1024]{2,1,0:T(2,128)(2,1)}, f32[1,2,64,1024]{3,2,1,0:T(8,128)}, f32[50,1024]{1,0:T(8,128)}, f32[...) custom-call(bf16[2,64,1024]{2,1,0:T(8,128)(2,1)} %get-tuple-element., ...), custom_call_target="tpu_custom_call" | custom-call | tf_op jit(solution)/shard_map/place/pallas_call | solution.py:1465
